TPU v7x, 128 devices: a whole 4x4x4 slice. The times are simulated.
128 devices in a mesh: lat: 16 (over y, z_hi, core), lon: 8 (over z_lo, x).
Axes of the slice: x: 4, y: 4, z: 4 (z_hi: 2, z_lo: 2; z = z_hi * 2 + z_lo), core: 2. Of those that a mesh axis runs over, the one named last changes fastest.
Arguments:
- fields: bfloat16 [4, 128, 512, 640], P(None, 'lat', 'lon'), may hold values from -6 to 6
- kernel: float32 [128, 9, 3, 512], P('lat'), may hold values from -0.09375 to 0.09375
- theta: float32 [3, 640], P(None, 'lon'), may hold values from -4 to 4
- row_start: int32 [128], P('lat'), may hold values from 0 to 123, as said below
- row_count: int32 [128], P('lat'), may hold values from 1 to 9
- norm_gain: float32 [640], replicated, may hold values from 0.1 to 1.9
- w_in: bfloat16 [640, 1280], replicated, may hold values from -0.25 to 0.25
- b_in: float32 [1280], replicated, may hold values from -3 to 3
- w_out: bfloat16 [1280, 640], replicated, may hold values from -0.15625 to 0.15625
Outputs:
- block_out: bfloat16 [4, 128, 512, 640], P(None, 'lat', 'lon')
Inputs may be any that keep to these rules, and one draw needn't show every extreme that they name: Output row i draws on rows row_start[i] to row_start[i] + row_count[i] - 1, all inside the grid and within 4 rows of i.
All inputs are finite; a program needn't handle non-finite values.
Results may differ from a plain program's by a relative error of at most 0.0085.
Values may be sent and summed in bfloat16 or wider, within the bound.
No kernel may reach another device: no remote copies, remote signals or barrier semaphores. Data moves between devices by JAX's collectives and lax.ppermute only.
A program may use at most 192 MiB of HBM per device.

v0:
```python
import functools

import jax
import jax.numpy as jnp
import ml_dtypes
import numpy as np
from jax import lax
from jax.experimental import pallas as pl
from jax.experimental.pallas import tpu as pltpu
from jax.sharding import PartitionSpec as P

BF16 = jnp.bfloat16
F32 = jnp.float32

LON_DEV = 8
ROWS = 8
HALF = 4
ENS = 4
CHUNK = 64
CHAN = 640
CH = 80
COLS = ENS * CH
NLON = 512
SLOTS = 9
KB = 3
FB = 16
FS = 16
WIN = 12
PTS = ENS * HALF * CHUNK
HID = 1280
VMEM = 56 * 1024 * 1024


def tables():
    point = np.arange(NLON)
    freq = np.arange(NLON // 2)
    angle = 2.0 * np.pi * ((freq[:, None] * point[None, :]) % NLON) / NLON
    re, im = np.cos(angle), -np.sin(angle)
    im[0] = np.cos(np.pi * point)
    weight = np.full((NLON // 2, 1), 2.0 / NLON)
    weight[0] = 1.0 / NLON
    onward = np.stack([re.reshape(FB, FS, NLON), im.reshape(FB, FS, NLON)], axis=1)
    back = np.stack(
        [(re * weight).reshape(FB, FS, NLON), (im * weight).reshape(FB, FS, NLON)], axis=1
    )
    return (
        onward.reshape(NLON, NLON).astype(ml_dtypes.bfloat16),
        back.reshape(NLON, NLON).astype(ml_dtypes.bfloat16),
    )


def params(*semantics):
    return pltpu.CompilerParams(vmem_limit_bytes=VMEM, dimension_semantics=semantics)


def cost(flops, nbytes):
    return pl.CostEstimate(flops=int(flops), bytes_accessed=int(nbytes), transcendentals=0)


def pack_kernel(x_ref, o_ref):
    x = x_ref[0].reshape(HALF * CHUNK, CHAN)
    o_ref[...] = x.T


def pack(fields, half):
    wide = HALF * CHUNK
    return pl.pallas_call(
        pack_kernel,
        grid=(ENS,),
        in_specs=[pl.BlockSpec((1, HALF, CHUNK, CHAN), lambda e: (e, half, 0, 0))],
        out_specs=pl.BlockSpec((CHAN, wide), lambda e: (0, e)),
        out_shape=jax.ShapeDtypeStruct((CHAN, PTS), BF16),
        compiler_params=params("arbitrary"),
        cost_estimate=cost(0, 4 * CHAN * PTS),
        name="pack",
    )(fields)


def dft_rows_kernel(x_ref, w_ref, o_ref):
    for pair in range(2):
        rows = [[], []]
        for e in range(ENS):
            parts = [[], []]
            base = (e * 2 + pair) * 128
            for d in range(LON_DEV):
                tile = x_ref[d * CH : (d + 1) * CH, base : base + 128]
                parts[0].append(tile[:, :CHUNK])
                parts[1].append(tile[:, CHUNK:])
            for r in range(2):
                rows[r].append(jnp.concatenate(parts[r], axis=1))
        for r in range(2):
            x = jnp.concatenate(rows[r], axis=0)
            s = lax.dot_general(
                w_ref[...], x, (((1,), (1,)), ((), ())), preferred_element_type=F32
            )
            at = (pair * 2 + r) * 2 * FS
            o_ref[:, at : at + 2 * FS, :] = s.astype(BF16).reshape(FB, 2 * FS, COLS)


def dft(received, onward):
    return pl.pallas_call(
        dft_rows_kernel,
        out_shape=jax.ShapeDtypeStruct((FB, HALF * 2 * FS, COLS), BF16),
        compiler_params=params(),
        cost_estimate=cost(2 * HALF * NLON * NLON * COLS, 8 * CHAN * PTS),
        name="dft",
    )(received, onward)


def coef_kernel(start_ref, count_ref, first_ref, k_ref, w_ref, o_ref):
    half = pl.program_id(0)
    kern = k_ref[...].astype(BF16)
    hat = lax.dot_general(w_ref[...], kern, (((1,), (1,)), ((), ())), preferred_element_type=F32)
    hat = hat.astype(BF16).reshape(FB, 2, FS, SLOTS * KB * HALF)
    hat_re = hat[:, 0].reshape(FB * FS, SLOTS * KB * HALF)
    hat_im = hat[:, 1].reshape(FB * FS, SLOTS * KB * HALF)
    lanes = WIN * 2 * FS
    taps = SLOTS * KB * HALF
    tap = lax.broadcasted_iota(jnp.int32, (taps, lanes), 0)
    window = lax.broadcasted_iota(jnp.int32, (taps, lanes), 1) // (2 * FS)
    lane = lax.broadcasted_iota(jnp.int32, (FB * FS, lanes), 1)
    freq = lax.broadcasted_iota(jnp.int32, (FB * FS, lanes), 0)
    same = (lane % FS) == (freq % FS)
    imag = (lane // FS) % 2 == 1
    zero = freq == 0
    for i in range(HALF):
        row = half * HALF + i
        offset = start_ref[row] - (first_ref[0] + (half - 1) * HALF)
        slot = window - offset
        live = (slot >= 0) & (slot < count_ref[row])
        for k in range(KB):
            pick = (live & (tap == (i * SLOTS + slot) * KB + k)).astype(F32).astype(BF16)
            re = jnp.dot(hat_re, pick, preferred_element_type=F32)
            im = jnp.dot(hat_im, pick, preferred_element_type=F32)
            top = jnp.where(imag, jnp.where(zero, 0.0, -im), re)
            low = jnp.where(imag, jnp.where(zero, im, re), jnp.where(zero, 0.0, im))
            top = jnp.where(same, top, 0.0).astype(BF16).reshape(FB, FS, lanes)
            low = jnp.where(same, low, 0.0).astype(BF16).reshape(FB, FS, lanes)
            at = (i * KB + k) * 2 * FS
            o_ref[0, :, at : at + FS, :] = top
            o_ref[0, :, at + FS : at + 2 * FS, :] = low


def coefs(row_start, row_count, first, kernel, onward):
    smem = pl.BlockSpec(memory_space=pltpu.SMEM)
    taps = HALF * SLOTS * KB
    size = HALF * KB * 2 * FS
    return pl.pallas_call(
        coef_kernel,
        grid=(2,),
        in_specs=[
            smem,
            smem,
            smem,
            pl.BlockSpec((None, taps, NLON), lambda h: (h, 0, 0)),
            pl.BlockSpec((NLON, NLON), lambda h: (0, 0)),
        ],
        out_specs=pl.BlockSpec((1, FB, size, WIN * 2 * FS), lambda h: (h, 0, 0, 0)),
        out_shape=jax.ShapeDtypeStruct((2, FB, size, WIN * 2 * FS), BF16),
        compiler_params=params("arbitrary"),
        cost_estimate=cost(8e9, 1e7),
        name="coefs",
    )(row_start, row_count, first, kernel.reshape(2, taps, NLON), onward)


STEP = 4


def mix_kernel(g_ref, a_ref, b_ref, c_ref, theta_ref, back_ref, o_ref, t_ref):
    step = pl.program_id(0)
    theta = [theta_ref[k : k + 1, :] for k in range(KB)]
    for f in range(STEP):
        x = jnp.concatenate([a_ref[f], b_ref[f], c_ref[f]], axis=0)
        p = jnp.dot(g_ref[0, f], x, preferred_element_type=F32)
        for i in range(HALF):
            total = None
            for k in range(KB):
                at = (i * KB + k) * 2 * FS
                term = p[at : at + 2 * FS, :] * theta[k]
                total = term if total is None else total + term
            t_ref[i, pl.ds((step * STEP + f) * 2 * FS, 2 * FS), :] = total.astype(BF16)

    @pl.when(step == FB // STEP - 1)
    def _():
        for pair in range(2):
            y = [
                lax.dot_general(
                    t_ref[pair * 2 + r],
                    back_ref[...],
                    (((0,), (0,)), ((), ())),
                    preferred_element_type=F32,
                ).astype(BF16)
                for r in range(2)
            ]
            for e in range(ENS):
                base = (e * 2 + pair) * 128
                for d in range(LON_DEV):
                    o_ref[d * CH : (d + 1) * CH, base : base + 128] = jnp.concatenate(
                        [v[e * CH : (e + 1) * CH, d * CHUNK : (d + 1) * CHUNK] for v in y], axis=1
                    )


def mix(coef, half, spectra, theta, back):
    size = HALF * KB * 2 * FS
    spec = pl.BlockSpec((STEP, HALF * 2 * FS, COLS), lambda s: (s, 0, 0))
    return pl.pallas_call(
        mix_kernel,
        grid=(FB // STEP,),
        in_specs=[
            pl.BlockSpec((1, STEP, size, WIN * 2 * FS), lambda s: (half, s, 0, 0)),
            spec,
            spec,
            spec,
            pl.BlockSpec((KB, COLS), lambda s: (0, 0)),
            pl.BlockSpec((NLON, NLON), lambda s: (0, 0)),
        ],
        out_specs=pl.BlockSpec((CHAN, PTS), lambda s: (0, 0)),
        out_shape=jax.ShapeDtypeStruct((CHAN, PTS), BF16),
        scratch_shapes=[pltpu.VMEM((HALF, NLON, COLS), BF16)],
        compiler_params=params("arbitrary"),
        cost_estimate=cost(4e9, 1.6e7),
        name="mix",
    )(coef, *spectra, theta, back)


def mlp_kernel(y_ref, x_ref, gain_ref, w_in_ref, b_in_ref, w_out_ref, *rest):
    o_ref = rest[-1]
    values = y_ref[...].astype(F32)
    mean = jnp.mean(values, axis=0, keepdims=True)
    away = values - mean
    var = jnp.mean(away * away, axis=0, keepdims=True)
    normed = (away * lax.rsqrt(var + 1e-5) * gain_ref[...]).astype(BF16)
    hidden = jnp.dot(normed.T, w_in_ref[...], preferred_element_type=F32) + b_in_ref[...]
    hidden = (0.5 * hidden * (1.0 + lax.erf(hidden * np.float32(0.5**0.5)))).astype(BF16)
    branch = jnp.dot(hidden, w_out_ref[...], preferred_element_type=F32)
    x = x_ref[0].reshape(HALF * CHUNK, CHAN).astype(F32)
    o_ref[0] = (x + branch).astype(BF16).reshape(HALF, CHUNK, CHAN)


def mlp(y, fields, half, gain, w_in, b_in, w_out, before=None):
    wide = HALF * CHUNK
    points = pl.BlockSpec((1, HALF, CHUNK, CHAN), lambda e: (e, half, 0, 0))
    whole = lambda *shape: pl.BlockSpec(shape, lambda e: (0, 0))
    extra = () if before is None else (before,)
    return pl.pallas_call(
        mlp_kernel,
        grid=(ENS,),
        in_specs=[
            pl.BlockSpec((CHAN, wide), lambda e: (0, e)),
            points,
            whole(CHAN, 1),
            whole(CHAN, HID),
            whole(1, HID),
            whole(HID, CHAN),
        ]
        + [pl.BlockSpec(memory_space=pl.ANY)] * len(extra),
        out_specs=points,
        out_shape=jax.ShapeDtypeStruct((ENS, ROWS, CHUNK, CHAN), BF16),
        input_output_aliases={6: 0} if extra else {},
        compiler_params=params("arbitrary"),
        cost_estimate=cost(4 * PTS * CHAN * HID, 1.2e7),
        name="mlp",
    )(y, fields, gain, w_in, b_in, w_out, *extra)


def shards(fields, kernel, theta, row_start, row_count, norm_gain, w_in, b_in, w_out):
    onward, back = (jnp.asarray(t) for t in tables())
    size = lax.axis_size("lat")
    up = [(i, i + 1) for i in range(size - 1)]
    down = [(j, i) for i, j in up]
    swap = functools.partial(
        lax.all_to_all, axis_name="lon", split_axis=0, concat_axis=0, tiled=True
    )
    low = swap(pack(fields, 0))
    high = swap(pack(fields, 1))
    after = lax.ppermute(low, "lat", down)
    before = lax.ppermute(high, "lat", up)
    first = (lax.axis_index("lat") * ROWS).astype(jnp.int32).reshape(1)
    coef = coefs(row_start, row_count, first, kernel, onward)
    theta4 = jnp.tile(theta, (1, ENS))
    spec_low = dft(low, onward)
    spec_high = dft(high, onward)
    spec_after = dft(after, onward)
    conv_high = swap(mix(coef, 1, (spec_low, spec_high, spec_after), theta4, back))
    spec_before = dft(before, onward)
    conv_low = swap(mix(coef, 0, (spec_before, spec_low, spec_high), theta4, back))
    rest = (norm_gain[:, None], w_in, b_in[None, :], w_out)
    out = mlp(conv_high, fields, 1, *rest)
    return mlp(conv_low, fields, 0, *rest, before=out)


def solution(mesh):
    placed = (
        P(None, "lat", "lon", None),
        P("lat", None, None, None),
        P(None, "lon"),
        P("lat"),
        P("lat"),
        P(),
        P(),
        P(),
        P(),
    )
    return jax.shard_map(
        shards, mesh=mesh, in_specs=placed, out_specs=P(None, "lat", "lon", None), check_vma=False
    )
```

profile of v0, /device:TPU:1, one launch (start us, length us, event | category | flops | bytes accessed | tf_op | source)
XLA Modules:
  0.0 148.6 jit_solution(11985012697651382102)
XLA Ops:
  0.0 3.8 %pack.3 = bf16[640,1024]{1,0:T(8,128)(2,1)} custom-call(bf16[4,8,64,640]{3,2,1,0:T(8,128)(2,1)} %x_ref.7), custom_call_target="tpu_custom_call" | custom-call | bytes 2621440 | tf_op jit(solution)/shard_map/pack/pallas_call | solution.py:67
  3.8 6.2 %all-to-all-start.1 = ((bf16[8,80,1024]{2,1,0:T(8,128)(2,1)}), bf16[8,80,1024]{2,1,0:T(8,128)(2,1)S(1)}, u32[]{:S(2)}, u32[]{:S(2)}) async-start(bf16[8,80,1024]{2,1,0:T(8,128)(2,1)} %bitcast.17), calls=%async_computation.1 | async-start | bytes 2621440 | tf_op jit(solution)/shard_map/all_to_all | solution.py:274
  10.0 3.7 %pack.2 = bf16[640,1024]{1,0:T(8,128)(2,1)} custom-call(bf16[4,8,64,640]{3,2,1,0:T(8,128)(2,1)} %x_ref.7), custom_call_target="tpu_custom_call" | custom-call | bytes 2621440 | tf_op jit(solution)/shard_map/pack/pallas_call | solution.py:67
  13.7 14.9 %all-to-all-done.1 = bf16[8,80,1024]{2,1,0:T(8,128)(2,1)S(1)} async-done(((bf16[8,80,1024]{2,1,0:T(8,128)(2,1)}), bf16[8,80,1024]{2,1,0:T(8,128)(2,1)S(1)}, u32[]{:S(2)}, u32[]{:S(2)}) %all-to-all-start.1) | async-done | bytes 1310752 | tf_op jit(solution)/shard_map/all_to_all | solution.py:274
  28.6 0.0 copy-start.2
  28.6 3.6 %all-to-all-start = ((bf16[8,80,1024]{2,1,0:T(8,128)(2,1)}), bf16[8,80,1024]{2,1,0:T(8,128)(2,1)S(1)}, u32[]{:S(2)}, u32[]{:S(2)}) async-start(bf16[8,80,1024]{2,1,0:T(8,128)(2,1)} %bitcast.16), calls=%async_computation | async-start | bytes 2621440 | tf_op jit(solution)/shard_map/all_to_all | solution.py:275
  32.2 2.8 %collective-permute-start.1 = (bf16[640,1024]{1,0:T(8,128)(2,1)S(1)}, bf16[640,1024]{1,0:T(8,128)(2,1)}, u32[]{:S(2)}, u32[]{:S(2)}) collective-permute-start(bf16[640,1024]{1,0:T(8,128)(2,1)S(1)} %bitcast.14), channel_id=1, source_target_pairs={{8,0},{16,8},{24,16},{32,24},{40,32},{48,40},{56,48},{64,56},{72,6... | collective-permute-start | bytes 3932168 | tf_op jit(solution)/shard_map/ppermute | solution.py:276
  34.9 1.3 copy.14
  36.3 0.0 copy-done.2
  36.3 1.0 reshape.19.k_ref
  37.3 16.0 %all-to-all-done = bf16[8,80,1024]{2,1,0:T(8,128)(2,1)S(1)} async-done(((bf16[8,80,1024]{2,1,0:T(8,128)(2,1)}), bf16[8,80,1024]{2,1,0:T(8,128)(2,1)S(1)}, u32[]{:S(2)}, u32[]{:S(2)}) %all-to-all-start) | async-done | bytes 1310752 | tf_op jit(solution)/shard_map/all_to_all | solution.py:275
  53.3 0.0 copy-start.1
  53.3 3.5 %collective-permute-start = (bf16[640,1024]{1,0:T(8,128)(2,1)S(1)}, bf16[640,1024]{1,0:T(8,128)(2,1)}, u32[]{:S(2)}, u32[]{:S(2)}) collective-permute-start(bf16[640,1024]{1,0:T(8,128)(2,1)S(1)} %bitcast.12), channel_id=1, source_target_pairs={{0,8},{8,16},{16,24},{24,32},{32,40},{40,48},{48,56},{56,64},{64,7... | collective-permute-start | bytes 3932168 | tf_op jit(solution)/shard_map/ppermute | solution.py:277
  56.8 0.0 copy-start.6
  56.8 7.7 %coefs.1.g_ref = bf16[2,16,384,384]{3,2,1,0:T(8,128)(2,1)} custom-call(s32[8]{0:T(128)} %start_ref.1, s32[8]{0:T(128)} %count_ref.1, s32[1]{0:T(128)} %bitcast.first_ref, f32[2,108,512]{2,1,0:T(8,128)} %reshape.19.k_ref, bf16[512,512]{1,0:T(8,128)(2,1)} %constant.12.clone.w_ref), custom_call_target="tpu_custom_call" | custom-call | flops 8000000000 | bytes 10000000 | tf_op jit(solution)/shard_map/coefs/pallas_call | solution.py:148
  64.4 0.0 copy-done.1
  64.4 0.0 copy-done.6
  64.5 0.7 tile.10.theta_ref
  65.1 3.9 %dft.5.b_ref.a_ref = bf16[16,128,320]{2,1,0:T(8,128)(2,1)} custom-call(bf16[640,1024]{1,0:T(8,128)(2,1)} %bitcast.15, bf16[512,512]{1,0:T(8,128)(2,1)} %constant.12.clone.w_ref), custom_call_target="tpu_custom_call" | custom-call | flops 671088640 | bytes 5242880 | tf_op jit(solution)/shard_map/dft/pallas_call | solution.py:101
  69.0 3.9 %dft.6.c_ref.b_ref = bf16[16,128,320]{2,1,0:T(8,128)(2,1)} custom-call(bf16[640,1024]{1,0:T(8,128)(2,1)} %bitcast.13, bf16[512,512]{1,0:T(8,128)(2,1)} %constant.12.clone.w_ref), custom_call_target="tpu_custom_call" | custom-call | flops 671088640 | bytes 5242880 | tf_op jit(solution)/shard_map/dft/pallas_call | solution.py:101
  73.0 0.0 collective-permute-done.1.x_ref
  73.0 3.9 %dft.7.c_ref = bf16[16,128,320]{2,1,0:T(8,128)(2,1)} custom-call(bf16[640,1024]{1,0:T(8,128)(2,1)} %collective-permute-done.1.x_ref, bf16[512,512]{1,0:T(8,128)(2,1)} %constant.12.clone.w_ref), custom_call_target="tpu_custom_call" | custom-call | flops 671088640 | bytes 5242880 | tf_op jit(solution)/shard_map/dft/pallas_call | solution.py:101
  76.9 8.5 %mix.3 = bf16[640,1024]{1,0:T(8,128)(2,1)} custom-call(bf16[2,16,384,384]{3,2,1,0:T(8,128)(2,1)} %coefs.1.g_ref, bf16[16,128,320]{2,1,0:T(8,128)(2,1)} %dft.5.b_ref.a_ref, bf16[16,128,320]{2,1,0:T(8,128)(2,1)} %dft.6.c_ref.b_ref, bf16[16,128,320]{2,1,0:T(8,128)(2,1)} %dft.7.c_ref, f32[3,320]{1,0:T(4,128)} %tile.10.theta_ref, ...), custom_call_target="tpu_custom_call" | custom-call | flops 4000000000 | bytes 16000000 | tf_op jit(solution)/shard_map/mix/pallas_call | solution.py:206
  85.4 12.1 %all-to-all-start.3 = ((bf16[8,80,1024]{2,1,0:T(8,128)(2,1)}), bf16[8,80,1024]{2,1,0:T(8,128)(2,1)S(1)}, u32[]{:S(2)}, u32[]{:S(2)}) async-start(bf16[8,80,1024]{2,1,0:T(8,128)(2,1)} %bitcast.9), calls=%async_computation.3 | async-start | bytes 2621440 | tf_op jit(solution)/shard_map/all_to_all | solution.py:284
  97.5 0.0 collective-permute-done.x_ref
  97.5 3.9 %dft.4.a_ref = bf16[16,128,320]{2,1,0:T(8,128)(2,1)} custom-call(bf16[640,1024]{1,0:T(8,128)(2,1)} %collective-permute-done.x_ref, bf16[512,512]{1,0:T(8,128)(2,1)} %constant.12.clone.w_ref), custom_call_target="tpu_custom_call" | custom-call | flops 671088640 | bytes 5242880 | tf_op jit(solution)/shard_map/dft/pallas_call | solution.py:101
  101.4 8.5 %mix.2 = bf16[640,1024]{1,0:T(8,128)(2,1)} custom-call(bf16[2,16,384,384]{3,2,1,0:T(8,128)(2,1)} %coefs.1.g_ref, bf16[16,128,320]{2,1,0:T(8,128)(2,1)} %dft.4.a_ref, bf16[16,128,320]{2,1,0:T(8,128)(2,1)} %dft.5.b_ref.a_ref, bf16[16,128,320]{2,1,0:T(8,128)(2,1)} %dft.6.c_ref.b_ref, f32[3,320]{1,0:T(4,128)} %tile.10.theta_ref, ...), custom_call_target="tpu_custom_call" | custom-call | flops 4000000000 | bytes 16000000 | tf_op jit(solution)/shard_map/mix/pallas_call | solution.py:206
  109.9 0.0 copy-start.5
  109.9 0.0 copy-start.4
  109.9 6.2 %all-to-all-done.3 = bf16[8,80,1024]{2,1,0:T(8,128)(2,1)S(1)} async-done(((bf16[8,80,1024]{2,1,0:T(8,128)(2,1)}), bf16[8,80,1024]{2,1,0:T(8,128)(2,1)S(1)}, u32[]{:S(2)}, u32[]{:S(2)}) %all-to-all-start.3) | async-done | bytes 1310752 | tf_op jit(solution)/shard_map/all_to_all | solution.py:284
  116.1 0.0 copy-start.3
  116.1 3.8 %all-to-all-start.2 = ((bf16[8,80,1024]{2,1,0:T(8,128)(2,1)}), bf16[8,80,1024]{2,1,0:T(8,128)(2,1)S(1)}, u32[]{:S(2)}, u32[]{:S(2)}) async-start(bf16[8,80,1024]{2,1,0:T(8,128)(2,1)} %bitcast.10), calls=%async_computation.2 | async-start | bytes 2621440 | tf_op jit(solution)/shard_map/all_to_all | solution.py:286
  119.8 0.0 copy-done.5
  119.8 0.9 broadcast_in_dim.8.gain_ref
  120.7 0.0 copy-done.4
  120.7 0.6 broadcast_in_dim.7.b_in_ref
  121.3 0.0 copy-done.3
  121.3 9.1 %mlp.2.rest_0_ = bf16[4,8,64,640]{3,2,1,0:T(8,128)(2,1)} custom-call(bf16[640,1024]{1,0:T(8,128)(2,1)} %bitcast.18, bf16[4,8,64,640]{3,2,1,0:T(8,128)(2,1)} %x_ref.7, f32[640,1]{1,0:T(8,128)} %broadcast_in_dim.8.gain_ref, bf16[640,1280]{1,0:T(8,128)(2,1)} %w_in_ref.3, f32[1,1280]{1,0:T(1,128)} %broadcast_in_dim.7.b_in_ref, bf16[1280,640]{1,0:T(8,128)(2,1)} %w_out_ref.3), custom_call_target="tpu_custom_call" | custom-call | flops 3355443200 | bytes 12000000 | tf_op jit(solution)/shard_map/mlp/pallas_call | solution.py:245
  130.4 8.0 %all-to-all-done.2 = bf16[8,80,1024]{2,1,0:T(8,128)(2,1)S(1)} async-done(((bf16[8,80,1024]{2,1,0:T(8,128)(2,1)}), bf16[8,80,1024]{2,1,0:T(8,128)(2,1)S(1)}, u32[]{:S(2)}, u32[]{:S(2)}) %all-to-all-start.2) | async-done | bytes 1310752 | tf_op jit(solution)/shard_map/all_to_all | solution.py:286
  138.4 0.0 copy-start
  138.4 1.1 copy-done
  139.5 9.1 %mlp.3 = bf16[4,8,64,640]{3,2,1,0:T(8,128)(2,1)} custom-call(bf16[640,1024]{1,0:T(8,128)(2,1)} %bitcast.11, bf16[4,8,64,640]{3,2,1,0:T(8,128)(2,1)} %x_ref.7, f32[640,1]{1,0:T(8,128)} %broadcast_in_dim.8.gain_ref, bf16[640,1280]{1,0:T(8,128)(2,1)} %w_in_ref.3, f32[1,1280]{1,0:T(1,128)} %broadcast_in_dim.7.b_in_ref, ...), custom_call_target="tpu_custom_call", output_to_operand_aliasing={{}: (6, {})} | custom-call | flops 3355443200 | bytes 12000000 | tf_op jit(solution)/shard_map/mlp/pallas_call | solution.py:245
  (1 shorter events, 0.0 us)
Async XLA Ops:
  3.8 24.8 %all-to-all-start.1 = ((bf16[8,80,1024]{2,1,0:T(8,128)(2,1)}), bf16[8,80,1024]{2,1,0:T(8,128)(2,1)S(1)}, u32[]{:S(2)}, u32[]{:S(2)}) async-start(bf16[8,80,1024]{2,1,0:T(8,128)(2,1)} %bitcast.17), calls=%async_computation.1 | async-start | bytes 2621440 | tf_op jit(solution)/shard_map/all_to_all | solution.py:274
  28.6 7.7 %copy-start.2 = (bf16[8,80,1024]{2,1,0:T(8,128)(2,1)}, bf16[8,80,1024]{2,1,0:T(8,128)(2,1)S(1)}, u32[]{:S(2)}) copy-start(bf16[8,80,1024]{2,1,0:T(8,128)(2,1)S(1)} %all-to-all-done.1) | copy-start | bytes 3932164
  28.6 24.7 %all-to-all-start = ((bf16[8,80,1024]{2,1,0:T(8,128)(2,1)}), bf16[8,80,1024]{2,1,0:T(8,128)(2,1)S(1)}, u32[]{:S(2)}, u32[]{:S(2)}) async-start(bf16[8,80,1024]{2,1,0:T(8,128)(2,1)} %bitcast.16), calls=%async_computation | async-start | bytes 2621440 | tf_op jit(solution)/shard_map/all_to_all | solution.py:275
  32.2 40.8 %collective-permute-start.1 = (bf16[640,1024]{1,0:T(8,128)(2,1)S(1)}, bf16[640,1024]{1,0:T(8,128)(2,1)}, u32[]{:S(2)}, u32[]{:S(2)}) collective-permute-start(bf16[640,1024]{1,0:T(8,128)(2,1)S(1)} %bitcast.14), channel_id=1, source_target_pairs={{8,0},{16,8},{24,16},{32,24},{40,32},{48,40},{56,48},{64,56},{72,6... | collective-permute-start | bytes 3932168 | tf_op jit(solution)/shard_map/ppermute | solution.py:276
  53.3 11.2 %copy-start.1 = (bf16[8,80,1024]{2,1,0:T(8,128)(2,1)}, bf16[8,80,1024]{2,1,0:T(8,128)(2,1)S(1)}, u32[]{:S(2)}) copy-start(bf16[8,80,1024]{2,1,0:T(8,128)(2,1)S(1)} %all-to-all-done) | copy-start | bytes 3932164
  53.3 44.2 %collective-permute-start = (bf16[640,1024]{1,0:T(8,128)(2,1)S(1)}, bf16[640,1024]{1,0:T(8,128)(2,1)}, u32[]{:S(2)}, u32[]{:S(2)}) collective-permute-start(bf16[640,1024]{1,0:T(8,128)(2,1)S(1)} %bitcast.12), channel_id=1, source_target_pairs={{0,8},{8,16},{16,24},{24,32},{32,40},{40,48},{48,56},{56,64},{64,7... | collective-permute-start | bytes 3932168 | tf_op jit(solution)/shard_map/ppermute | solution.py:277
  56.8 7.7 %copy-start.6 = (f32[3,80]{1,0:T(4,128)S(1)}, f32[3,80]{1,0:T(4,128)}, u32[]{:S(2)}) copy-start(f32[3,80]{1,0:T(4,128)} %param.13) | copy-start | bytes 2884
  85.4 30.7 %all-to-all-start.3 = ((bf16[8,80,1024]{2,1,0:T(8,128)(2,1)}), bf16[8,80,1024]{2,1,0:T(8,128)(2,1)S(1)}, u32[]{:S(2)}, u32[]{:S(2)}) async-start(bf16[8,80,1024]{2,1,0:T(8,128)(2,1)} %bitcast.9), calls=%async_computation.3 | async-start | bytes 2621440 | tf_op jit(solution)/shard_map/all_to_all | solution.py:284
  109.9 10.0 %copy-start.5 = (f32[640]{0:T(1024)S(1)}, f32[640]{0:T(1024)}, u32[]{:S(2)}) copy-start(f32[640]{0:T(1024)} %param.16) | copy-start | bytes 7684
  109.9 10.8 %copy-start.4 = (f32[1280]{0:T(1024)S(1)}, f32[1280]{0:T(1024)}, u32[]{:S(2)}) copy-start(f32[1280]{0:T(1024)} %param.18) | copy-start | bytes 15364
  116.1 5.2 %copy-start.3 = (bf16[8,80,1024]{2,1,0:T(8,128)(2,1)}, bf16[8,80,1024]{2,1,0:T(8,128)(2,1)S(1)}, u32[]{:S(2)}) copy-start(bf16[8,80,1024]{2,1,0:T(8,128)(2,1)S(1)} %all-to-all-done.3) | copy-start | bytes 3932164
  116.1 22.3 %all-to-all-start.2 = ((bf16[8,80,1024]{2,1,0:T(8,128)(2,1)}), bf16[8,80,1024]{2,1,0:T(8,128)(2,1)S(1)}, u32[]{:S(2)}, u32[]{:S(2)}) async-start(bf16[8,80,1024]{2,1,0:T(8,128)(2,1)} %bitcast.10), calls=%async_computation.2 | async-start | bytes 2621440 | tf_op jit(solution)/shard_map/all_to_all | solution.py:286
  138.4 1.1 copy-start
where the time goes:
time: 149 us
  Pallas kernels  65.9 us (44%)
  waiting for transfers between devices  45.1 us (30%)
  starting transfers between devices  31.9 us (21%)
  local copies, waits for them, and re-layouts  5.58 us (4%)
    pallas_call x2, Pallas kernels, mlp(): pl.pallas_call(mlp_kernel, grid=(ENS,), in_specs=[pl.BlockSpec((CHAN, wid...  18.2 us
    pallas_call x2, Pallas kernels, mix(): pl.pallas_call(mix_kernel, grid=(FB // STEP,), in_specs=[pl.BlockSpec((1,...  17 us
    all_to_all x1, waiting for transfers between devices, shards(): high = swap(pack(fields, 1))  16 us
    pallas_call x4, Pallas kernels, dft(): pl.pallas_call(dft_rows_kernel, out_shape=jax.ShapeDtypeStruct((FB, HALF...  15.6 us
    all_to_all x1, waiting for transfers between devices, shards(): low = swap(pack(fields, 0))  14.9 us
    all_to_all x1, starting transfers between devices, shards(): swap(mix(coef, 1, (spec_low, spec_high, spec_after), theta4, back))  12.1 us
    all_to_all x1, waiting for transfers between devices, shards(): swap(mix(coef, 0, (spec_before, spec_low, spec_high), theta4, back))  7.98 us
    pallas_call x1, Pallas kernels, coefs(): pl.pallas_call(coef_kernel, grid=(2,), in_specs=[smem, smem, smem, pl.Blo...  7.67 us
  transfers between devices with their start and end apart: 6, of which 4 were waited for; matrix products, arithmetic and copies ran while one was open for 3% of the time, Pallas kernels for 36%

commit v1 on v0

--- a/solution.py
+++ b/solution.py
@@ -28,6 +28,7 @@
 WIN = 12
 PTS = ENS * HALF * CHUNK
 HID = 1280
+MID = CHAN // 2
 VMEM = 56 * 1024 * 1024
 
 
@@ -57,23 +58,30 @@
     return pl.CostEstimate(flops=int(flops), bytes_accessed=int(nbytes), transcendentals=0)
 
 
-def pack_kernel(x_ref, o_ref):
-    x = x_ref[0].reshape(HALF * CHUNK, CHAN)
-    o_ref[...] = x.T
-
-
-def pack(fields, half):
+def pack_kernel(turn_ref, x_ref, *rest):
+    o_ref = rest[-1]
+    x = x_ref[0].reshape(HALF * CHUNK, CHAN).T
+    at = pl.multiple_of(turn_ref[0] * MID, MID)
+    o_ref[pl.ds(at, MID), :] = x[:MID]
+    o_ref[pl.ds(MID - at, MID), :] = x[MID:]
+
+
+def pack(turn, fields, half, *after):
     wide = HALF * CHUNK
     return pl.pallas_call(
         pack_kernel,
         grid=(ENS,),
-        in_specs=[pl.BlockSpec((1, HALF, CHUNK, CHAN), lambda e: (e, half, 0, 0))],
+        in_specs=[
+            pl.BlockSpec(memory_space=pltpu.SMEM),
+            pl.BlockSpec((1, HALF, CHUNK, CHAN), lambda e: (e, half, 0, 0)),
+        ]
+        + [pl.BlockSpec(memory_space=pl.ANY)] * len(after),
         out_specs=pl.BlockSpec((CHAN, wide), lambda e: (0, e)),
         out_shape=jax.ShapeDtypeStruct((CHAN, PTS), BF16),
         compiler_params=params("arbitrary"),
         cost_estimate=cost(0, 4 * CHAN * PTS),
         name="pack",
-    )(fields)
+    )(turn, fields, *after)
 
 
 def dft_rows_kernel(x_ref, w_ref, o_ref):
@@ -107,7 +115,8 @@
     )(received, onward)
 
 
-def coef_kernel(start_ref, count_ref, first_ref, k_ref, w_ref, o_ref):
+def coef_kernel(start_ref, count_ref, first_ref, k_ref, w_ref, *rest):
+    o_ref = rest[-1]
     half = pl.program_id(0)
     kern = k_ref[...].astype(BF16)
     hat = lax.dot_general(w_ref[...], kern, (((1,), (1,)), ((), ())), preferred_element_type=F32)
@@ -141,7 +150,7 @@
             o_ref[0, :, at + FS : at + 2 * FS, :] = low
 
 
-def coefs(row_start, row_count, first, kernel, onward):
+def coefs(row_start, row_count, first, kernel, onward, *after):
     smem = pl.BlockSpec(memory_space=pltpu.SMEM)
     taps = HALF * SLOTS * KB
     size = HALF * KB * 2 * FS
@@ -154,13 +163,14 @@
             smem,
             pl.BlockSpec((None, taps, NLON), lambda h: (h, 0, 0)),
             pl.BlockSpec((NLON, NLON), lambda h: (0, 0)),
-        ],
+        ]
+        + [pl.BlockSpec(memory_space=pl.ANY)] * len(after),
         out_specs=pl.BlockSpec((1, FB, size, WIN * 2 * FS), lambda h: (h, 0, 0, 0)),
         out_shape=jax.ShapeDtypeStruct((2, FB, size, WIN * 2 * FS), BF16),
         compiler_params=params("arbitrary"),
         cost_estimate=cost(8e9, 1e7),
         name="coefs",
-    )(row_start, row_count, first, kernel.reshape(2, taps, NLON), onward)
+    )(row_start, row_count, first, kernel.reshape(2, taps, NLON), onward, *after)
 
 
 STEP = 4
@@ -223,9 +233,11 @@
     )(coef, *spectra, theta, back)
 
 
-def mlp_kernel(y_ref, x_ref, gain_ref, w_in_ref, b_in_ref, w_out_ref, *rest):
+def mlp_kernel(turn_ref, y_ref, x_ref, gain_ref, w_in_ref, b_in_ref, w_out_ref, *rest):
     o_ref = rest[-1]
-    values = y_ref[...].astype(F32)
+    at = pl.multiple_of(turn_ref[0] * MID, MID)
+    values = jnp.concatenate([y_ref[pl.ds(at, MID), :], y_ref[pl.ds(MID - at, MID), :]], axis=0)
+    values = values.astype(F32)
     mean = jnp.mean(values, axis=0, keepdims=True)
     away = values - mean
     var = jnp.mean(away * away, axis=0, keepdims=True)
@@ -237,7 +249,7 @@
     o_ref[0] = (x + branch).astype(BF16).reshape(HALF, CHUNK, CHAN)
 
 
-def mlp(y, fields, half, gain, w_in, b_in, w_out, before=None):
+def mlp(turn, y, fields, half, gain, w_in, b_in, w_out, before=None):
     wide = HALF * CHUNK
     points = pl.BlockSpec((1, HALF, CHUNK, CHAN), lambda e: (e, half, 0, 0))
     whole = lambda *shape: pl.BlockSpec(shape, lambda e: (0, 0))
@@ -246,6 +258,7 @@
         mlp_kernel,
         grid=(ENS,),
         in_specs=[
+            pl.BlockSpec(memory_space=pltpu.SMEM),
             pl.BlockSpec((CHAN, wide), lambda e: (0, e)),
             points,
             whole(CHAN, 1),
@@ -256,37 +269,54 @@
         + [pl.BlockSpec(memory_space=pl.ANY)] * len(extra),
         out_specs=points,
         out_shape=jax.ShapeDtypeStruct((ENS, ROWS, CHUNK, CHAN), BF16),
-        input_output_aliases={6: 0} if extra else {},
+        input_output_aliases={7: 0} if extra else {},
         compiler_params=params("arbitrary"),
         cost_estimate=cost(4 * PTS * CHAN * HID, 1.2e7),
         name="mlp",
-    )(y, fields, gain, w_in, b_in, w_out, *extra)
+    )(turn, y, fields, gain, w_in, b_in, w_out, *extra)
+
+
+def turned(lat):
+    return (lat // 2) % 2
+
+
+def band_perm(lats, lons, step):
+    pairs = []
+    for lat in range(lats):
+        if 0 <= lat + step < lats:
+            cross = (turned(lat) ^ turned(lat + step)) * (lons // 2)
+            pairs += [(lat * lons + t, (lat + step) * lons + (t ^ cross)) for t in range(lons)]
+    return pairs
 
 
 def shards(fields, kernel, theta, row_start, row_count, norm_gain, w_in, b_in, w_out):
     onward, back = (jnp.asarray(t) for t in tables())
-    size = lax.axis_size("lat")
-    up = [(i, i + 1) for i in range(size - 1)]
-    down = [(j, i) for i, j in up]
+    lats, lons = lax.axis_size("lat"), lax.axis_size("lon")
+    lat = lax.axis_index("lat").astype(jnp.int32)
+    turn = turned(lat).reshape(1)
     swap = functools.partial(
         lax.all_to_all, axis_name="lon", split_axis=0, concat_axis=0, tiled=True
     )
-    low = swap(pack(fields, 0))
-    high = swap(pack(fields, 1))
-    after = lax.ppermute(low, "lat", down)
-    before = lax.ppermute(high, "lat", up)
-    first = (lax.axis_index("lat") * ROWS).astype(jnp.int32).reshape(1)
-    coef = coefs(row_start, row_count, first, kernel, onward)
-    theta4 = jnp.tile(theta, (1, ENS))
+    shift = lambda v, step: lax.ppermute(v, ("lat", "lon"), band_perm(lats, lons, step))
+    other = lax.ppermute(theta, "lon", [(t, t ^ (lons // 2)) for t in range(lons)])
+    theta4 = jnp.tile(jnp.where(turn[0] == 1, other, theta), (1, ENS))
+
+    packed_low = pack(turn, fields, 0)
+    low = swap(packed_low)
+    coef = coefs(row_start, row_count, (lat * ROWS).reshape(1), kernel, onward, packed_low)
+    high = swap(pack(turn, fields, 1, coef))
+    after = shift(low, -1)
     spec_low = dft(low, onward)
+    high, spec_low = lax.optimization_barrier((high, spec_low))
+    before = shift(high, 1)
+    spec_after = dft(after, onward)
     spec_high = dft(high, onward)
-    spec_after = dft(after, onward)
     conv_high = swap(mix(coef, 1, (spec_low, spec_high, spec_after), theta4, back))
     spec_before = dft(before, onward)
     conv_low = swap(mix(coef, 0, (spec_before, spec_low, spec_high), theta4, back))
     rest = (norm_gain[:, None], w_in, b_in[None, :], w_out)
-    out = mlp(conv_high, fields, 1, *rest)
-    return mlp(conv_low, fields, 0, *rest, before=out)
+    out = mlp(turn, conv_high, fields, 1, *rest)
+    return mlp(turn, conv_low, fields, 0, *rest, before=out)
 
 
 def solution(mesh):

time: 149 us -> 128 us (0.86)
  waiting for transfers between devices: 45.1 us -> 29.2 us
  starting transfers between devices: 31.9 us -> 26.7 us
    all_to_all x2, waiting for transfers between devices: 30.9 us -> 16.1 us  [the longest x1 10.2 us: shards(): high = swap(pack(turn, fields, 1, coef))]
    all_to_all x1, starting transfers between devices: 12.1 us -> 3.75 us  [shards(): swap(mix(coef, 1, (spec_low, spec_high, spec_after), theta4, back))]
    ppermute x2 -> x3, starting transfers between devices: 6.23 us -> 9.46 us  [the longest x2 7.74 us: shards(): lax.ppermute(v, ('lat', 'lon'), band_perm(lats, lons, step))]
  transfers between devices with their start and end apart: 6 -> 7, of which waited for: 4 -> 4; matrix products, arithmetic and copies ran while one was open for 3% -> 3% of each run, Pallas kernels for 36% -> 42%
where the time goes in v1:
time: 128 us
  Pallas kernels  65.9 us (51%)
  waiting for transfers between devices  29.2 us (23%)
  starting transfers between devices  26.7 us (21%)
  local copies, waits for them, and re-layouts  5.65 us (4%)
    pallas_call x2, Pallas kernels, mlp(): pl.pallas_call(mlp_kernel, grid=(ENS,), in_specs=[pl.BlockSpec(memory_spa...  18.3 us
    pallas_call x2, Pallas kernels, mix(): pl.pallas_call(mix_kernel, grid=(FB // STEP,), in_specs=[pl.BlockSpec((1,...  17 us
    pallas_call x4, Pallas kernels, dft(): pl.pallas_call(dft_rows_kernel, out_shape=jax.ShapeDtypeStruct((FB, HALF...  15.6 us
    all_to_all x1, waiting for transfers between devices, shards(): high = swap(pack(turn, fields, 1, coef))  10.2 us
    all_to_all x1, waiting for transfers between devices, shards(): swap(mix(coef, 0, (spec_before, spec_low, spec_high), theta4, back))  8.03 us
    ppermute x2, starting transfers between devices, shards(): lax.ppermute(v, ('lat', 'lon'), band_perm(lats, lons, step))  7.74 us
    pallas_call x1, Pallas kernels, coefs(): pl.pallas_call(coef_kernel, grid=(2,), in_specs=[smem, smem, smem, pl.Blo...  7.63 us
    pallas_call x2, Pallas kernels, pack(): pl.pallas_call(pack_kernel, grid=(ENS,), in_specs=[pl.BlockSpec(memory_sp...  7.42 us
  transfers between devices with their start and end apart: 7, of which 4 were waited for; matrix products, arithmetic and copies ran while one was open for 3% of the time, Pallas kernels for 42%

profile of v1, /device:TPU:1, one launch (start us, length us, event | category | flops | bytes accessed | tf_op | source)
XLA Modules:
  0.0 127.6 jit_solution(14130897728591439195)
XLA Ops:
  0.0 3.7 %pack.2.rest_0_ = bf16[640,1024]{1,0:T(8,128)(2,1)} custom-call(s32[1]{0:T(128)} %bitcast.turn_ref, bf16[4,8,64,640]{3,2,1,0:T(8,128)(2,1)} %x_ref.7), custom_call_target="tpu_custom_call" | custom-call | bytes 2621440 | tf_op jit(solution)/shard_map/pack/pallas_call | solution.py:71
  3.7 0.0 copy-start.4
  3.7 6.3 %all-to-all-start.1 = ((bf16[8,80,1024]{2,1,0:T(8,128)(2,1)}), bf16[8,80,1024]{2,1,0:T(8,128)(2,1)S(1)}, u32[]{:S(2)}, u32[]{:S(2)}) async-start(bf16[8,80,1024]{2,1,0:T(8,128)(2,1)} %bitcast.17), calls=%async_computation.1 | async-start | bytes 2621440 | tf_op jit(solution)/shard_map/all_to_all | solution.py:305
  10.0 0.0 copy-done.4
  10.0 0.3 copy.14
  10.3 1.0 reshape.23.k_ref
  11.4 7.6 %coefs.1.rest_0_.g_ref = bf16[2,16,384,384]{3,2,1,0:T(8,128)(2,1)} custom-call(s32[8]{0:T(128)} %start_ref.1, s32[8]{0:T(128)} %count_ref.1, s32[1]{0:T(128)} %bitcast.1.first_ref, f32[2,108,512]{2,1,0:T(8,128)} %reshape.23.k_ref, bf16[512,512]{1,0:T(8,128)(2,1)} %constant.37.clone.w_ref, bf16[640,1024]{1,0:T(8,128)(2,1)} %pack.2.rest_0_), custom_call_target="tpu_custom_call" | custom-call | flops 8000000000 | bytes 10000000 | tf_op jit(solution)/shard_map/coefs/pallas_call | solution.py:157
  19.0 3.7 %pack.3 = bf16[640,1024]{1,0:T(8,128)(2,1)} custom-call(s32[1]{0:T(128)} %bitcast.turn_ref, bf16[4,8,64,640]{3,2,1,0:T(8,128)(2,1)} %x_ref.7, bf16[2,16,384,384]{3,2,1,0:T(8,128)(2,1)} %coefs.1.rest_0_.g_ref), custom_call_target="tpu_custom_call" | custom-call | bytes 2621440 | tf_op jit(solution)/shard_map/pack/pallas_call | solution.py:71
  22.7 0.0 copy-start.7
  22.7 5.9 %all-to-all-done.1 = bf16[8,80,1024]{2,1,0:T(8,128)(2,1)S(1)} async-done(((bf16[8,80,1024]{2,1,0:T(8,128)(2,1)}), bf16[8,80,1024]{2,1,0:T(8,128)(2,1)S(1)}, u32[]{:S(2)}, u32[]{:S(2)}) %all-to-all-start.1) | async-done | bytes 1310752 | tf_op jit(solution)/shard_map/all_to_all | solution.py:305
  28.6 0.0 copy-start.1
  28.7 3.6 %all-to-all-start = ((bf16[8,80,1024]{2,1,0:T(8,128)(2,1)}), bf16[8,80,1024]{2,1,0:T(8,128)(2,1)S(1)}, u32[]{:S(2)}, u32[]{:S(2)}) async-start(bf16[8,80,1024]{2,1,0:T(8,128)(2,1)} %bitcast.18), calls=%async_computation | async-start | bytes 2621440 | tf_op jit(solution)/shard_map/all_to_all | solution.py:307
  32.2 2.8 %collective-permute-start.2 = (bf16[640,1024]{1,0:T(8,128)(2,1)S(1)}, bf16[640,1024]{1,0:T(8,128)(2,1)}, u32[]{:S(2)}, u32[]{:S(2)}) collective-permute-start(bf16[640,1024]{1,0:T(8,128)(2,1)S(1)} %bitcast.13), channel_id=1, source_target_pairs={{8,0},{9,1},{10,2},{11,3},{12,4},{13,5},{14,6},{15,7},{16,12},{17,... | collective-permute-start | bytes 3932168 | tf_op jit(solution)/shard_map/ppermute | solution.py:300
  35.0 0.0 copy-done.7
  35.0 1.7 %collective-permute-start.1 = (f32[3,80]{1,0:T(4,128)S(1)}, f32[3,80]{1,0:T(4,128)S(1)}, u32[]{:S(2)}, u32[]{:S(2)}) collective-permute-start(f32[3,80]{1,0:T(4,128)S(1)} %copy-done.7), channel_id=1, source_target_pairs={{0,4},{1,5},{2,6},{3,7},{4,0},{5,1},{6,2},{7,3},{8,12},{9,13},{10,... | collective-permute-start | bytes 2888 | tf_op jit(solution)/shard_map/ppermute | solution.py:301
  36.7 0.0 copy-done.1
  36.7 3.9 %dft.4.b_ref.a_ref = bf16[16,128,320]{2,1,0:T(8,128)(2,1)} custom-call(bf16[640,1024]{1,0:T(8,128)(2,1)} %bitcast.14, bf16[512,512]{1,0:T(8,128)(2,1)} %constant.37.clone.w_ref), custom_call_target="tpu_custom_call" | custom-call | flops 671088640 | bytes 5242880 | tf_op jit(solution)/shard_map/dft/pallas_call | solution.py:109
  40.6 10.2 %all-to-all-done = bf16[8,80,1024]{2,1,0:T(8,128)(2,1)S(1)} async-done(((bf16[8,80,1024]{2,1,0:T(8,128)(2,1)}), bf16[8,80,1024]{2,1,0:T(8,128)(2,1)S(1)}, u32[]{:S(2)}, u32[]{:S(2)}) %all-to-all-start) | async-done | bytes 1310752 | tf_op jit(solution)/shard_map/all_to_all | solution.py:307
  50.8 0.0 copy-start.2
  50.8 5.0 %collective-permute-start = (bf16[640,1024]{1,0:T(8,128)(2,1)S(1)}, bf16[640,1024]{1,0:T(8,128)(2,1)}, u32[]{:S(2)}, u32[]{:S(2)}) collective-permute-start(bf16[640,1024]{1,0:T(8,128)(2,1)S(1)} %bitcast.15), channel_id=1, source_target_pairs={{0,8},{1,9},{2,10},{3,11},{4,12},{5,13},{6,14},{7,15},{8,20},{9,21... | collective-permute-start | bytes 3932168 | tf_op jit(solution)/shard_map/ppermute | solution.py:300
  55.8 0.0 collective-permute-done.1
  55.8 0.7 tile.10.theta_ref
  56.5 0.0 copy-done.2
  56.5 3.9 %dft.6.c_ref.b_ref = bf16[16,128,320]{2,1,0:T(8,128)(2,1)} custom-call(bf16[640,1024]{1,0:T(8,128)(2,1)} %bitcast.16, bf16[512,512]{1,0:T(8,128)(2,1)} %constant.37.clone.w_ref), custom_call_target="tpu_custom_call" | custom-call | flops 671088640 | bytes 5242880 | tf_op jit(solution)/shard_map/dft/pallas_call | solution.py:109
  60.4 0.0 collective-permute-done.2.x_ref
  60.4 3.9 %dft.7.c_ref = bf16[16,128,320]{2,1,0:T(8,128)(2,1)} custom-call(bf16[640,1024]{1,0:T(8,128)(2,1)} %collective-permute-done.2.x_ref, bf16[512,512]{1,0:T(8,128)(2,1)} %constant.37.clone.w_ref), custom_call_target="tpu_custom_call" | custom-call | flops 671088640 | bytes 5242880 | tf_op jit(solution)/shard_map/dft/pallas_call | solution.py:109
  64.3 8.5 %mix.3 = bf16[640,1024]{1,0:T(8,128)(2,1)} custom-call(bf16[2,16,384,384]{3,2,1,0:T(8,128)(2,1)} %coefs.1.rest_0_.g_ref, bf16[16,128,320]{2,1,0:T(8,128)(2,1)} %dft.4.b_ref.a_ref, bf16[16,128,320]{2,1,0:T(8,128)(2,1)} %dft.6.c_ref.b_ref, bf16[16,128,320]{2,1,0:T(8,128)(2,1)} %dft.7.c_ref, f32[3,320]{1,0:T(4,128)} %tile.10.theta_ref, ...), custom_call_target="tpu_custom_call" | custom-call | flops 4000000000 | bytes 16000000 | tf_op jit(solution)/shard_map/mix/pallas_call | solution.py:216
  72.8 3.7 %all-to-all-start.3 = ((bf16[8,80,1024]{2,1,0:T(8,128)(2,1)}), bf16[8,80,1024]{2,1,0:T(8,128)(2,1)S(1)}, u32[]{:S(2)}, u32[]{:S(2)}) async-start(bf16[8,80,1024]{2,1,0:T(8,128)(2,1)} %bitcast.10), calls=%async_computation.3 | async-start | bytes 2621440 | tf_op jit(solution)/shard_map/all_to_all | solution.py:314
  76.6 0.0 collective-permute-done.x_ref
  76.6 3.9 %dft.5.a_ref = bf16[16,128,320]{2,1,0:T(8,128)(2,1)} custom-call(bf16[640,1024]{1,0:T(8,128)(2,1)} %collective-permute-done.x_ref, bf16[512,512]{1,0:T(8,128)(2,1)} %constant.37.clone.w_ref), custom_call_target="tpu_custom_call" | custom-call | flops 671088640 | bytes 5242880 | tf_op jit(solution)/shard_map/dft/pallas_call | solution.py:109
  80.5 8.5 %mix.2 = bf16[640,1024]{1,0:T(8,128)(2,1)} custom-call(bf16[2,16,384,384]{3,2,1,0:T(8,128)(2,1)} %coefs.1.rest_0_.g_ref, bf16[16,128,320]{2,1,0:T(8,128)(2,1)} %dft.5.a_ref, bf16[16,128,320]{2,1,0:T(8,128)(2,1)} %dft.4.b_ref.a_ref, bf16[16,128,320]{2,1,0:T(8,128)(2,1)} %dft.6.c_ref.b_ref, f32[3,320]{1,0:T(4,128)} %tile.10.theta_ref, ...), custom_call_target="tpu_custom_call" | custom-call | flops 4000000000 | bytes 16000000 | tf_op jit(solution)/shard_map/mix/pallas_call | solution.py:216
  89.0 0.0 copy-start.6
  89.0 0.0 copy-start.5
  89.0 5.0 %all-to-all-done.3 = bf16[8,80,1024]{2,1,0:T(8,128)(2,1)S(1)} async-done(((bf16[8,80,1024]{2,1,0:T(8,128)(2,1)}), bf16[8,80,1024]{2,1,0:T(8,128)(2,1)S(1)}, u32[]{:S(2)}, u32[]{:S(2)}) %all-to-all-start.3) | async-done | bytes 1310752 | tf_op jit(solution)/shard_map/all_to_all | solution.py:314
  94.0 0.0 copy-start.3
  94.0 1.1 copy-done.3
  95.1 3.6 %all-to-all-start.2 = ((bf16[8,80,1024]{2,1,0:T(8,128)(2,1)}), bf16[8,80,1024]{2,1,0:T(8,128)(2,1)S(1)}, u32[]{:S(2)}, u32[]{:S(2)}) async-start(bf16[8,80,1024]{2,1,0:T(8,128)(2,1)} %bitcast.11), calls=%async_computation.2 | async-start | bytes 2621440 | tf_op jit(solution)/shard_map/all_to_all | solution.py:316
  98.7 0.0 copy-done.6
  98.7 0.9 broadcast_in_dim.8.gain_ref
  99.6 0.0 copy-done.5
  99.6 0.6 broadcast_in_dim.7.b_in_ref
  100.2 9.1 %mlp.2.rest_0_ = bf16[4,8,64,640]{3,2,1,0:T(8,128)(2,1)} custom-call(s32[1]{0:T(128)} %bitcast.turn_ref, bf16[640,1024]{1,0:T(8,128)(2,1)} %bitcast.19, bf16[4,8,64,640]{3,2,1,0:T(8,128)(2,1)} %x_ref.7, f32[640,1]{1,0:T(8,128)} %broadcast_in_dim.8.gain_ref, bf16[640,1280]{1,0:T(8,128)(2,1)} %w_in_ref.3, f32[1,1280]{1,0:T(1,128)} %broadcast_in_dim.7.b_in_ref, ...), custom_call_target="tpu_custom_call" | custom-call | flops 3355443200 | bytes 12000000 | tf_op jit(solution)/shard_map/mlp/pallas_call | solution.py:257
  109.3 8.0 %all-to-all-done.2 = bf16[8,80,1024]{2,1,0:T(8,128)(2,1)S(1)} async-done(((bf16[8,80,1024]{2,1,0:T(8,128)(2,1)}), bf16[8,80,1024]{2,1,0:T(8,128)(2,1)S(1)}, u32[]{:S(2)}, u32[]{:S(2)}) %all-to-all-start.2) | async-done | bytes 1310752 | tf_op jit(solution)/shard_map/all_to_all | solution.py:316
  117.4 0.0 copy-start
  117.4 1.1 copy-done
  118.5 9.1 %mlp.3 = bf16[4,8,64,640]{3,2,1,0:T(8,128)(2,1)} custom-call(s32[1]{0:T(128)} %bitcast.turn_ref, bf16[640,1024]{1,0:T(8,128)(2,1)} %bitcast.12, bf16[4,8,64,640]{3,2,1,0:T(8,128)(2,1)} %x_ref.7, f32[640,1]{1,0:T(8,128)} %broadcast_in_dim.8.gain_ref, bf16[640,1280]{1,0:T(8,128)(2,1)} %w_in_ref.3, ...), custom_call_target="tpu_custom_call", output_to_operand_aliasing={{}: (7, {})} | custom-call | flops 3355443200 | bytes 12000000 | tf_op jit(solution)/shard_map/mlp/pallas_call | solution.py:257
  (2 shorter events, 0.0 us)
Async XLA Ops:
  3.7 6.3 %copy-start.4 = (f32[8,9,3,512]{3,0,2,1:T(8,128)S(1)}, f32[8,9,3,512]{3,0,2,1:T(8,128)}, u32[]{:S(2)}) copy-start(f32[8,9,3,512]{3,0,2,1:T(8,128)} %param.12) | copy-start | bytes 1327108
  3.7 25.0 %all-to-all-start.1 = ((bf16[8,80,1024]{2,1,0:T(8,128)(2,1)}), bf16[8,80,1024]{2,1,0:T(8,128)(2,1)S(1)}, u32[]{:S(2)}, u32[]{:S(2)}) async-start(bf16[8,80,1024]{2,1,0:T(8,128)(2,1)} %bitcast.17), calls=%async_computation.1 | async-start | bytes 2621440 | tf_op jit(solution)/shard_map/all_to_all | solution.py:305
  22.7 12.3 %copy-start.7 = (f32[3,80]{1,0:T(4,128)S(1)}, f32[3,80]{1,0:T(4,128)}, u32[]{:S(2)}) copy-start(f32[3,80]{1,0:T(4,128)} %param.13) | copy-start | bytes 2884
  28.6 8.1 %copy-start.1 = (bf16[8,80,1024]{2,1,0:T(8,128)(2,1)}, bf16[8,80,1024]{2,1,0:T(8,128)(2,1)S(1)}, u32[]{:S(2)}) copy-start(bf16[8,80,1024]{2,1,0:T(8,128)(2,1)S(1)} %all-to-all-done.1) | copy-start | bytes 3932164
  28.7 22.2 %all-to-all-start = ((bf16[8,80,1024]{2,1,0:T(8,128)(2,1)}), bf16[8,80,1024]{2,1,0:T(8,128)(2,1)S(1)}, u32[]{:S(2)}, u32[]{:S(2)}) async-start(bf16[8,80,1024]{2,1,0:T(8,128)(2,1)} %bitcast.18), calls=%async_computation | async-start | bytes 2621440 | tf_op jit(solution)/shard_map/all_to_all | solution.py:307
  32.2 28.2 %collective-permute-start.2 = (bf16[640,1024]{1,0:T(8,128)(2,1)S(1)}, bf16[640,1024]{1,0:T(8,128)(2,1)}, u32[]{:S(2)}, u32[]{:S(2)}) collective-permute-start(bf16[640,1024]{1,0:T(8,128)(2,1)S(1)} %bitcast.13), channel_id=1, source_target_pairs={{8,0},{9,1},{10,2},{11,3},{12,4},{13,5},{14,6},{15,7},{16,12},{17,... | collective-permute-start | bytes 3932168 | tf_op jit(solution)/shard_map/ppermute | solution.py:300
  35.0 20.8 %collective-permute-start.1 = (f32[3,80]{1,0:T(4,128)S(1)}, f32[3,80]{1,0:T(4,128)S(1)}, u32[]{:S(2)}, u32[]{:S(2)}) collective-permute-start(f32[3,80]{1,0:T(4,128)S(1)} %copy-done.7), channel_id=1, source_target_pairs={{0,4},{1,5},{2,6},{3,7},{4,0},{5,1},{6,2},{7,3},{8,12},{9,13},{10,... | collective-permute-start | bytes 2888 | tf_op jit(solution)/shard_map/ppermute | solution.py:301
  50.8 5.7 %copy-start.2 = (bf16[8,80,1024]{2,1,0:T(8,128)(2,1)}, bf16[8,80,1024]{2,1,0:T(8,128)(2,1)S(1)}, u32[]{:S(2)}) copy-start(bf16[8,80,1024]{2,1,0:T(8,128)(2,1)S(1)} %all-to-all-done) | copy-start | bytes 3932164
  50.8 25.7 %collective-permute-start = (bf16[640,1024]{1,0:T(8,128)(2,1)S(1)}, bf16[640,1024]{1,0:T(8,128)(2,1)}, u32[]{:S(2)}, u32[]{:S(2)}) collective-permute-start(bf16[640,1024]{1,0:T(8,128)(2,1)S(1)} %bitcast.15), channel_id=1, source_target_pairs={{0,8},{1,9},{2,10},{3,11},{4,12},{5,13},{6,14},{7,15},{8,20},{9,21... | collective-permute-start | bytes 3932168 | tf_op jit(solution)/shard_map/ppermute | solution.py:300
  72.8 21.2 %all-to-all-start.3 = ((bf16[8,80,1024]{2,1,0:T(8,128)(2,1)}), bf16[8,80,1024]{2,1,0:T(8,128)(2,1)S(1)}, u32[]{:S(2)}, u32[]{:S(2)}) async-start(bf16[8,80,1024]{2,1,0:T(8,128)(2,1)} %bitcast.10), calls=%async_computation.3 | async-start | bytes 2621440 | tf_op jit(solution)/shard_map/all_to_all | solution.py:314
  89.0 9.7 %copy-start.6 = (f32[640]{0:T(1024)S(1)}, f32[640]{0:T(1024)}, u32[]{:S(2)}) copy-start(f32[640]{0:T(1024)} %param.16) | copy-start | bytes 7684
  89.0 10.6 %copy-start.5 = (f32[1280]{0:T(1024)S(1)}, f32[1280]{0:T(1024)}, u32[]{:S(2)}) copy-start(f32[1280]{0:T(1024)} %param.18) | copy-start | bytes 15364
  94.0 1.1 copy-start.3
  95.1 22.2 %all-to-all-start.2 = ((bf16[8,80,1024]{2,1,0:T(8,128)(2,1)}), bf16[8,80,1024]{2,1,0:T(8,128)(2,1)S(1)}, u32[]{:S(2)}, u32[]{:S(2)}) async-start(bf16[8,80,1024]{2,1,0:T(8,128)(2,1)} %bitcast.11), calls=%async_computation.2 | async-start | bytes 2621440 | tf_op jit(solution)/shard_map/all_to_all | solution.py:316
  117.4 1.1 copy-start

commit v2 on v1

--- a/solution.py
+++ b/solution.py
@@ -29,7 +29,11 @@
 PTS = ENS * HALF * CHUNK
 HID = 1280
 MID = CHAN // 2
-VMEM = 56 * 1024 * 1024
+LIMIT = 58 * 1024 * 1024
+GROUP = 2
+ANY = pl.BlockSpec(memory_space=pl.ANY)
+SMEM = pl.BlockSpec(memory_space=pltpu.SMEM)
+VMEM = pl.BlockSpec(memory_space=pltpu.VMEM)
 
 
 def tables():
@@ -51,40 +55,63 @@
 
 
 def params(*semantics):
-    return pltpu.CompilerParams(vmem_limit_bytes=VMEM, dimension_semantics=semantics)
+    return pltpu.CompilerParams(vmem_limit_bytes=LIMIT, dimension_semantics=semantics)
+
+
+def near(value):
+    return pltpu.with_memory_space_constraint(value, pltpu.VMEM)
+
+
+def far(value):
+    return pltpu.with_memory_space_constraint(value, pltpu.HBM)
 
 
 def cost(flops, nbytes):
     return pl.CostEstimate(flops=int(flops), bytes_accessed=int(nbytes), transcendentals=0)
 
 
-def pack_kernel(turn_ref, x_ref, *rest):
-    o_ref = rest[-1]
-    x = x_ref[0].reshape(HALF * CHUNK, CHAN).T
+def pack_kernel(half, turn_ref, x_ref, *rest):
+    o_ref, x_buf, o_buf, x_sem, o_sem = rest[-5:]
+    wide = HALF * CHUNK
+    copies = [
+        pltpu.make_async_copy(x_ref.at[e, pl.ds(half * HALF, HALF)], x_buf.at[e], x_sem.at[e])
+        for e in range(ENS)
+    ]
+    for c in copies:
+        c.start()
     at = pl.multiple_of(turn_ref[0] * MID, MID)
-    o_ref[pl.ds(at, MID), :] = x[:MID]
-    o_ref[pl.ds(MID - at, MID), :] = x[MID:]
+    outs = []
+    for e in range(ENS):
+        copies[e].wait()
+        x = x_buf[e].reshape(wide, CHAN).T
+        lanes = slice(e * wide, (e + 1) * wide)
+        o_buf[pl.ds(at, MID), lanes] = x[:MID]
+        o_buf[pl.ds(MID - at, MID), lanes] = x[MID:]
+        outs.append(pltpu.make_async_copy(o_buf.at[:, lanes], o_ref.at[:, lanes], o_sem.at[e]))
+        outs[e].start()
+    for c in outs:
+        c.wait()
 
 
 def pack(turn, fields, half, *after):
-    wide = HALF * CHUNK
     return pl.pallas_call(
-        pack_kernel,
-        grid=(ENS,),
-        in_specs=[
-            pl.BlockSpec(memory_space=pltpu.SMEM),
-            pl.BlockSpec((1, HALF, CHUNK, CHAN), lambda e: (e, half, 0, 0)),
-        ]
-        + [pl.BlockSpec(memory_space=pl.ANY)] * len(after),
-        out_specs=pl.BlockSpec((CHAN, wide), lambda e: (0, e)),
+        functools.partial(pack_kernel, half),
+        in_specs=[pl.BlockSpec(memory_space=pltpu.SMEM)] + [ANY] * (1 + len(after)),
+        out_specs=ANY,
         out_shape=jax.ShapeDtypeStruct((CHAN, PTS), BF16),
-        compiler_params=params("arbitrary"),
+        scratch_shapes=[
+            pltpu.VMEM((ENS, HALF, CHUNK, CHAN), BF16),
+            pltpu.VMEM((CHAN, PTS), BF16),
+            pltpu.SemaphoreType.DMA((ENS,)),
+            pltpu.SemaphoreType.DMA((ENS,)),
+        ],
+        compiler_params=params(),
         cost_estimate=cost(0, 4 * CHAN * PTS),
         name="pack",
     )(turn, fields, *after)
 
 
-def dft_rows_kernel(x_ref, w_ref, o_ref):
+def dft_rows(x_ref, w, o_ref, at):
     for pair in range(2):
         rows = [[], []]
         for e in range(ENS):
@@ -98,21 +125,23 @@
                 rows[r].append(jnp.concatenate(parts[r], axis=1))
         for r in range(2):
             x = jnp.concatenate(rows[r], axis=0)
-            s = lax.dot_general(
-                w_ref[...], x, (((1,), (1,)), ((), ())), preferred_element_type=F32
-            )
-            at = (pair * 2 + r) * 2 * FS
-            o_ref[:, at : at + 2 * FS, :] = s.astype(BF16).reshape(FB, 2 * FS, COLS)
+            s = lax.dot_general(w, x, (((1,), (1,)), ((), ())), preferred_element_type=F32)
+            row = at + (pair * 2 + r) * 2 * FS
+            o_ref[:, row : row + 2 * FS, :] = s.astype(BF16).reshape(FB, 2 * FS, COLS)
+
+
+def dft_kernel(x_ref, w_ref, o_ref):
+    dft_rows(x_ref, w_ref[...], o_ref, 0)
 
 
 def dft(received, onward):
     return pl.pallas_call(
-        dft_rows_kernel,
+        dft_kernel,
         out_shape=jax.ShapeDtypeStruct((FB, HALF * 2 * FS, COLS), BF16),
         compiler_params=params(),
         cost_estimate=cost(2 * HALF * NLON * NLON * COLS, 8 * CHAN * PTS),
         name="dft",
-    )(received, onward)
+    )(far(received), onward)
 
 
 def coef_kernel(start_ref, count_ref, first_ref, k_ref, w_ref, *rest):
@@ -174,106 +203,154 @@
 
 
 STEP = 4
-
-
-def mix_kernel(g_ref, a_ref, b_ref, c_ref, theta_ref, back_ref, o_ref, t_ref):
-    step = pl.program_id(0)
+STEPS = FB // STEP
+
+
+def conv_kernel(
+    half, g_ref, low_ref, high_ref, halo_ref, theta_ref, w_ref, back_ref, o_ref, *rest
+):
+    g_buf, s_buf, w_buf, t_buf, g_sem, low_sem, w_sem = rest
+    band = HALF * 2 * FS
+    halo_at, low_at, high_at = (2 * band, 0, band) if half else (0, band, 2 * band)
+    ws = [
+        pltpu.make_async_copy(ref, w_buf.at[n], w_sem.at[n]) for n, ref in enumerate((w_ref, back_ref))
+    ]
+    ws[0].start()
+    gs, lows = [], []
+    for s in range(STEPS):
+        part = pl.ds(s * STEP, STEP)
+        gs.append(pltpu.make_async_copy(g_ref.at[half, part], g_buf.at[part], g_sem.at[s]))
+        lows.append(
+            pltpu.make_async_copy(
+                low_ref.at[part], s_buf.at[part, pl.ds(low_at, band)], low_sem.at[s]
+            )
+        )
+        gs[s].start()
+        lows[s].start()
+    ws[1].start()
+    ws[0].wait()
+    dft_rows(high_ref, w_buf[0], s_buf, high_at)
+    dft_rows(halo_ref, w_buf[0], s_buf, halo_at)
     theta = [theta_ref[k : k + 1, :] for k in range(KB)]
-    for f in range(STEP):
-        x = jnp.concatenate([a_ref[f], b_ref[f], c_ref[f]], axis=0)
-        p = jnp.dot(g_ref[0, f], x, preferred_element_type=F32)
-        for i in range(HALF):
-            total = None
-            for k in range(KB):
-                at = (i * KB + k) * 2 * FS
-                term = p[at : at + 2 * FS, :] * theta[k]
-                total = term if total is None else total + term
-            t_ref[i, pl.ds((step * STEP + f) * 2 * FS, 2 * FS), :] = total.astype(BF16)
-
-    @pl.when(step == FB // STEP - 1)
-    def _():
-        for pair in range(2):
-            y = [
-                lax.dot_general(
-                    t_ref[pair * 2 + r],
-                    back_ref[...],
-                    (((0,), (0,)), ((), ())),
-                    preferred_element_type=F32,
-                ).astype(BF16)
-                for r in range(2)
-            ]
-            for e in range(ENS):
-                base = (e * 2 + pair) * 128
-                for d in range(LON_DEV):
-                    o_ref[d * CH : (d + 1) * CH, base : base + 128] = jnp.concatenate(
-                        [v[e * CH : (e + 1) * CH, d * CHUNK : (d + 1) * CHUNK] for v in y], axis=1
-                    )
-
-
-def mix(coef, half, spectra, theta, back):
+    for step in range(STEPS):
+        gs[step].wait()
+        lows[step].wait()
+        for block in range(step * STEP, (step + 1) * STEP):
+            p = jnp.dot(g_buf[block], s_buf[block], preferred_element_type=F32)
+            for i in range(HALF):
+                total = None
+                for k in range(KB):
+                    at = (i * KB + k) * 2 * FS
+                    term = p[at : at + 2 * FS, :] * theta[k]
+                    total = term if total is None else total + term
+                t_buf[i, block * 2 * FS : (block + 1) * 2 * FS, :] = total.astype(BF16)
+    ws[1].wait()
+    for pair in range(2):
+        y = [
+            lax.dot_general(
+                t_buf[pair * 2 + r],
+                w_buf[1],
+                (((0,), (0,)), ((), ())),
+                preferred_element_type=F32,
+            ).astype(BF16)
+            for r in range(2)
+        ]
+        for e in range(ENS):
+            base = (e * 2 + pair) * 128
+            for d in range(LON_DEV):
+                o_ref[d * CH : (d + 1) * CH, base : base + 128] = jnp.concatenate(
+                    [v[e * CH : (e + 1) * CH, d * CHUNK : (d + 1) * CHUNK] for v in y], axis=1
+                )
+
+
+def conv(coef, half, spec_low, high, halo, theta, onward, back):
     size = HALF * KB * 2 * FS
-    spec = pl.BlockSpec((STEP, HALF * 2 * FS, COLS), lambda s: (s, 0, 0))
+    span = WIN * 2 * FS
     return pl.pallas_call(
-        mix_kernel,
-        grid=(FB // STEP,),
-        in_specs=[
-            pl.BlockSpec((1, STEP, size, WIN * 2 * FS), lambda s: (half, s, 0, 0)),
-            spec,
-            spec,
-            spec,
-            pl.BlockSpec((KB, COLS), lambda s: (0, 0)),
-            pl.BlockSpec((NLON, NLON), lambda s: (0, 0)),
+        functools.partial(conv_kernel, half),
+        in_specs=[ANY, ANY, VMEM, VMEM, VMEM, ANY, ANY],
+        out_specs=VMEM,
+        out_shape=pltpu.VMEM((CHAN, PTS), BF16),
+        scratch_shapes=[
+            pltpu.VMEM((FB, size, span), BF16),
+            pltpu.VMEM((FB, span, COLS), BF16),
+            pltpu.VMEM((2, NLON, NLON), BF16),
+            pltpu.VMEM((HALF, NLON, COLS), BF16),
+            pltpu.SemaphoreType.DMA((STEPS,)),
+            pltpu.SemaphoreType.DMA((STEPS,)),
+            pltpu.SemaphoreType.DMA((2,)),
         ],
-        out_specs=pl.BlockSpec((CHAN, PTS), lambda s: (0, 0)),
-        out_shape=jax.ShapeDtypeStruct((CHAN, PTS), BF16),
-        scratch_shapes=[pltpu.VMEM((HALF, NLON, COLS), BF16)],
-        compiler_params=params("arbitrary"),
-        cost_estimate=cost(4e9, 1.6e7),
-        name="mix",
-    )(coef, *spectra, theta, back)
-
-
-def mlp_kernel(turn_ref, y_ref, x_ref, gain_ref, w_in_ref, b_in_ref, w_out_ref, *rest):
-    o_ref = rest[-1]
+        compiler_params=params(),
+        cost_estimate=cost(6e9, 1.2e7),
+        name="conv",
+    )(coef, spec_low, near(high), near(halo), theta, onward, back)
+
+
+def mlp_kernel(half, turn_ref, y_ref, x_ref, gain_ref, w_in_ref, b_in_ref, w_out_ref, *rest):
+    o_ref, x_buf, w_in_buf, w_out_buf, o_buf, x_sem, w_sem, o_sem = rest[-8:]
+    wide = HALF * CHUNK
+    rows = pl.ds(half * HALF, HALF)
+    first = pltpu.make_async_copy(w_in_ref, w_in_buf, w_sem.at[0])
+    second = pltpu.make_async_copy(w_out_ref, w_out_buf, w_sem.at[1])
+    xs = [
+        pltpu.make_async_copy(x_ref.at[e, rows], x_buf.at[e], x_sem.at[e]) for e in range(ENS)
+    ]
+    for c in [first, second, *xs]:
+        c.start()
     at = pl.multiple_of(turn_ref[0] * MID, MID)
-    values = jnp.concatenate([y_ref[pl.ds(at, MID), :], y_ref[pl.ds(MID - at, MID), :]], axis=0)
-    values = values.astype(F32)
-    mean = jnp.mean(values, axis=0, keepdims=True)
-    away = values - mean
-    var = jnp.mean(away * away, axis=0, keepdims=True)
-    normed = (away * lax.rsqrt(var + 1e-5) * gain_ref[...]).astype(BF16)
-    hidden = jnp.dot(normed.T, w_in_ref[...], preferred_element_type=F32) + b_in_ref[...]
-    hidden = (0.5 * hidden * (1.0 + lax.erf(hidden * np.float32(0.5**0.5)))).astype(BF16)
-    branch = jnp.dot(hidden, w_out_ref[...], preferred_element_type=F32)
-    x = x_ref[0].reshape(HALF * CHUNK, CHAN).astype(F32)
-    o_ref[0] = (x + branch).astype(BF16).reshape(HALF, CHUNK, CHAN)
+    outs = []
+    for part in range(ENS // GROUP):
+        lanes = slice(part * GROUP * wide, (part + 1) * GROUP * wide)
+        values = jnp.concatenate(
+            [y_ref[pl.ds(at, MID), lanes], y_ref[pl.ds(MID - at, MID), lanes]], axis=0
+        ).astype(F32)
+        mean = jnp.mean(values, axis=0, keepdims=True)
+        away = values - mean
+        var = jnp.mean(away * away, axis=0, keepdims=True)
+        normed = (away * lax.rsqrt(var + 1e-5) * gain_ref[...]).astype(BF16).T
+        if part == 0:
+            first.wait()
+        hidden = jnp.dot(normed, w_in_buf[...], preferred_element_type=F32) + b_in_ref[...]
+        hidden = (0.5 * hidden * (1.0 + lax.erf(hidden * np.float32(0.5**0.5)))).astype(BF16)
+        if part == 0:
+            second.wait()
+        branch = jnp.dot(hidden, w_out_buf[...], preferred_element_type=F32)
+        for g in range(GROUP):
+            e = part * GROUP + g
+            xs[e].wait()
+            x = x_buf[e].reshape(wide, CHAN).astype(F32)
+            o_buf[e] = (
+                (x + branch[g * wide : (g + 1) * wide]).astype(BF16).reshape(HALF, CHUNK, CHAN)
+            )
+            outs.append(pltpu.make_async_copy(o_buf.at[e], o_ref.at[e, rows], o_sem.at[e]))
+            outs[e].start()
+    for c in outs:
+        c.wait()
 
 
 def mlp(turn, y, fields, half, gain, w_in, b_in, w_out, before=None):
-    wide = HALF * CHUNK
-    points = pl.BlockSpec((1, HALF, CHUNK, CHAN), lambda e: (e, half, 0, 0))
-    whole = lambda *shape: pl.BlockSpec(shape, lambda e: (0, 0))
     extra = () if before is None else (before,)
+    points = (ENS, HALF, CHUNK, CHAN)
+    sems = pltpu.SemaphoreType.DMA
     return pl.pallas_call(
-        mlp_kernel,
-        grid=(ENS,),
-        in_specs=[
-            pl.BlockSpec(memory_space=pltpu.SMEM),
-            pl.BlockSpec((CHAN, wide), lambda e: (0, e)),
-            points,
-            whole(CHAN, 1),
-            whole(CHAN, HID),
-            whole(1, HID),
-            whole(HID, CHAN),
-        ]
-        + [pl.BlockSpec(memory_space=pl.ANY)] * len(extra),
-        out_specs=points,
+        functools.partial(mlp_kernel, half),
+        in_specs=[SMEM, VMEM, ANY, VMEM, ANY, VMEM, ANY] + [ANY] * len(extra),
+        out_specs=ANY,
         out_shape=jax.ShapeDtypeStruct((ENS, ROWS, CHUNK, CHAN), BF16),
         input_output_aliases={7: 0} if extra else {},
-        compiler_params=params("arbitrary"),
+        scratch_shapes=[
+            pltpu.VMEM(points, BF16),
+            pltpu.VMEM((CHAN, HID), BF16),
+            pltpu.VMEM((HID, CHAN), BF16),
+            pltpu.VMEM(points, BF16),
+            sems((ENS,)),
+            sems((2,)),
+            sems((ENS,)),
+        ],
+        compiler_params=params(),
         cost_estimate=cost(4 * PTS * CHAN * HID, 1.2e7),
         name="mlp",
-    )(turn, y, fields, gain, w_in, b_in, w_out, *extra)
+    )(turn, near(y), fields, gain, w_in, b_in, w_out, *extra)
 
 
 def turned(lat):
@@ -309,11 +386,8 @@
     spec_low = dft(low, onward)
     high, spec_low = lax.optimization_barrier((high, spec_low))
     before = shift(high, 1)
-    spec_after = dft(after, onward)
-    spec_high = dft(high, onward)
-    conv_high = swap(mix(coef, 1, (spec_low, spec_high, spec_after), theta4, back))
-    spec_before = dft(before, onward)
-    conv_low = swap(mix(coef, 0, (spec_before, spec_low, spec_high), theta4, back))
+    conv_high = swap(conv(coef, 1, spec_low, high, after, theta4, onward, back))
+    conv_low = swap(conv(coef, 0, spec_low, high, before, theta4, onward, back))
     rest = (norm_gain[:, None], w_in, b_in[None, :], w_out)
     out = mlp(turn, conv_high, fields, 1, *rest)
     return mlp(turn, conv_low, fields, 0, *rest, before=out)

time: 128 us -> 122 us (0.953)
  Pallas kernels: 65.9 us -> 57.4 us
  waiting for transfers between devices: 29.2 us -> 31.1 us
    pallas_call x10 -> x7, Pallas kernels: 58.3 us -> 49.8 us  [the longest x2 22.3 us: conv(): pl.pallas_call(functools.partial(conv_kernel, half), in_specs=[ANY, ANY,...]
    all_to_all x1, waiting for transfers between devices: 5.94 us -> 7.27 us  [shards(): low = swap(packed_low)]
  transfers between devices with their start and end apart: 7 -> 7, of which waited for: 4 -> 4; matrix products, arithmetic and copies ran while one was open for 3% -> 3% of each run, Pallas kernels for 42% -> 38%
where the time goes in v2:
time: 122 us; the launch traced here: 121 us
  Pallas kernels  57.4 us (47%)
  waiting for transfers between devices  31.1 us (25%)
  starting transfers between devices  27.5 us (23%)
  local copies, waits for them, and re-layouts  4.57 us (4%)
    pallas_call x2, Pallas kernels, conv(): pl.pallas_call(functools.partial(conv_kernel, half), in_specs=[ANY, ANY,...  22.3 us
    pallas_call x2, Pallas kernels, mlp(): pl.pallas_call(functools.partial(mlp_kernel, half), in_specs=[SMEM, VMEM,...  18.8 us
    all_to_all x1, waiting for transfers between devices, shards(): high = swap(pack(turn, fields, 1, coef))  10.2 us
    ppermute x2, starting transfers between devices, shards(): lax.ppermute(v, ('lat', 'lon'), band_perm(lats, lons, step))  7.73 us
    pallas_call x1, Pallas kernels, coefs(): pl.pallas_call(coef_kernel, grid=(2,), in_specs=[smem, smem, smem, pl.Blo...  7.65 us
    all_to_all x1, waiting for transfers between devices, shards(): conv_low = swap(conv(coef, 0, spec_low, high, before, theta4, onward, back))  7.53 us
    all_to_all x1, waiting for transfers between devices, shards(): low = swap(packed_low)  7.27 us
    all_to_all x1, starting transfers between devices, shards(): low = swap(packed_low)  6.35 us
  transfers between devices with their start and end apart: 7, of which 4 were waited for; matrix products, arithmetic and copies ran while one was open for 3% of the time, Pallas kernels for 38%

profile of v2, /device:TPU:1, one launch (start us, length us, event | category | flops | bytes accessed | tf_op | source)
XLA Modules:
  0.0 120.9 jit_solution(13171130388410982668)
XLA Ops:
  0.0 2.3 %pack.2.rest_0_ = bf16[640,1024]{1,0:T(8,128)(2,1)} custom-call(s32[1]{0:T(128)} %bitcast.turn_ref, bf16[4,8,64,640]{3,2,1,0:T(8,128)(2,1)} %x_ref.7), custom_call_target="tpu_custom_call" | custom-call | bytes 2621440 | tf_op jit(solution)/shard_map/pack/pallas_call | solution.py:97
  2.4 0.0 copy-start.1
  2.4 6.3 %all-to-all-start.1 = ((bf16[8,80,1024]{2,1,0:T(8,128)(2,1)}), bf16[8,80,1024]{2,1,0:T(8,128)(2,1)S(1)}, u32[]{:S(2)}, u32[]{:S(2)}) async-start(bf16[8,80,1024]{2,1,0:T(8,128)(2,1)} %bitcast.16), calls=%async_computation.1 | async-start | bytes 2621440 | tf_op jit(solution)/shard_map/all_to_all | solution.py:382
  8.7 0.0 copy-done.1
  8.7 0.3 copy.14
  9.0 1.0 reshape.23.k_ref
  10.0 7.6 %coefs.1.rest_0_.g_ref = bf16[2,16,384,384]{3,2,1,0:T(8,128)(2,1)} custom-call(s32[8]{0:T(128)} %start_ref.1, s32[8]{0:T(128)} %count_ref.1, s32[1]{0:T(128)} %bitcast.1.first_ref, f32[2,108,512]{2,1,0:T(8,128)} %reshape.23.k_ref, bf16[512,512]{1,0:T(8,128)(2,1)} %constant.37.clone.w_ref, bf16[640,1024]{1,0:T(8,128)(2,1)} %pack.2.rest_0_), custom_call_target="tpu_custom_call" | custom-call | flops 8000000000 | bytes 10000000 | tf_op jit(solution)/shard_map/coefs/pallas_call | solution.py:186
  17.7 2.4 %pack.3 = bf16[640,1024]{1,0:T(8,128)(2,1)} custom-call(s32[1]{0:T(128)} %bitcast.turn_ref, bf16[4,8,64,640]{3,2,1,0:T(8,128)(2,1)} %x_ref.7, bf16[2,16,384,384]{3,2,1,0:T(8,128)(2,1)} %coefs.1.rest_0_.g_ref), custom_call_target="tpu_custom_call" | custom-call | bytes 2621440 | tf_op jit(solution)/shard_map/pack/pallas_call | solution.py:97
  20.1 7.3 %all-to-all-done.1 = bf16[8,80,1024]{2,1,0:T(8,128)(2,1)S(1)} async-done(((bf16[8,80,1024]{2,1,0:T(8,128)(2,1)}), bf16[8,80,1024]{2,1,0:T(8,128)(2,1)S(1)}, u32[]{:S(2)}, u32[]{:S(2)}) %all-to-all-start.1) | async-done | bytes 1310752 | tf_op jit(solution)/shard_map/all_to_all | solution.py:382
  27.3 0.0 copy-start
  27.3 0.0 copy-start.4
  27.3 1.1 copy-done
  28.4 3.6 %all-to-all-start = ((bf16[8,80,1024]{2,1,0:T(8,128)(2,1)}), bf16[8,80,1024]{2,1,0:T(8,128)(2,1)S(1)}, u32[]{:S(2)}, u32[]{:S(2)}) async-start(bf16[8,80,1024]{2,1,0:T(8,128)(2,1)} %bitcast.17), calls=%async_computation | async-start | bytes 2621440 | tf_op jit(solution)/shard_map/all_to_all | solution.py:384
  32.0 2.8 %collective-permute-start.2 = (bf16[640,1024]{1,0:T(8,128)(2,1)}, bf16[640,1024]{1,0:T(8,128)(2,1)S(1)}, u32[]{:S(2)}, u32[]{:S(2)}) collective-permute-start(bf16[640,1024]{1,0:T(8,128)(2,1)} %bitcast.14), channel_id=1, source_target_pairs={{8,0},{9,1},{10,2},{11,3},{12,4},{13,5},{14,6},{15,7},{16,12},{17,... | collective-permute-start | bytes 3932168 | tf_op jit(solution)/shard_map/ppermute | solution.py:377
  34.8 0.0 copy-done.4
  34.8 1.7 %collective-permute-start.1 = (f32[3,80]{1,0:T(4,128)S(1)}, f32[3,80]{1,0:T(4,128)S(1)}, u32[]{:S(2)}, u32[]{:S(2)}) collective-permute-start(f32[3,80]{1,0:T(4,128)S(1)} %copy-done.4), channel_id=1, source_target_pairs={{0,4},{1,5},{2,6},{3,7},{4,0},{5,1},{6,2},{7,3},{8,12},{9,13},{10,... | collective-permute-start | bytes 2888 | tf_op jit(solution)/shard_map/ppermute | solution.py:378
  36.5 3.9 %dft.1.low_ref = bf16[16,128,320]{2,1,0:T(8,128)(2,1)} custom-call(bf16[640,1024]{1,0:T(8,128)(2,1)} %bitcast.15, bf16[512,512]{1,0:T(8,128)(2,1)} %constant.37.clone.w_ref), custom_call_target="tpu_custom_call" | custom-call | flops 671088640 | bytes 5242880 | tf_op jit(solution)/shard_map/dft/pallas_call | solution.py:138
  40.4 10.2 %all-to-all-done = bf16[8,80,1024]{2,1,0:T(8,128)(2,1)S(1)} async-done(((bf16[8,80,1024]{2,1,0:T(8,128)(2,1)}), bf16[8,80,1024]{2,1,0:T(8,128)(2,1)S(1)}, u32[]{:S(2)}, u32[]{:S(2)}) %all-to-all-start) | async-done | bytes 1310752 | tf_op jit(solution)/shard_map/all_to_all | solution.py:384
  50.6 5.0 %collective-permute-start = (bf16[640,1024]{1,0:T(8,128)(2,1)S(1)}, bf16[640,1024]{1,0:T(8,128)(2,1)}, u32[]{:S(2)}, u32[]{:S(2)}) collective-permute-start(bf16[640,1024]{1,0:T(8,128)(2,1)S(1)} %bitcast.11), channel_id=1, source_target_pairs={{0,8},{1,9},{2,10},{3,11},{4,12},{5,13},{6,14},{7,15},{8,20},{9,21... | collective-permute-start | bytes 3932168 | tf_op jit(solution)/shard_map/ppermute | solution.py:377
  55.6 0.0 collective-permute-done.1
  55.6 0.7 tile.10.theta_ref
  56.3 0.0 collective-permute-done.2.halo_ref
  56.3 10.8 %conv.3 = bf16[640,1024]{1,0:T(8,128)(2,1)} custom-call(bf16[2,16,384,384]{3,2,1,0:T(8,128)(2,1)} %coefs.1.rest_0_.g_ref, bf16[16,128,320]{2,1,0:T(8,128)(2,1)} %dft.1.low_ref, bf16[640,1024]{1,0:T(8,128)(2,1)S(1)} %bitcast.12, bf16[640,1024]{1,0:T(8,128)(2,1)S(1)} %collective-permute-done.2.halo_ref, f32[3,320]{1,0:T(4,128)} %tile.10.theta_ref, ...), custom_call_target="tpu_custom_call" | custom-call | flops 6000000000 | bytes 12000000 | tf_op jit(solution)/shard_map/conv/pallas_call | solution.py:269
  67.1 4.5 %all-to-all-start.3 = ((bf16[8,80,1024]{2,1,0:T(8,128)(2,1)}), bf16[8,80,1024]{2,1,0:T(8,128)(2,1)}, u32[]{:S(2)}, u32[]{:S(2)}) async-start(bf16[8,80,1024]{2,1,0:T(8,128)(2,1)} %bitcast.8), calls=%async_computation.3 | async-start | bytes 2621440 | tf_op jit(solution)/shard_map/all_to_all | solution.py:389
  71.6 0.0 collective-permute-done.halo_ref
  71.6 11.5 %conv.2 = bf16[640,1024]{1,0:T(8,128)(2,1)} custom-call(bf16[2,16,384,384]{3,2,1,0:T(8,128)(2,1)} %coefs.1.rest_0_.g_ref, bf16[16,128,320]{2,1,0:T(8,128)(2,1)} %dft.1.low_ref, bf16[640,1024]{1,0:T(8,128)(2,1)S(1)} %bitcast.13, bf16[640,1024]{1,0:T(8,128)(2,1)} %collective-permute-done.halo_ref, f32[3,320]{1,0:T(4,128)} %tile.10.theta_ref, ...), custom_call_target="tpu_custom_call" | custom-call | flops 6000000000 | bytes 12000000 | tf_op jit(solution)/shard_map/conv/pallas_call | solution.py:269
  83.1 6.1 %all-to-all-done.3 = bf16[8,80,1024]{2,1,0:T(8,128)(2,1)} async-done(((bf16[8,80,1024]{2,1,0:T(8,128)(2,1)}), bf16[8,80,1024]{2,1,0:T(8,128)(2,1)}, u32[]{:S(2)}, u32[]{:S(2)}) %all-to-all-start.3) | async-done | bytes 1310752 | tf_op jit(solution)/shard_map/all_to_all | solution.py:389
  89.2 0.0 copy-start.3
  89.2 0.0 copy-start.2
  89.2 3.7 %all-to-all-start.2 = ((bf16[8,80,1024]{2,1,0:T(8,128)(2,1)}), bf16[8,80,1024]{2,1,0:T(8,128)(2,1)S(1)}, u32[]{:S(2)}, u32[]{:S(2)}) async-start(bf16[8,80,1024]{2,1,0:T(8,128)(2,1)} %bitcast.6), calls=%async_computation.2 | async-start | bytes 2621440 | tf_op jit(solution)/shard_map/all_to_all | solution.py:390
  92.9 0.0 copy-done.3
  93.0 0.9 broadcast_in_dim.8.gain_ref
  93.8 0.0 copy-done.2
  93.8 0.6 broadcast_in_dim.7.b_in_ref
  94.4 9.6 %mlp.2.rest_0_ = bf16[4,8,64,640]{3,2,1,0:T(8,128)(2,1)} custom-call(s32[1]{0:T(128)} %bitcast.turn_ref, bf16[640,1024]{1,0:T(8,128)(2,1)} %bitcast.9.y_ref, bf16[4,8,64,640]{3,2,1,0:T(8,128)(2,1)} %x_ref.7, f32[640,1]{1,0:T(8,128)} %broadcast_in_dim.8.gain_ref, bf16[640,1280]{1,0:T(8,128)(2,1)} %w_in_ref.3, f32[1,1280]{1,0:T(1,128)} %broadcast_in_dim.7.b_in_ref, ...), custom_call_target="tpu_custom_call" | custom-call | flops 3355443200 | bytes 12000000 | tf_op jit(solution)/shard_map/mlp/pallas_call | solution.py:335
  104.1 7.5 %all-to-all-done.2 = bf16[8,80,1024]{2,1,0:T(8,128)(2,1)S(1)} async-done(((bf16[8,80,1024]{2,1,0:T(8,128)(2,1)}), bf16[8,80,1024]{2,1,0:T(8,128)(2,1)S(1)}, u32[]{:S(2)}, u32[]{:S(2)}) %all-to-all-start.2) | async-done | bytes 1310752 | tf_op jit(solution)/shard_map/all_to_all | solution.py:390
  111.6 9.2 %mlp.3 = bf16[4,8,64,640]{3,2,1,0:T(8,128)(2,1)} custom-call(s32[1]{0:T(128)} %bitcast.turn_ref, bf16[640,1024]{1,0:T(8,128)(2,1)S(1)} %bitcast.10, bf16[4,8,64,640]{3,2,1,0:T(8,128)(2,1)} %x_ref.7, f32[640,1]{1,0:T(8,128)} %broadcast_in_dim.8.gain_ref, bf16[640,1280]{1,0:T(8,128)(2,1)} %w_in_ref.3, ...), custom_call_target="tpu_custom_call", output_to_operand_aliasing={{}: (7, {})} | custom-call | flops 3355443200 | bytes 12000000 | tf_op jit(solution)/shard_map/mlp/pallas_call | solution.py:335
  (2 shorter events, 0.0 us)
Async XLA Ops:
  2.4 6.4 %copy-start.1 = (f32[8,9,3,512]{3,0,2,1:T(8,128)S(1)}, f32[8,9,3,512]{3,0,2,1:T(8,128)}, u32[]{:S(2)}) copy-start(f32[8,9,3,512]{3,0,2,1:T(8,128)} %param.12) | copy-start | bytes 1327108
  2.4 25.0 %all-to-all-start.1 = ((bf16[8,80,1024]{2,1,0:T(8,128)(2,1)}), bf16[8,80,1024]{2,1,0:T(8,128)(2,1)S(1)}, u32[]{:S(2)}, u32[]{:S(2)}) async-start(bf16[8,80,1024]{2,1,0:T(8,128)(2,1)} %bitcast.16), calls=%async_computation.1 | async-start | bytes 2621440 | tf_op jit(solution)/shard_map/all_to_all | solution.py:382
  27.3 1.1 copy-start
  27.3 7.4 %copy-start.4 = (f32[3,80]{1,0:T(4,128)S(1)}, f32[3,80]{1,0:T(4,128)}, u32[]{:S(2)}) copy-start(f32[3,80]{1,0:T(4,128)} %param.13) | copy-start | bytes 2884
  28.4 22.2 %all-to-all-start = ((bf16[8,80,1024]{2,1,0:T(8,128)(2,1)}), bf16[8,80,1024]{2,1,0:T(8,128)(2,1)S(1)}, u32[]{:S(2)}, u32[]{:S(2)}) async-start(bf16[8,80,1024]{2,1,0:T(8,128)(2,1)} %bitcast.17), calls=%async_computation | async-start | bytes 2621440 | tf_op jit(solution)/shard_map/all_to_all | solution.py:384
  32.0 24.3 %collective-permute-start.2 = (bf16[640,1024]{1,0:T(8,128)(2,1)}, bf16[640,1024]{1,0:T(8,128)(2,1)S(1)}, u32[]{:S(2)}, u32[]{:S(2)}) collective-permute-start(bf16[640,1024]{1,0:T(8,128)(2,1)} %bitcast.14), channel_id=1, source_target_pairs={{8,0},{9,1},{10,2},{11,3},{12,4},{13,5},{14,6},{15,7},{16,12},{17,... | collective-permute-start | bytes 3932168 | tf_op jit(solution)/shard_map/ppermute | solution.py:377
  34.8 20.8 %collective-permute-start.1 = (f32[3,80]{1,0:T(4,128)S(1)}, f32[3,80]{1,0:T(4,128)S(1)}, u32[]{:S(2)}, u32[]{:S(2)}) collective-permute-start(f32[3,80]{1,0:T(4,128)S(1)} %copy-done.4), channel_id=1, source_target_pairs={{0,4},{1,5},{2,6},{3,7},{4,0},{5,1},{6,2},{7,3},{8,12},{9,13},{10,... | collective-permute-start | bytes 2888 | tf_op jit(solution)/shard_map/ppermute | solution.py:378
  50.6 21.0 %collective-permute-start = (bf16[640,1024]{1,0:T(8,128)(2,1)S(1)}, bf16[640,1024]{1,0:T(8,128)(2,1)}, u32[]{:S(2)}, u32[]{:S(2)}) collective-permute-start(bf16[640,1024]{1,0:T(8,128)(2,1)S(1)} %bitcast.11), channel_id=1, source_target_pairs={{0,8},{1,9},{2,10},{3,11},{4,12},{5,13},{6,14},{7,15},{8,20},{9,21... | collective-permute-start | bytes 3932168 | tf_op jit(solution)/shard_map/ppermute | solution.py:377
  67.1 22.1 %all-to-all-start.3 = ((bf16[8,80,1024]{2,1,0:T(8,128)(2,1)}), bf16[8,80,1024]{2,1,0:T(8,128)(2,1)}, u32[]{:S(2)}, u32[]{:S(2)}) async-start(bf16[8,80,1024]{2,1,0:T(8,128)(2,1)} %bitcast.8), calls=%async_computation.3 | async-start | bytes 2621440 | tf_op jit(solution)/shard_map/all_to_all | solution.py:389
  89.2 3.7 %copy-start.3 = (f32[640]{0:T(1024)S(1)}, f32[640]{0:T(1024)}, u32[]{:S(2)}) copy-start(f32[640]{0:T(1024)} %param.16) | copy-start | bytes 7684
  89.2 4.6 %copy-start.2 = (f32[1280]{0:T(1024)S(1)}, f32[1280]{0:T(1024)}, u32[]{:S(2)}) copy-start(f32[1280]{0:T(1024)} %param.18) | copy-start | bytes 15364
  89.2 22.4 %all-to-all-start.2 = ((bf16[8,80,1024]{2,1,0:T(8,128)(2,1)}), bf16[8,80,1024]{2,1,0:T(8,128)(2,1)S(1)}, u32[]{:S(2)}, u32[]{:S(2)}) async-start(bf16[8,80,1024]{2,1,0:T(8,128)(2,1)} %bitcast.6), calls=%async_computation.2 | async-start | bytes 2621440 | tf_op jit(solution)/shard_map/all_to_all | solution.py:390

commit v3 on v2

--- a/solution.py
+++ b/solution.py
@@ -25,6 +25,7 @@
 KB = 3
 FB = 16
 FS = 16
+BAND = HALF * 2 * FS
 WIN = 12
 PTS = ENS * HALF * CHUNK
 HID = 1280
@@ -62,8 +63,8 @@
     return pltpu.with_memory_space_constraint(value, pltpu.VMEM)
 
 
-def far(value):
-    return pltpu.with_memory_space_constraint(value, pltpu.HBM)
+def block_of(index):
+    return pl.ds(pl.multiple_of(index * CH, CH), CH)
 
 
 def cost(flops, nbytes):
@@ -130,22 +131,8 @@
             o_ref[:, row : row + 2 * FS, :] = s.astype(BF16).reshape(FB, 2 * FS, COLS)
 
 
-def dft_kernel(x_ref, w_ref, o_ref):
-    dft_rows(x_ref, w_ref[...], o_ref, 0)
-
-
-def dft(received, onward):
-    return pl.pallas_call(
-        dft_kernel,
-        out_shape=jax.ShapeDtypeStruct((FB, HALF * 2 * FS, COLS), BF16),
-        compiler_params=params(),
-        cost_estimate=cost(2 * HALF * NLON * NLON * COLS, 8 * CHAN * PTS),
-        name="dft",
-    )(far(received), onward)
-
-
 def coef_kernel(start_ref, count_ref, first_ref, k_ref, w_ref, *rest):
-    o_ref = rest[-1]
+    low_ref, rest_ref = rest[-2:]
     half = pl.program_id(0)
     kern = k_ref[...].astype(BF16)
     hat = lax.dot_general(w_ref[...], kern, (((1,), (1,)), ((), ())), preferred_element_type=F32)
@@ -156,6 +143,7 @@
     taps = SLOTS * KB * HALF
     tap = lax.broadcasted_iota(jnp.int32, (taps, lanes), 0)
     window = lax.broadcasted_iota(jnp.int32, (taps, lanes), 1) // (2 * FS)
+    window = jnp.where((half == 0) & (window < 2 * HALF), window ^ HALF, window)
     lane = lax.broadcasted_iota(jnp.int32, (FB * FS, lanes), 1)
     freq = lax.broadcasted_iota(jnp.int32, (FB * FS, lanes), 0)
     same = (lane % FS) == (freq % FS)
@@ -175,8 +163,10 @@
             top = jnp.where(same, top, 0.0).astype(BF16).reshape(FB, FS, lanes)
             low = jnp.where(same, low, 0.0).astype(BF16).reshape(FB, FS, lanes)
             at = (i * KB + k) * 2 * FS
-            o_ref[0, :, at : at + FS, :] = top
-            o_ref[0, :, at + FS : at + 2 * FS, :] = low
+            low_ref[0, :, at : at + FS, :] = top[:, :, :BAND]
+            rest_ref[0, :, at : at + FS, :] = top[:, :, BAND:]
+            low_ref[0, :, at + FS : at + 2 * FS, :] = low[:, :, :BAND]
+            rest_ref[0, :, at + FS : at + 2 * FS, :] = low[:, :, BAND:]
 
 
 def coefs(row_start, row_count, first, kernel, onward, *after):
@@ -194,57 +184,100 @@
             pl.BlockSpec((NLON, NLON), lambda h: (0, 0)),
         ]
         + [pl.BlockSpec(memory_space=pl.ANY)] * len(after),
-        out_specs=pl.BlockSpec((1, FB, size, WIN * 2 * FS), lambda h: (h, 0, 0, 0)),
-        out_shape=jax.ShapeDtypeStruct((2, FB, size, WIN * 2 * FS), BF16),
+        out_specs=[pl.BlockSpec((1, FB, size, n), lambda h: (h, 0, 0, 0)) for n in (BAND, 2 * BAND)],
+        out_shape=[jax.ShapeDtypeStruct((2, FB, size, n), BF16) for n in (BAND, 2 * BAND)],
         compiler_params=params("arbitrary"),
         cost_estimate=cost(8e9, 1e7),
         name="coefs",
     )(row_start, row_count, first, kernel.reshape(2, taps, NLON), onward, *after)
 
 
+def combine(p, theta):
+    rows = []
+    for i in range(HALF):
+        total = None
+        for k in range(KB):
+            at = (i * KB + k) * 2 * FS
+            term = p[at : at + 2 * FS, :] * theta[k]
+            total = term if total is None else total + term
+        rows.append(total)
+    return rows
+
+
+def low_kernel(x_ref, w_ref, g_ref, theta_ref, o_ref, s_buf):
+    @pl.when(pl.program_id(0) == 0)
+    def _():
+        dft_rows(x_ref, w_ref[...], s_buf, 0)
+
+    theta = [theta_ref[k : k + 1, :] for k in range(KB)]
+    for block in range(FB):
+        p = jnp.dot(g_ref[0, block], s_buf[block], preferred_element_type=F32)
+        for i, row in enumerate(combine(p, theta)):
+            o_ref[0, i, block * 2 * FS : (block + 1) * 2 * FS, :] = row
+
+
+def low_share(received, onward, coef_low, theta):
+    whole = lambda *shape: pl.BlockSpec(shape, lambda h: (0,) * len(shape))
+    return pl.pallas_call(
+        low_kernel,
+        grid=(2,),
+        in_specs=[
+            whole(CHAN, PTS),
+            whole(NLON, NLON),
+            pl.BlockSpec((1, FB, HALF * KB * 2 * FS, BAND), lambda h: (h, 0, 0, 0)),
+            whole(KB, COLS),
+        ],
+        out_specs=pl.BlockSpec((1, HALF, NLON, COLS), lambda h: (h, 0, 0, 0)),
+        out_shape=jax.ShapeDtypeStruct((2, HALF, NLON, COLS), F32),
+        scratch_shapes=[pltpu.VMEM((FB, BAND, COLS), BF16)],
+        compiler_params=params("arbitrary"),
+        cost_estimate=cost(2e9, 8e6),
+        name="low",
+    )(received, onward, coef_low, theta)
+
+
 STEP = 4
 STEPS = FB // STEP
 
 
 def conv_kernel(
-    half, g_ref, low_ref, high_ref, halo_ref, theta_ref, w_ref, back_ref, o_ref, *rest
+    half, me_ref, g_ref, low_ref, high_ref, halo_ref, theta_ref, w_ref, back_ref, *rest
 ):
-    g_buf, s_buf, w_buf, t_buf, g_sem, low_sem, w_sem = rest
-    band = HALF * 2 * FS
-    halo_at, low_at, high_at = (2 * band, 0, band) if half else (0, band, 2 * band)
-    ws = [
-        pltpu.make_async_copy(ref, w_buf.at[n], w_sem.at[n]) for n, ref in enumerate((w_ref, back_ref))
-    ]
-    ws[0].start()
+    count = len(rest) - 11
+    pieces, rest = rest[:count], rest[count:]
+    o_buf, g_buf, s_buf, l_buf, x_buf, w_buf, t_buf, g_sem, l_sem, w_sem, o_sem = rest
+    halo_at, high_at = (BAND, 0) if half else (0, BAND)
+    moves = [(w_ref, w_buf.at[0]), (halo_ref, x_buf.at[1]), (back_ref, w_buf.at[1])]
+    moves += [] if half else [(high_ref, x_buf.at[0])]
+    ws = [pltpu.make_async_copy(ref, to, w_sem.at[n]) for n, (ref, to) in enumerate(moves)]
     gs, lows = [], []
     for s in range(STEPS):
         part = pl.ds(s * STEP, STEP)
+        rows = pl.ds(s * STEP * 2 * FS, STEP * 2 * FS)
         gs.append(pltpu.make_async_copy(g_ref.at[half, part], g_buf.at[part], g_sem.at[s]))
-        lows.append(
-            pltpu.make_async_copy(
-                low_ref.at[part], s_buf.at[part, pl.ds(low_at, band)], low_sem.at[s]
-            )
-        )
+        lows.append(pltpu.make_async_copy(low_ref.at[half, :, rows], l_buf.at[:, rows], l_sem.at[s]))
+    for c in ws[:1] + ws[3:] + ws[1:2]:
+        c.start()
+    for s in range(STEPS):
         gs[s].start()
         lows[s].start()
-    ws[1].start()
-    ws[0].wait()
-    dft_rows(high_ref, w_buf[0], s_buf, high_at)
-    dft_rows(halo_ref, w_buf[0], s_buf, halo_at)
+    ws[2].start()
+    for c in ws[:1] + ws[3:]:
+        c.wait()
+    dft_rows(high_ref if half else x_buf.at[0], w_buf[0], s_buf, high_at)
+    ws[1].wait()
+    dft_rows(x_buf.at[1], w_buf[0], s_buf, halo_at)
     theta = [theta_ref[k : k + 1, :] for k in range(KB)]
     for step in range(STEPS):
         gs[step].wait()
         lows[step].wait()
         for block in range(step * STEP, (step + 1) * STEP):
             p = jnp.dot(g_buf[block], s_buf[block], preferred_element_type=F32)
-            for i in range(HALF):
-                total = None
-                for k in range(KB):
-                    at = (i * KB + k) * 2 * FS
-                    term = p[at : at + 2 * FS, :] * theta[k]
-                    total = term if total is None else total + term
-                t_buf[i, block * 2 * FS : (block + 1) * 2 * FS, :] = total.astype(BF16)
-    ws[1].wait()
+            rows = slice(block * 2 * FS, (block + 1) * 2 * FS)
+            for i, row in enumerate(combine(p, theta)):
+                t_buf[i, rows, :] = (row + l_buf[i, rows, :]).astype(BF16)
+    ws[2].wait()
+    outs = []
     for pair in range(2):
         y = [
             lax.dot_general(
@@ -258,36 +291,67 @@
         for e in range(ENS):
             base = (e * 2 + pair) * 128
             for d in range(LON_DEV):
-                o_ref[d * CH : (d + 1) * CH, base : base + 128] = jnp.concatenate(
+                o_buf[d * CH : (d + 1) * CH, base : base + 128] = jnp.concatenate(
                     [v[e * CH : (e + 1) * CH, d * CHUNK : (d + 1) * CHUNK] for v in y], axis=1
                 )
-
-
-def conv(coef, half, spec_low, high, halo, theta, onward, back):
+            if count == 1:
+                lanes = slice(base, base + 128)
+                outs.append(
+                    pltpu.make_async_copy(
+                        o_buf.at[:, lanes], pieces[0].at[:, lanes], o_sem.at[pair * ENS + e]
+                    )
+                )
+                outs[-1].start()
+    if count > 1:
+        outs = [
+            pltpu.make_async_copy(o_buf.at[block_of(me_ref[0] ^ k)], piece, o_sem.at[k])
+            for k, piece in enumerate(pieces)
+        ]
+        for c in outs:
+            c.start()
+    for c in outs:
+        c.wait()
+
+
+def conv(me, coef, half, low, high, halo, theta, onward, back, split):
     size = HALF * KB * 2 * FS
-    span = WIN * 2 * FS
+    sems = pltpu.SemaphoreType.DMA
+    shape = (CH, PTS) if split else (CHAN, PTS)
+    count = LON_DEV if split else 1
     return pl.pallas_call(
         functools.partial(conv_kernel, half),
-        in_specs=[ANY, ANY, VMEM, VMEM, VMEM, ANY, ANY],
-        out_specs=VMEM,
-        out_shape=pltpu.VMEM((CHAN, PTS), BF16),
+        in_specs=[SMEM, ANY, ANY, VMEM if half else ANY, ANY, VMEM, ANY, ANY],
+        out_specs=[ANY] * count,
+        out_shape=[jax.ShapeDtypeStruct(shape, BF16)] * count,
         scratch_shapes=[
-            pltpu.VMEM((FB, size, span), BF16),
-            pltpu.VMEM((FB, span, COLS), BF16),
+            pltpu.VMEM((CHAN, PTS), BF16),
+            pltpu.VMEM((FB, size, 2 * BAND), BF16),
+            pltpu.VMEM((FB, 2 * BAND, COLS), BF16),
+            pltpu.VMEM((HALF, NLON, COLS), F32),
+            pltpu.VMEM((2, CHAN, PTS), BF16),
             pltpu.VMEM((2, NLON, NLON), BF16),
             pltpu.VMEM((HALF, NLON, COLS), BF16),
-            pltpu.SemaphoreType.DMA((STEPS,)),
-            pltpu.SemaphoreType.DMA((STEPS,)),
-            pltpu.SemaphoreType.DMA((2,)),
+            sems((STEPS,)),
+            sems((STEPS,)),
+            sems((4,)),
+            sems((LON_DEV,)),
         ],
         compiler_params=params(),
         cost_estimate=cost(6e9, 1.2e7),
         name="conv",
-    )(coef, spec_low, near(high), near(halo), theta, onward, back)
-
-
-def mlp_kernel(half, turn_ref, y_ref, x_ref, gain_ref, w_in_ref, b_in_ref, w_out_ref, *rest):
-    o_ref, x_buf, w_in_buf, w_out_buf, o_buf, x_sem, w_sem, o_sem = rest[-8:]
+    )(me, coef, low, near(high) if half else high, halo, theta, onward, back)
+
+
+def mlp_kernel(half, count, me_ref, turn_ref, *refs):
+    pieces, refs = refs[:count], refs[count:]
+    x_ref, gain_ref, w_in_ref, b_in_ref, w_out_ref, *rest = refs
+    o_ref, y_buf, x_buf, w_in_buf, w_out_buf, o_buf, y_sem, x_sem, w_sem, o_sem = rest[-10:]
+    turned_by = turn_ref[0] * (LON_DEV // 2)
+    ys = [
+        pltpu.make_async_copy(piece, y_buf.at[block_of(me_ref[0] ^ k ^ turned_by)], y_sem.at[k])
+        for k, piece in enumerate(pieces)
+        if count > 1
+    ]
     wide = HALF * CHUNK
     rows = pl.ds(half * HALF, HALF)
     first = pltpu.make_async_copy(w_in_ref, w_in_buf, w_sem.at[0])
@@ -295,15 +359,21 @@
     xs = [
         pltpu.make_async_copy(x_ref.at[e, rows], x_buf.at[e], x_sem.at[e]) for e in range(ENS)
     ]
-    for c in [first, second, *xs]:
+    for c in [*ys, first, second, *xs]:
         c.start()
+    for c in ys:
+        c.wait()
     at = pl.multiple_of(turn_ref[0] * MID, MID)
     outs = []
     for part in range(ENS // GROUP):
         lanes = slice(part * GROUP * wide, (part + 1) * GROUP * wide)
-        values = jnp.concatenate(
-            [y_ref[pl.ds(at, MID), lanes], y_ref[pl.ds(MID - at, MID), lanes]], axis=0
-        ).astype(F32)
+        if count > 1:
+            values = y_buf[:, lanes].astype(F32)
+        else:
+            y_ref = pieces[0]
+            values = jnp.concatenate(
+                [y_ref[pl.ds(at, MID), lanes], y_ref[pl.ds(MID - at, MID), lanes]], axis=0
+            ).astype(F32)
         mean = jnp.mean(values, axis=0, keepdims=True)
         away = values - mean
         var = jnp.mean(away * away, axis=0, keepdims=True)
@@ -328,21 +398,27 @@
         c.wait()
 
 
-def mlp(turn, y, fields, half, gain, w_in, b_in, w_out, before=None):
+def mlp(me, turn, ys, fields, half, gain, w_in, b_in, w_out, before=None):
     extra = () if before is None else (before,)
+    count = len(ys)
     points = (ENS, HALF, CHUNK, CHAN)
     sems = pltpu.SemaphoreType.DMA
     return pl.pallas_call(
-        functools.partial(mlp_kernel, half),
-        in_specs=[SMEM, VMEM, ANY, VMEM, ANY, VMEM, ANY] + [ANY] * len(extra),
+        functools.partial(mlp_kernel, half, count),
+        in_specs=[SMEM, SMEM]
+        + ([ANY] * count if count > 1 else [VMEM])
+        + [ANY, VMEM, ANY, VMEM, ANY]
+        + [ANY] * len(extra),
         out_specs=ANY,
         out_shape=jax.ShapeDtypeStruct((ENS, ROWS, CHUNK, CHAN), BF16),
-        input_output_aliases={7: 0} if extra else {},
+        input_output_aliases={count + 7: 0} if extra else {},
         scratch_shapes=[
+            pltpu.VMEM((CHAN, PTS) if count > 1 else (16, 128), BF16),
             pltpu.VMEM(points, BF16),
             pltpu.VMEM((CHAN, HID), BF16),
             pltpu.VMEM((HID, CHAN), BF16),
             pltpu.VMEM(points, BF16),
+            sems((LON_DEV,)),
             sems((ENS,)),
             sems((2,)),
             sems((ENS,)),
@@ -350,7 +426,7 @@
         compiler_params=params(),
         cost_estimate=cost(4 * PTS * CHAN * HID, 1.2e7),
         name="mlp",
-    )(turn, near(y), fields, gain, w_in, b_in, w_out, *extra)
+    )(me, turn, *(ys if count > 1 else [near(ys[0])]), fields, gain, w_in, b_in, w_out, *extra)
 
 
 def turned(lat):
@@ -371,6 +447,7 @@
     lats, lons = lax.axis_size("lat"), lax.axis_size("lon")
     lat = lax.axis_index("lat").astype(jnp.int32)
     turn = turned(lat).reshape(1)
+    me = lax.axis_index("lon").astype(jnp.int32).reshape(1)
     swap = functools.partial(
         lax.all_to_all, axis_name="lon", split_axis=0, concat_axis=0, tiled=True
     )
@@ -378,19 +455,25 @@
     other = lax.ppermute(theta, "lon", [(t, t ^ (lons // 2)) for t in range(lons)])
     theta4 = jnp.tile(jnp.where(turn[0] == 1, other, theta), (1, ENS))
 
+    rest = (norm_gain[:, None], w_in, b_in[None, :], w_out)
     packed_low = pack(turn, fields, 0)
     low = swap(packed_low)
-    coef = coefs(row_start, row_count, (lat * ROWS).reshape(1), kernel, onward, packed_low)
-    high = swap(pack(turn, fields, 1, coef))
+    coef_low, coef = coefs(
+        row_start, row_count, (lat * ROWS).reshape(1), kernel, onward, packed_low
+    )
+    high = swap(pack(turn, fields, 1, coef, theta4, rest[0], rest[2]))
     after = shift(low, -1)
-    spec_low = dft(low, onward)
-    high, spec_low = lax.optimization_barrier((high, spec_low))
+    share = low_share(low, onward, coef_low, theta4)
+    high, share = lax.optimization_barrier((high, share))
     before = shift(high, 1)
-    conv_high = swap(conv(coef, 1, spec_low, high, after, theta4, onward, back))
-    conv_low = swap(conv(coef, 0, spec_low, high, before, theta4, onward, back))
-    rest = (norm_gain[:, None], w_in, b_in[None, :], w_out)
-    out = mlp(turn, conv_high, fields, 1, *rest)
-    return mlp(turn, conv_low, fields, 0, *rest, before=out)
+    (conv_high,) = conv(me, coef, 1, share, high, after, theta4, onward, back, False)
+    conv_high = swap(conv_high)
+    pieces = conv(me, coef, 0, share, high, before, theta4, onward, back, True)
+    conv_low = [pieces[0]] + [
+        lax.ppermute(pieces[k], "lon", [(t, t ^ k) for t in range(lons)]) for k in range(1, lons)
+    ]
+    out = mlp(me, turn, [conv_high], fields, 1, *rest)
+    return mlp(me, turn, conv_low, fields, 0, *rest, before=out)
 
 
 def solution(mesh):

time: 122 us -> 118 us (0.967)
  waiting for transfers between devices: 31.1 us -> 19.1 us
  starting transfers between devices: 27.5 us -> 34.2 us
  Pallas kernels: 57.4 us -> 59 us
    all_to_all x3 -> x2, waiting for transfers between devices: 23.8 us -> 8.19 us  [the longest x1 8.19 us: shards(): high = swap(pack(turn, fields, 1, coef, theta4, rest[0], rest[2]))]
    ppermute x0 -> x7, starting transfers between devices: none -> 9.56 us  [shards(): lax.ppermute(pieces[k], 'lon', [(t, t ^ k) for t in range(lons)])]
    ppermute x0 -> x7, waiting for transfers between devices: none -> 5.92 us  [shards(): lax.ppermute(pieces[k], 'lon', [(t, t ^ k) for t in range(lons)])]
    all_to_all x1, waiting for transfers between devices: 7.27 us -> 3.45 us  [shards(): low = swap(packed_low)]
    all_to_all x3 -> x2, starting transfers between devices: 11.7 us -> 8.97 us  [the longest x1 5.39 us: shards(): high = swap(pack(turn, fields, 1, coef, theta4, rest[0], rest[2]))]
    ppermute x2, waiting for transfers between devices: 0.01 us -> 1.48 us  [shards(): lax.ppermute(v, ('lat', 'lon'), band_perm(lats, lons, step))]
    pallas_call x5, Pallas kernels: 45 us -> 46.5 us  [the longest x2 19.5 us: mlp(): pl.pallas_call(functools.partial(mlp_kernel, half, count), in_specs=[SMEM...]
  transfers between devices with their start and end apart: 7 -> 13, of which waited for: 4 -> 5; matrix products, arithmetic and copies ran while one was open for 3% -> 3% of each run, Pallas kernels for 38% -> 40%
where the time goes in v3:
time: 118 us; the launch traced here: 117 us
  Pallas kernels  59 us (50%)
  starting transfers between devices  34.2 us (29%)
  waiting for transfers between devices  19.1 us (16%)
  local copies, waits for them, and re-layouts  4.35 us (4%)
    pallas_call x2, Pallas kernels, mlp(): pl.pallas_call(functools.partial(mlp_kernel, half, count), in_specs=[SMEM...  19.5 us
    pallas_call x2, Pallas kernels, conv(): pl.pallas_call(functools.partial(conv_kernel, half), in_specs=[SMEM, ANY,...  19.2 us
    ppermute x7, starting transfers between devices, shards(): lax.ppermute(pieces[k], 'lon', [(t, t ^ k) for t in range(lons)])  9.56 us
    all_to_all x1, waiting for transfers between devices, shards(): high = swap(pack(turn, fields, 1, coef, theta4, rest[0], rest[2]))  8.19 us
    ppermute x2, starting transfers between devices, shards(): lax.ppermute(v, ('lat', 'lon'), band_perm(lats, lons, step))  7.86 us
    pallas_call x1, Pallas kernels, coefs(): pl.pallas_call(coef_kernel, grid=(2,), in_specs=[smem, smem, smem, pl.Blo...  7.77 us
    pallas_call x1, Pallas kernels, low_share(): pl.pallas_call(low_kernel, grid=(2,), in_specs=[whole(CHAN, PTS), whole(N...  7.76 us
    all_to_all x1, starting transfers between devices, shards(): low = swap(packed_low)  6.35 us
  transfers between devices with their start and end apart: 13, of which 5 were waited for; matrix products, arithmetic and copies ran while one was open for 3% of the time, Pallas kernels for 40%

profile of v3, /device:TPU:1, one launch (start us, length us, event | category | flops | bytes accessed | tf_op | source)
XLA Modules:
  0.0 117.0 jit_solution(3521549967589254740)
XLA Ops:
  0.0 2.3 %pack.2.rest_0_ = bf16[640,1024]{1,0:T(8,128)(2,1)} custom-call(s32[1]{0:T(128)} %bitcast.1.turn_ref, bf16[4,8,64,640]{3,2,1,0:T(8,128)(2,1)} %refs_8_.1), custom_call_target="tpu_custom_call" | custom-call | bytes 2621440 | tf_op jit(solution)/shard_map/pack/pallas_call | solution.py:98
  2.4 0.0 copy-start.12
  2.4 0.0 copy-start.2
  2.4 6.3 %all-to-all-start.1 = ((bf16[8,80,1024]{2,1,0:T(8,128)(2,1)}), bf16[8,80,1024]{2,1,0:T(8,128)(2,1)S(1)}, u32[]{:S(2)}, u32[]{:S(2)}) async-start(bf16[8,80,1024]{2,1,0:T(8,128)(2,1)} %bitcast.13), calls=%async_computation.1 | async-start | bytes 2621440 | tf_op jit(solution)/shard_map/all_to_all | solution.py:460
  8.7 0.0 copy-done.12
  8.7 1.5 %collective-permute-start = (f32[3,80]{1,0:T(4,128)S(1)}, f32[3,80]{1,0:T(4,128)S(1)}, u32[]{:S(2)}, u32[]{:S(2)}) collective-permute-start(f32[3,80]{1,0:T(4,128)S(1)} %copy-done.12), channel_id=1, source_target_pairs={{0,4},{1,5},{2,6},{3,7},{4,0},{5,1},{6,2},{7,3},{8,12},{9,13},{10,... | collective-permute-start | bytes 2888 | tf_op jit(solution)/shard_map/ppermute | solution.py:455
  10.2 0.0 copy-done.2
  10.2 0.3 copy.14
  10.5 1.0 reshape.25.k_ref
  11.5 0.0 copy-start.11
  11.5 0.0 copy-start.10
  11.5 7.8 %coefs.1 = (bf16[2,16,384,128]{3,2,1,0:T(8,128)(2,1)}, bf16[2,16,384,256]{3,2,1,0:T(8,128)(2,1)}) custom-call(s32[8]{0:T(128)} %start_ref.1, s32[8]{0:T(128)} %count_ref.1, s32[1]{0:T(128)} %bitcast.2.first_ref, f32[2,108,512]{2,1,0:T(8,128)} %reshape.25.k_ref, bf16[512,512]{1,0:T(8,128)(2,1)} %constant.40.clone.w_ref, bf16[640,1024]{1,0:T(8,128)(2,1)} %pack.2.rest_0_), custom_call_target="tpu_custom_call" | custom-call | flops 8000000000 | bytes 10000000 | tf_op jit(solution)/shard_map/coefs/pallas_call | solution.py:176
  19.3 0.0 copy-done.11
  19.3 0.9 broadcast_in_dim.8.rest_2_.refs_2_.refs_9_
  20.2 0.0 copy-done.10
  20.2 0.6 broadcast_in_dim.7.rest_3_.refs_4_.refs_11_
  20.8 0.0 collective-permute-done
  20.8 0.7 tile.10.rest_1_.theta_ref
  21.5 2.4 %pack.3 = bf16[640,1024]{1,0:T(8,128)(2,1)} custom-call(s32[1]{0:T(128)} %bitcast.1.turn_ref, bf16[4,8,64,640]{3,2,1,0:T(8,128)(2,1)} %refs_8_.1, bf16[2,16,384,256]{3,2,1,0:T(8,128)(2,1)} %get-tuple-element.17.rest_0_.g_ref, f32[3,320]{1,0:T(4,128)} %tile.10.rest_1_.theta_ref, f32[640,1]{1,0:T(8,128)} %broadcast_in_dim.8.rest_2_.refs_2_.refs_9_, ...), custom_call_target="tpu_custom_call" | custom-call | bytes 2621440 | tf_op jit(solution)/shard_map/pack/pallas_call | solution.py:98
  23.9 3.5 %all-to-all-done.1 = bf16[8,80,1024]{2,1,0:T(8,128)(2,1)S(1)} async-done(((bf16[8,80,1024]{2,1,0:T(8,128)(2,1)}), bf16[8,80,1024]{2,1,0:T(8,128)(2,1)S(1)}, u32[]{:S(2)}, u32[]{:S(2)}) %all-to-all-start.1) | async-done | bytes 1310752 | tf_op jit(solution)/shard_map/all_to_all | solution.py:460
  27.3 0.0 copy-start.1
  27.4 5.4 %all-to-all-start = ((bf16[8,80,1024]{2,1,0:T(8,128)(2,1)}), bf16[8,80,1024]{2,1,0:T(8,128)(2,1)S(1)}, u32[]{:S(2)}, u32[]{:S(2)}) async-start(bf16[8,80,1024]{2,1,0:T(8,128)(2,1)} %bitcast.16), calls=%async_computation | async-start | bytes 2621440 | tf_op jit(solution)/shard_map/all_to_all | solution.py:464
  32.7 2.7 %collective-permute-start.9 = (bf16[640,1024]{1,0:T(8,128)(2,1)S(1)}, bf16[640,1024]{1,0:T(8,128)(2,1)}, u32[]{:S(2)}, u32[]{:S(2)}) collective-permute-start(bf16[640,1024]{1,0:T(8,128)(2,1)S(1)} %bitcast.14), channel_id=1, source_target_pairs={{8,0},{9,1},{10,2},{11,3},{12,4},{13,5},{14,6},{15,7},{16,12},{17,... | collective-permute-start | bytes 3932168 | tf_op jit(solution)/shard_map/ppermute | solution.py:454
  35.4 0.0 copy-done.1
  35.4 7.8 %low.1.low_ref = f32[2,4,512,320]{3,2,1,0:T(8,128)} custom-call(bf16[640,1024]{1,0:T(8,128)(2,1)} %bitcast.15, bf16[512,512]{1,0:T(8,128)(2,1)} %constant.40.clone.w_ref, bf16[2,16,384,128]{3,2,1,0:T(8,128)(2,1)} %get-tuple-element.18.g_ref, f32[3,320]{1,0:T(4,128)} %tile.10.rest_1_.theta_ref), custom_call_target="tpu_custom_call" | custom-call | flops 2000000000 | bytes 8000000 | tf_op jit(solution)/shard_map/low/pallas_call | solution.py:221
  43.2 8.2 %all-to-all-done = bf16[8,80,1024]{2,1,0:T(8,128)(2,1)S(1)} async-done(((bf16[8,80,1024]{2,1,0:T(8,128)(2,1)}), bf16[8,80,1024]{2,1,0:T(8,128)(2,1)S(1)}, u32[]{:S(2)}, u32[]{:S(2)}) %all-to-all-start) | async-done | bytes 1310752 | tf_op jit(solution)/shard_map/all_to_all | solution.py:464
  51.4 0.0 copy-start
  51.4 5.2 %collective-permute-start.1 = (bf16[640,1024]{1,0:T(8,128)(2,1)S(1)}, bf16[640,1024]{1,0:T(8,128)(2,1)}, u32[]{:S(2)}, u32[]{:S(2)}) collective-permute-start(bf16[640,1024]{1,0:T(8,128)(2,1)S(1)} %bitcast.10), channel_id=1, source_target_pairs={{0,8},{1,9},{2,10},{3,11},{4,12},{5,13},{6,14},{7,15},{8,20},{9,21... | collective-permute-start | bytes 3932168 | tf_op jit(solution)/shard_map/ppermute | solution.py:454
  56.6 0.0 collective-permute-done.9.halo_ref
  56.6 9.2 %conv.3 = bf16[640,1024]{1,0:T(8,128)(2,1)} custom-call(s32[1]{0:T(128)} %bitcast.me_ref, bf16[2,16,384,256]{3,2,1,0:T(8,128)(2,1)} %get-tuple-element.17.rest_0_.g_ref, f32[2,4,512,320]{3,2,1,0:T(8,128)} %low.1.low_ref, bf16[640,1024]{1,0:T(8,128)(2,1)S(1)} %bitcast.11, bf16[640,1024]{1,0:T(8,128)(2,1)} %collective-permute-done.9.halo_ref, ...), custom_call_target="tpu_custom_call" | custom-call | flops 6000000000 | bytes 12000000 | tf_op jit(solution)/shard_map/conv/pallas_call | solution.py:321
  65.9 0.0 copy-done
  65.9 3.6 %all-to-all-start.2 = ((bf16[8,80,1024]{2,1,0:T(8,128)(2,1)}), bf16[8,80,1024]{2,1,0:T(8,128)(2,1)S(1)}, u32[]{:S(2)}, u32[]{:S(2)}) async-start(bf16[8,80,1024]{2,1,0:T(8,128)(2,1)} %bitcast.17), calls=%async_computation.2 | async-start | bytes 2621440 | tf_op jit(solution)/shard_map/all_to_all | solution.py:470
  69.5 1.5 %collective-permute-done.1.halo_ref = bf16[640,1024]{1,0:T(8,128)(2,1)} collective-permute-done((bf16[640,1024]{1,0:T(8,128)(2,1)S(1)}, bf16[640,1024]{1,0:T(8,128)(2,1)}, u32[]{:S(2)}, u32[]{:S(2)}) %collective-permute-start.1) | collective-permute-done | bytes 1310752 | tf_op jit(solution)/shard_map/ppermute | solution.py:454
  70.9 10.0 %conv.2 = (bf16[80,1024]{1,0:T(8,128)(2,1)}, bf16[80,1024]{1,0:T(8,128)(2,1)}, bf16[80,1024]{1,0:T(8,128)(2,1)}, bf16[80,1024]{1,0:T(8,128)(2,1)}, bf16[80,1024]...) custom-call(s32[1]{0:T(128)} %bitcast.me_ref, ...), custom_call_target="tpu_custom_call" | custom-call | flops 6000000000 | bytes 12000000 | tf_op jit(solution)/shard_map/conv/pallas_call | solution.py:321
  80.9 0.7 collective-permute-start.2
  81.6 1.8 %collective-permute-start.3 = (bf16[80,1024]{1,0:T(8,128)(2,1)}, bf16[80,1024]{1,0:T(8,128)(2,1)S(1)}, u32[]{:S(2)}, u32[]{:S(2)}) collective-permute-start(bf16[80,1024]{1,0:T(8,128)(2,1)} %get-tuple-element.23), channel_id=1, source_target_pairs={{0,2},{1,3},{2,0},{3,1},{4,6},{5,7},{6,4},{7,5},{8,10},{9,11},{10,... | collective-permute-start | bytes 491528 | tf_op jit(solution)/shard_map/ppermute | solution.py:473
  83.4 1.5 %collective-permute-start.4 = (bf16[80,1024]{1,0:T(8,128)(2,1)}, bf16[80,1024]{1,0:T(8,128)(2,1)S(1)}, u32[]{:S(2)}, u32[]{:S(2)}) collective-permute-start(bf16[80,1024]{1,0:T(8,128)(2,1)} %get-tuple-element.24), channel_id=1, source_target_pairs={{0,3},{1,2},{2,1},{3,0},{4,7},{5,6},{6,5},{7,4},{8,11},{9,10},{10,... | collective-permute-start | bytes 491528 | tf_op jit(solution)/shard_map/ppermute | solution.py:473
  84.9 0.6 collective-permute-start.5
  85.4 0.0 collective-permute-start.6
  85.4 4.4 %collective-permute-done.2.refs_1_ = bf16[80,1024]{1,0:T(8,128)(2,1)S(1)} collective-permute-done((bf16[80,1024]{1,0:T(8,128)(2,1)}, bf16[80,1024]{1,0:T(8,128)(2,1)S(1)}, u32[]{:S(2)}, u32[]{:S(2)}) %collective-permute-start.2) | collective-permute-done | bytes 163872 | tf_op jit(solution)/shard_map/ppermute | solution.py:473
  89.9 0.0 copy-start.3
  89.9 3.3 %collective-permute-start.7 = (bf16[80,1024]{1,0:T(8,128)(2,1)}, bf16[80,1024]{1,0:T(8,128)(2,1)S(1)}, u32[]{:S(2)}, u32[]{:S(2)}) collective-permute-start(bf16[80,1024]{1,0:T(8,128)(2,1)} %get-tuple-element.27), channel_id=1, source_target_pairs={{0,6},{1,7},{2,4},{3,5},{4,2},{5,3},{6,0},{7,1},{8,14},{9,15},{10,... | collective-permute-start | bytes 491528 | tf_op jit(solution)/shard_map/ppermute | solution.py:473
  93.2 1.5 %collective-permute-done.3.refs_2_ = bf16[80,1024]{1,0:T(8,128)(2,1)S(1)} collective-permute-done((bf16[80,1024]{1,0:T(8,128)(2,1)}, bf16[80,1024]{1,0:T(8,128)(2,1)S(1)}, u32[]{:S(2)}, u32[]{:S(2)}) %collective-permute-start.3) | collective-permute-done | bytes 163872 | tf_op jit(solution)/shard_map/ppermute | solution.py:473
  94.7 1.7 %collective-permute-start.8 = (bf16[80,1024]{1,0:T(8,128)(2,1)}, bf16[80,1024]{1,0:T(8,128)(2,1)S(1)}, u32[]{:S(2)}, u32[]{:S(2)}) collective-permute-start(bf16[80,1024]{1,0:T(8,128)(2,1)} %get-tuple-element.28), channel_id=1, source_target_pairs={{0,7},{1,6},{2,5},{3,4},{4,3},{5,2},{6,1},{7,0},{8,15},{9,14},{10,... | collective-permute-start | bytes 491528 | tf_op jit(solution)/shard_map/ppermute | solution.py:473
  96.4 0.0 all-to-all-done.2
  96.4 9.2 %mlp.2.refs_13_ = bf16[4,8,64,640]{3,2,1,0:T(8,128)(2,1)} custom-call(s32[1]{0:T(128)} %bitcast.me_ref, s32[1]{0:T(128)} %bitcast.1.turn_ref, bf16[640,1024]{1,0:T(8,128)(2,1)S(1)} %bitcast.9, bf16[4,8,64,640]{3,2,1,0:T(8,128)(2,1)} %refs_8_.1, f32[640,1]{1,0:T(8,128)} %broadcast_in_dim.8.rest_2_.refs_2_.refs_9_, bf16[640,1280]{1,0:T(8,128)(2,1)} %refs_10_.1, ...), custom_call_target="tpu_custom_call" | custom-call | flops 3355443200 | bytes 12000000 | tf_op jit(solution)/shard_map/mlp/pallas_call | solution.py:406
  105.7 0.0 copy-done.3
  105.7 0.0 copy-done.4
  105.7 0.0 collective-permute-done.4.refs_3_
  105.7 0.0 copy-start.5
  105.7 0.0 collective-permute-done.5.refs_4_
  105.7 0.0 copy-start.6
  105.7 0.0 collective-permute-done.6.refs_5_
  105.7 0.0 copy-start.7
  105.7 0.0 collective-permute-done.7.refs_6_
  105.7 0.0 copy-start.8
  105.8 0.0 collective-permute-done.8.refs_7_
  105.8 0.0 copy-start.9
  105.8 0.6 copy-done.5
  106.4 0.1 copy-done.6
  106.4 0.1 copy-done.7
  106.5 0.0 copy-done.8
  106.5 0.1 copy-done.9
  106.6 10.2 %mlp.3 = bf16[4,8,64,640]{3,2,1,0:T(8,128)(2,1)} custom-call(s32[1]{0:T(128)} %bitcast.me_ref, s32[1]{0:T(128)} %bitcast.1.turn_ref, bf16[80,1024]{1,0:T(8,128)(2,1)} %get-tuple-element.21.refs_0_, bf16[80,1024]{1,0:T(8,128)(2,1)} %copy-done.3, bf16[80,1024]{1,0:T(8,128)(2,1)} %copy-done.4, ...), custom_call_target="tpu_custom_call", output_to_operand_aliasing={{}: (15, {})} | custom-call | flops 3355443200 | bytes 12000000 | tf_op jit(solution)/shard_map/mlp/pallas_call | solution.py:406
  (3 shorter events, 0.0 us)
Async XLA Ops:
  2.4 6.4 %copy-start.12 = (f32[3,80]{1,0:T(4,128)S(1)}, f32[3,80]{1,0:T(4,128)}, u32[]{:S(2)}) copy-start(f32[3,80]{1,0:T(4,128)} %param.13) | copy-start | bytes 2884
  2.4 7.8 %copy-start.2 = (f32[8,9,3,512]{3,0,2,1:T(8,128)S(1)}, f32[8,9,3,512]{3,0,2,1:T(8,128)}, u32[]{:S(2)}) copy-start(f32[8,9,3,512]{3,0,2,1:T(8,128)} %param.12) | copy-start | bytes 1327108
  2.4 25.0 %all-to-all-start.1 = ((bf16[8,80,1024]{2,1,0:T(8,128)(2,1)}), bf16[8,80,1024]{2,1,0:T(8,128)(2,1)S(1)}, u32[]{:S(2)}, u32[]{:S(2)}) async-start(bf16[8,80,1024]{2,1,0:T(8,128)(2,1)} %bitcast.13), calls=%async_computation.1 | async-start | bytes 2621440 | tf_op jit(solution)/shard_map/all_to_all | solution.py:460
  8.7 12.0 %collective-permute-start = (f32[3,80]{1,0:T(4,128)S(1)}, f32[3,80]{1,0:T(4,128)S(1)}, u32[]{:S(2)}, u32[]{:S(2)}) collective-permute-start(f32[3,80]{1,0:T(4,128)S(1)} %copy-done.12), channel_id=1, source_target_pairs={{0,4},{1,5},{2,6},{3,7},{4,0},{5,1},{6,2},{7,3},{8,12},{9,13},{10,... | collective-permute-start | bytes 2888 | tf_op jit(solution)/shard_map/ppermute | solution.py:455
  11.5 7.8 %copy-start.11 = (f32[640]{0:T(1024)S(1)}, f32[640]{0:T(1024)}, u32[]{:S(2)}) copy-start(f32[640]{0:T(1024)} %param.16) | copy-start | bytes 7684
  11.5 8.7 %copy-start.10 = (f32[1280]{0:T(1024)S(1)}, f32[1280]{0:T(1024)}, u32[]{:S(2)}) copy-start(f32[1280]{0:T(1024)} %param.18) | copy-start | bytes 15364
  27.3 8.1 %copy-start.1 = (bf16[8,80,1024]{2,1,0:T(8,128)(2,1)}, bf16[8,80,1024]{2,1,0:T(8,128)(2,1)S(1)}, u32[]{:S(2)}) copy-start(bf16[8,80,1024]{2,1,0:T(8,128)(2,1)S(1)} %all-to-all-done.1) | copy-start | bytes 3932164
  27.4 24.0 %all-to-all-start = ((bf16[8,80,1024]{2,1,0:T(8,128)(2,1)}), bf16[8,80,1024]{2,1,0:T(8,128)(2,1)S(1)}, u32[]{:S(2)}, u32[]{:S(2)}) async-start(bf16[8,80,1024]{2,1,0:T(8,128)(2,1)} %bitcast.16), calls=%async_computation | async-start | bytes 2621440 | tf_op jit(solution)/shard_map/all_to_all | solution.py:464
  32.7 23.8 %collective-permute-start.9 = (bf16[640,1024]{1,0:T(8,128)(2,1)S(1)}, bf16[640,1024]{1,0:T(8,128)(2,1)}, u32[]{:S(2)}, u32[]{:S(2)}) collective-permute-start(bf16[640,1024]{1,0:T(8,128)(2,1)S(1)} %bitcast.14), channel_id=1, source_target_pairs={{8,0},{9,1},{10,2},{11,3},{12,4},{13,5},{14,6},{15,7},{16,12},{17,... | collective-permute-start | bytes 3932168 | tf_op jit(solution)/shard_map/ppermute | solution.py:454
  51.4 14.5 %copy-start = (bf16[8,80,1024]{2,1,0:T(8,128)(2,1)}, bf16[8,80,1024]{2,1,0:T(8,128)(2,1)S(1)}, u32[]{:S(2)}) copy-start(bf16[8,80,1024]{2,1,0:T(8,128)(2,1)S(1)} %all-to-all-done) | copy-start | bytes 3932164
  51.4 19.5 %collective-permute-start.1 = (bf16[640,1024]{1,0:T(8,128)(2,1)S(1)}, bf16[640,1024]{1,0:T(8,128)(2,1)}, u32[]{:S(2)}, u32[]{:S(2)}) collective-permute-start(bf16[640,1024]{1,0:T(8,128)(2,1)S(1)} %bitcast.10), channel_id=1, source_target_pairs={{0,8},{1,9},{2,10},{3,11},{4,12},{5,13},{6,14},{7,15},{8,20},{9,21... | collective-permute-start | bytes 3932168 | tf_op jit(solution)/shard_map/ppermute | solution.py:454
  65.9 30.5 %all-to-all-start.2 = ((bf16[8,80,1024]{2,1,0:T(8,128)(2,1)}), bf16[8,80,1024]{2,1,0:T(8,128)(2,1)S(1)}, u32[]{:S(2)}, u32[]{:S(2)}) async-start(bf16[8,80,1024]{2,1,0:T(8,128)(2,1)} %bitcast.17), calls=%async_computation.2 | async-start | bytes 2621440 | tf_op jit(solution)/shard_map/all_to_all | solution.py:470
  80.9 8.9 %collective-permute-start.2 = (bf16[80,1024]{1,0:T(8,128)(2,1)}, bf16[80,1024]{1,0:T(8,128)(2,1)S(1)}, u32[]{:S(2)}, u32[]{:S(2)}) collective-permute-start(bf16[80,1024]{1,0:T(8,128)(2,1)} %get-tuple-element.22), channel_id=1, source_target_pairs={{0,1},{1,0},{2,3},{3,2},{4,5},{5,4},{6,7},{7,6},{8,9},{9,8},{10,11... | collective-permute-start | bytes 491528 | tf_op jit(solution)/shard_map/ppermute | solution.py:473
  81.6 13.1 %collective-permute-start.3 = (bf16[80,1024]{1,0:T(8,128)(2,1)}, bf16[80,1024]{1,0:T(8,128)(2,1)S(1)}, u32[]{:S(2)}, u32[]{:S(2)}) collective-permute-start(bf16[80,1024]{1,0:T(8,128)(2,1)} %get-tuple-element.23), channel_id=1, source_target_pairs={{0,2},{1,3},{2,0},{3,1},{4,6},{5,7},{6,4},{7,5},{8,10},{9,11},{10,... | collective-permute-start | bytes 491528 | tf_op jit(solution)/shard_map/ppermute | solution.py:473
  83.4 22.3 %collective-permute-start.4 = (bf16[80,1024]{1,0:T(8,128)(2,1)}, bf16[80,1024]{1,0:T(8,128)(2,1)S(1)}, u32[]{:S(2)}, u32[]{:S(2)}) collective-permute-start(bf16[80,1024]{1,0:T(8,128)(2,1)} %get-tuple-element.24), channel_id=1, source_target_pairs={{0,3},{1,2},{2,1},{3,0},{4,7},{5,6},{6,5},{7,4},{8,11},{9,10},{10,... | collective-permute-start | bytes 491528 | tf_op jit(solution)/shard_map/ppermute | solution.py:473
  84.9 20.8 %collective-permute-start.5 = (bf16[80,1024]{1,0:T(8,128)(2,1)}, bf16[80,1024]{1,0:T(8,128)(2,1)S(1)}, u32[]{:S(2)}, u32[]{:S(2)}) collective-permute-start(bf16[80,1024]{1,0:T(8,128)(2,1)} %get-tuple-element.25), channel_id=1, source_target_pairs={{0,4},{1,5},{2,6},{3,7},{4,0},{5,1},{6,2},{7,3},{8,12},{9,13},{10,... | collective-permute-start | bytes 491528 | tf_op jit(solution)/shard_map/ppermute | solution.py:473
  85.4 20.3 %collective-permute-start.6 = (bf16[80,1024]{1,0:T(8,128)(2,1)}, bf16[80,1024]{1,0:T(8,128)(2,1)S(1)}, u32[]{:S(2)}, u32[]{:S(2)}) collective-permute-start(bf16[80,1024]{1,0:T(8,128)(2,1)} %get-tuple-element.26), channel_id=1, source_target_pairs={{0,5},{1,4},{2,7},{3,6},{4,1},{5,0},{6,3},{7,2},{8,13},{9,12},{10,... | collective-permute-start | bytes 491528 | tf_op jit(solution)/shard_map/ppermute | solution.py:473
  89.9 15.8 %copy-start.3 = (bf16[80,1024]{1,0:T(8,128)(2,1)}, bf16[80,1024]{1,0:T(8,128)(2,1)S(1)}, u32[]{:S(2)}) copy-start(bf16[80,1024]{1,0:T(8,128)(2,1)S(1)} %collective-permute-done.2.refs_1_) | copy-start | bytes 491524
  89.9 15.9 %collective-permute-start.7 = (bf16[80,1024]{1,0:T(8,128)(2,1)}, bf16[80,1024]{1,0:T(8,128)(2,1)S(1)}, u32[]{:S(2)}, u32[]{:S(2)}) collective-permute-start(bf16[80,1024]{1,0:T(8,128)(2,1)} %get-tuple-element.27), channel_id=1, source_target_pairs={{0,6},{1,7},{2,4},{3,5},{4,2},{5,3},{6,0},{7,1},{8,14},{9,15},{10,... | collective-permute-start | bytes 491528 | tf_op jit(solution)/shard_map/ppermute | solution.py:473
  94.7 11.0 %copy-start.4 = (bf16[80,1024]{1,0:T(8,128)(2,1)}, bf16[80,1024]{1,0:T(8,128)(2,1)S(1)}, u32[]{:S(2)}) copy-start(bf16[80,1024]{1,0:T(8,128)(2,1)S(1)} %collective-permute-done.3.refs_2_) | copy-start | bytes 491524
  94.7 11.1 %collective-permute-start.8 = (bf16[80,1024]{1,0:T(8,128)(2,1)}, bf16[80,1024]{1,0:T(8,128)(2,1)S(1)}, u32[]{:S(2)}, u32[]{:S(2)}) collective-permute-start(bf16[80,1024]{1,0:T(8,128)(2,1)} %get-tuple-element.28), channel_id=1, source_target_pairs={{0,7},{1,6},{2,5},{3,4},{4,3},{5,2},{6,1},{7,0},{8,15},{9,14},{10,... | collective-permute-start | bytes 491528 | tf_op jit(solution)/shard_map/ppermute | solution.py:473
  105.7 0.7 copy-start.5
  105.7 0.7 copy-start.6
  105.7 0.8 copy-start.7
  105.7 0.8 copy-start.8
  105.8 0.8 copy-start.9

commit v4 on v3

--- a/solution.py
+++ b/solution.py
@@ -345,13 +345,8 @@
 def mlp_kernel(half, count, me_ref, turn_ref, *refs):
     pieces, refs = refs[:count], refs[count:]
     x_ref, gain_ref, w_in_ref, b_in_ref, w_out_ref, *rest = refs
-    o_ref, y_buf, x_buf, w_in_buf, w_out_buf, o_buf, y_sem, x_sem, w_sem, o_sem = rest[-10:]
+    o_ref, y_buf, x_buf, w_in_buf, w_out_buf, o_buf, x_sem, w_sem, o_sem = rest[-9:]
     turned_by = turn_ref[0] * (LON_DEV // 2)
-    ys = [
-        pltpu.make_async_copy(piece, y_buf.at[block_of(me_ref[0] ^ k ^ turned_by)], y_sem.at[k])
-        for k, piece in enumerate(pieces)
-        if count > 1
-    ]
     wide = HALF * CHUNK
     rows = pl.ds(half * HALF, HALF)
     first = pltpu.make_async_copy(w_in_ref, w_in_buf, w_sem.at[0])
@@ -359,10 +354,11 @@
     xs = [
         pltpu.make_async_copy(x_ref.at[e, rows], x_buf.at[e], x_sem.at[e]) for e in range(ENS)
     ]
-    for c in [*ys, first, second, *xs]:
+    for c in [first, second, *xs]:
         c.start()
-    for c in ys:
-        c.wait()
+    if count > 1:
+        for k, piece in enumerate(pieces):
+            y_buf[block_of(me_ref[0] ^ k ^ turned_by), :] = piece[...]
     at = pl.multiple_of(turn_ref[0] * MID, MID)
     outs = []
     for part in range(ENS // GROUP):
@@ -406,7 +402,7 @@
     return pl.pallas_call(
         functools.partial(mlp_kernel, half, count),
         in_specs=[SMEM, SMEM]
-        + ([ANY] * count if count > 1 else [VMEM])
+        + [VMEM] * count
         + [ANY, VMEM, ANY, VMEM, ANY]
         + [ANY] * len(extra),
         out_specs=ANY,
@@ -418,7 +414,6 @@
             pltpu.VMEM((CHAN, HID), BF16),
             pltpu.VMEM((HID, CHAN), BF16),
             pltpu.VMEM(points, BF16),
-            sems((LON_DEV,)),
             sems((ENS,)),
             sems((2,)),
             sems((ENS,)),
@@ -426,7 +421,7 @@
         compiler_params=params(),
         cost_estimate=cost(4 * PTS * CHAN * HID, 1.2e7),
         name="mlp",
-    )(me, turn, *(ys if count > 1 else [near(ys[0])]), fields, gain, w_in, b_in, w_out, *extra)
+    )(me, turn, *(near(y) for y in ys), fields, gain, w_in, b_in, w_out, *extra)
 
 
 def turned(lat):

time: 118 us -> 116 us (0.983)
  no operation moved by 1% of the time
where the time goes in v4:
time: 116 us; the launch traced here: 115 us
  Pallas kernels  57.9 us (50%)
  starting transfers between devices  34.2 us (29%)
  waiting for transfers between devices  19.1 us (16%)
  local copies, waits for them, and re-layouts  3.51 us (3%)
    pallas_call x2, Pallas kernels, conv(): pl.pallas_call(functools.partial(conv_kernel, half), in_specs=[SMEM, ANY,...  19.2 us
    pallas_call x2, Pallas kernels, mlp(): pl.pallas_call(functools.partial(mlp_kernel, half, count), in_specs=[SMEM...  18.4 us
    ppermute x7, starting transfers between devices, shards(): lax.ppermute(pieces[k], 'lon', [(t, t ^ k) for t in range(lons)])  9.55 us
    all_to_all x1, waiting for transfers between devices, shards(): high = swap(pack(turn, fields, 1, coef, theta4, rest[0], rest[2]))  8.19 us
    ppermute x2, starting transfers between devices, shards(): lax.ppermute(v, ('lat', 'lon'), band_perm(lats, lons, step))  7.86 us
    pallas_call x1, Pallas kernels, coefs(): pl.pallas_call(coef_kernel, grid=(2,), in_specs=[smem, smem, smem, pl.Blo...  7.81 us
    pallas_call x1, Pallas kernels, low_share(): pl.pallas_call(low_kernel, grid=(2,), in_specs=[whole(CHAN, PTS), whole(N...  7.76 us
    all_to_all x1, starting transfers between devices, shards(): low = swap(packed_low)  6.35 us
  transfers between devices with their start and end apart: 13, of which 5 were waited for; matrix products, arithmetic and copies ran while one was open for 3% of the time, Pallas kernels for 40%

profile of v4, /device:TPU:1, one launch (start us, length us, event | category | flops | bytes accessed | tf_op | source)
XLA Modules:
  0.0 115.0 jit_solution(8374840643279556445)
XLA Ops:
  0.0 2.3 %pack.2.rest_0_ = bf16[640,1024]{1,0:T(8,128)(2,1)} custom-call(s32[1]{0:T(128)} %bitcast.1.turn_ref, bf16[4,8,64,640]{3,2,1,0:T(8,128)(2,1)} %refs_8_.1), custom_call_target="tpu_custom_call" | custom-call | bytes 2621440 | tf_op jit(solution)/shard_map/pack/pallas_call | solution.py:98
  2.4 0.0 copy-start.6
  2.4 0.0 copy-start.3
  2.4 6.3 %all-to-all-start.1 = ((bf16[8,80,1024]{2,1,0:T(8,128)(2,1)}), bf16[8,80,1024]{2,1,0:T(8,128)(2,1)S(1)}, u32[]{:S(2)}, u32[]{:S(2)}) async-start(bf16[8,80,1024]{2,1,0:T(8,128)(2,1)} %bitcast.13), calls=%async_computation.1 | async-start | bytes 2621440 | tf_op jit(solution)/shard_map/all_to_all | solution.py:455
  8.7 0.0 copy-done.6
  8.7 1.5 %collective-permute-start = (f32[3,80]{1,0:T(4,128)S(1)}, f32[3,80]{1,0:T(4,128)S(1)}, u32[]{:S(2)}, u32[]{:S(2)}) collective-permute-start(f32[3,80]{1,0:T(4,128)S(1)} %copy-done.6), channel_id=1, source_target_pairs={{0,4},{1,5},{2,6},{3,7},{4,0},{5,1},{6,2},{7,3},{8,12},{9,13},{10,... | collective-permute-start | bytes 2888 | tf_op jit(solution)/shard_map/ppermute | solution.py:450
  10.2 0.0 copy-done.3
  10.2 0.3 copy.14
  10.5 1.0 reshape.25.k_ref
  11.5 0.0 copy-start.5
  11.5 0.0 copy-start.4
  11.5 7.8 %coefs.1 = (bf16[2,16,384,128]{3,2,1,0:T(8,128)(2,1)}, bf16[2,16,384,256]{3,2,1,0:T(8,128)(2,1)}) custom-call(s32[8]{0:T(128)} %start_ref.1, s32[8]{0:T(128)} %count_ref.1, s32[1]{0:T(128)} %bitcast.2.first_ref, f32[2,108,512]{2,1,0:T(8,128)} %reshape.25.k_ref, bf16[512,512]{1,0:T(8,128)(2,1)} %constant.40.clone.w_ref, bf16[640,1024]{1,0:T(8,128)(2,1)} %pack.2.rest_0_), custom_call_target="tpu_custom_call" | custom-call | flops 8000000000 | bytes 10000000 | tf_op jit(solution)/shard_map/coefs/pallas_call | solution.py:176
  19.3 0.0 copy-done.5
  19.3 0.9 broadcast_in_dim.8.rest_2_.refs_2_.refs_9_
  20.2 0.0 copy-done.4
  20.2 0.6 broadcast_in_dim.7.rest_3_.refs_4_.refs_11_
  20.8 0.0 collective-permute-done
  20.8 0.7 tile.10.rest_1_.theta_ref
  21.5 2.4 %pack.3 = bf16[640,1024]{1,0:T(8,128)(2,1)} custom-call(s32[1]{0:T(128)} %bitcast.1.turn_ref, bf16[4,8,64,640]{3,2,1,0:T(8,128)(2,1)} %refs_8_.1, bf16[2,16,384,256]{3,2,1,0:T(8,128)(2,1)} %get-tuple-element.17.rest_0_.g_ref, f32[3,320]{1,0:T(4,128)} %tile.10.rest_1_.theta_ref, f32[640,1]{1,0:T(8,128)} %broadcast_in_dim.8.rest_2_.refs_2_.refs_9_, ...), custom_call_target="tpu_custom_call" | custom-call | bytes 2621440 | tf_op jit(solution)/shard_map/pack/pallas_call | solution.py:98
  23.9 3.4 %all-to-all-done.1 = bf16[8,80,1024]{2,1,0:T(8,128)(2,1)S(1)} async-done(((bf16[8,80,1024]{2,1,0:T(8,128)(2,1)}), bf16[8,80,1024]{2,1,0:T(8,128)(2,1)S(1)}, u32[]{:S(2)}, u32[]{:S(2)}) %all-to-all-start.1) | async-done | bytes 1310752 | tf_op jit(solution)/shard_map/all_to_all | solution.py:455
  27.3 0.0 copy-start.2
  27.4 5.4 %all-to-all-start = ((bf16[8,80,1024]{2,1,0:T(8,128)(2,1)}), bf16[8,80,1024]{2,1,0:T(8,128)(2,1)S(1)}, u32[]{:S(2)}, u32[]{:S(2)}) async-start(bf16[8,80,1024]{2,1,0:T(8,128)(2,1)} %bitcast.16), calls=%async_computation | async-start | bytes 2621440 | tf_op jit(solution)/shard_map/all_to_all | solution.py:459
  32.7 2.7 %collective-permute-start.9 = (bf16[640,1024]{1,0:T(8,128)(2,1)S(1)}, bf16[640,1024]{1,0:T(8,128)(2,1)}, u32[]{:S(2)}, u32[]{:S(2)}) collective-permute-start(bf16[640,1024]{1,0:T(8,128)(2,1)S(1)} %bitcast.14), channel_id=1, source_target_pairs={{8,0},{9,1},{10,2},{11,3},{12,4},{13,5},{14,6},{15,7},{16,12},{17,... | collective-permute-start | bytes 3932168 | tf_op jit(solution)/shard_map/ppermute | solution.py:449
  35.4 0.0 copy-done.2
  35.4 7.8 %low.1.low_ref = f32[2,4,512,320]{3,2,1,0:T(8,128)} custom-call(bf16[640,1024]{1,0:T(8,128)(2,1)} %bitcast.15, bf16[512,512]{1,0:T(8,128)(2,1)} %constant.40.clone.w_ref, bf16[2,16,384,128]{3,2,1,0:T(8,128)(2,1)} %get-tuple-element.18.g_ref, f32[3,320]{1,0:T(4,128)} %tile.10.rest_1_.theta_ref), custom_call_target="tpu_custom_call" | custom-call | flops 2000000000 | bytes 8000000 | tf_op jit(solution)/shard_map/low/pallas_call | solution.py:221
  43.2 8.2 %all-to-all-done = bf16[8,80,1024]{2,1,0:T(8,128)(2,1)S(1)} async-done(((bf16[8,80,1024]{2,1,0:T(8,128)(2,1)}), bf16[8,80,1024]{2,1,0:T(8,128)(2,1)S(1)}, u32[]{:S(2)}, u32[]{:S(2)}) %all-to-all-start) | async-done | bytes 1310752 | tf_op jit(solution)/shard_map/all_to_all | solution.py:459
  51.4 0.0 copy-start
  51.4 5.2 %collective-permute-start.1 = (bf16[640,1024]{1,0:T(8,128)(2,1)S(1)}, bf16[640,1024]{1,0:T(8,128)(2,1)}, u32[]{:S(2)}, u32[]{:S(2)}) collective-permute-start(bf16[640,1024]{1,0:T(8,128)(2,1)S(1)} %bitcast.10), channel_id=1, source_target_pairs={{0,8},{1,9},{2,10},{3,11},{4,12},{5,13},{6,14},{7,15},{8,20},{9,21... | collective-permute-start | bytes 3932168 | tf_op jit(solution)/shard_map/ppermute | solution.py:449
  56.6 0.0 collective-permute-done.9.halo_ref
  56.6 9.2 %conv.3 = bf16[640,1024]{1,0:T(8,128)(2,1)} custom-call(s32[1]{0:T(128)} %bitcast.me_ref, bf16[2,16,384,256]{3,2,1,0:T(8,128)(2,1)} %get-tuple-element.17.rest_0_.g_ref, f32[2,4,512,320]{3,2,1,0:T(8,128)} %low.1.low_ref, bf16[640,1024]{1,0:T(8,128)(2,1)S(1)} %bitcast.11, bf16[640,1024]{1,0:T(8,128)(2,1)} %collective-permute-done.9.halo_ref, ...), custom_call_target="tpu_custom_call" | custom-call | flops 6000000000 | bytes 12000000 | tf_op jit(solution)/shard_map/conv/pallas_call | solution.py:321
  65.8 0.0 copy-done
  65.8 3.6 %all-to-all-start.2 = ((bf16[8,80,1024]{2,1,0:T(8,128)(2,1)}), bf16[8,80,1024]{2,1,0:T(8,128)(2,1)S(1)}, u32[]{:S(2)}, u32[]{:S(2)}) async-start(bf16[8,80,1024]{2,1,0:T(8,128)(2,1)} %bitcast.17), calls=%async_computation.2 | async-start | bytes 2621440 | tf_op jit(solution)/shard_map/all_to_all | solution.py:465
  69.4 1.5 %collective-permute-done.1.halo_ref = bf16[640,1024]{1,0:T(8,128)(2,1)} collective-permute-done((bf16[640,1024]{1,0:T(8,128)(2,1)S(1)}, bf16[640,1024]{1,0:T(8,128)(2,1)}, u32[]{:S(2)}, u32[]{:S(2)}) %collective-permute-start.1) | collective-permute-done | bytes 1310752 | tf_op jit(solution)/shard_map/ppermute | solution.py:449
  70.9 10.0 %conv.2 = (bf16[80,1024]{1,0:T(8,128)(2,1)}, bf16[80,1024]{1,0:T(8,128)(2,1)}, bf16[80,1024]{1,0:T(8,128)(2,1)}, bf16[80,1024]{1,0:T(8,128)(2,1)}, bf16[80,1024]...) custom-call(s32[1]{0:T(128)} %bitcast.me_ref, ...), custom_call_target="tpu_custom_call" | custom-call | flops 6000000000 | bytes 12000000 | tf_op jit(solution)/shard_map/conv/pallas_call | solution.py:321
  80.9 0.7 collective-permute-start.2
  81.5 1.8 %collective-permute-start.3 = (bf16[80,1024]{1,0:T(8,128)(2,1)}, bf16[80,1024]{1,0:T(8,128)(2,1)S(1)}, u32[]{:S(2)}, u32[]{:S(2)}) collective-permute-start(bf16[80,1024]{1,0:T(8,128)(2,1)} %get-tuple-element.23), channel_id=1, source_target_pairs={{0,2},{1,3},{2,0},{3,1},{4,6},{5,7},{6,4},{7,5},{8,10},{9,11},{10,... | collective-permute-start | bytes 491528 | tf_op jit(solution)/shard_map/ppermute | solution.py:468
  83.3 1.5 %collective-permute-start.4 = (bf16[80,1024]{1,0:T(8,128)(2,1)}, bf16[80,1024]{1,0:T(8,128)(2,1)S(1)}, u32[]{:S(2)}, u32[]{:S(2)}) collective-permute-start(bf16[80,1024]{1,0:T(8,128)(2,1)} %get-tuple-element.24), channel_id=1, source_target_pairs={{0,3},{1,2},{2,1},{3,0},{4,7},{5,6},{6,5},{7,4},{8,11},{9,10},{10,... | collective-permute-start | bytes 491528 | tf_op jit(solution)/shard_map/ppermute | solution.py:468
  84.8 0.6 collective-permute-start.5
  85.4 0.0 collective-permute-start.6
  85.4 4.4 %collective-permute-done.2.refs_1_ = bf16[80,1024]{1,0:T(8,128)(2,1)S(1)} collective-permute-done((bf16[80,1024]{1,0:T(8,128)(2,1)}, bf16[80,1024]{1,0:T(8,128)(2,1)S(1)}, u32[]{:S(2)}, u32[]{:S(2)}) %collective-permute-start.2) | collective-permute-done | bytes 163872 | tf_op jit(solution)/shard_map/ppermute | solution.py:468
  89.8 3.3 %collective-permute-start.7 = (bf16[80,1024]{1,0:T(8,128)(2,1)}, bf16[80,1024]{1,0:T(8,128)(2,1)S(1)}, u32[]{:S(2)}, u32[]{:S(2)}) collective-permute-start(bf16[80,1024]{1,0:T(8,128)(2,1)} %get-tuple-element.27), channel_id=1, source_target_pairs={{0,6},{1,7},{2,4},{3,5},{4,2},{5,3},{6,0},{7,1},{8,14},{9,15},{10,... | collective-permute-start | bytes 491528 | tf_op jit(solution)/shard_map/ppermute | solution.py:468
  93.1 1.5 %collective-permute-done.3.refs_2_ = bf16[80,1024]{1,0:T(8,128)(2,1)S(1)} collective-permute-done((bf16[80,1024]{1,0:T(8,128)(2,1)}, bf16[80,1024]{1,0:T(8,128)(2,1)S(1)}, u32[]{:S(2)}, u32[]{:S(2)}) %collective-permute-start.3) | collective-permute-done | bytes 163872 | tf_op jit(solution)/shard_map/ppermute | solution.py:468
  94.6 1.7 %collective-permute-start.8 = (bf16[80,1024]{1,0:T(8,128)(2,1)}, bf16[80,1024]{1,0:T(8,128)(2,1)S(1)}, u32[]{:S(2)}, u32[]{:S(2)}) collective-permute-start(bf16[80,1024]{1,0:T(8,128)(2,1)} %get-tuple-element.28), channel_id=1, source_target_pairs={{0,7},{1,6},{2,5},{3,4},{4,3},{5,2},{6,1},{7,0},{8,15},{9,14},{10,... | collective-permute-start | bytes 491528 | tf_op jit(solution)/shard_map/ppermute | solution.py:468
  96.3 0.0 all-to-all-done.2
  96.3 0.0 copy-start.1
  96.3 9.2 %mlp.2.refs_13_ = bf16[4,8,64,640]{3,2,1,0:T(8,128)(2,1)} custom-call(s32[1]{0:T(128)} %bitcast.me_ref, s32[1]{0:T(128)} %bitcast.1.turn_ref, bf16[640,1024]{1,0:T(8,128)(2,1)S(1)} %bitcast.9, bf16[4,8,64,640]{3,2,1,0:T(8,128)(2,1)} %refs_8_.1, f32[640,1]{1,0:T(8,128)} %broadcast_in_dim.8.rest_2_.refs_2_.refs_9_, bf16[640,1280]{1,0:T(8,128)(2,1)} %refs_10_.1, ...), custom_call_target="tpu_custom_call" | custom-call | flops 3355443200 | bytes 12000000 | tf_op jit(solution)/shard_map/mlp/pallas_call | solution.py:402
  105.6 0.0 collective-permute-done.4.refs_3_
  105.6 0.0 collective-permute-done.5.refs_4_
  105.6 0.0 collective-permute-done.6.refs_5_
  105.6 0.0 collective-permute-done.7.refs_6_
  105.6 0.0 collective-permute-done.8.refs_7_
  105.6 0.0 copy-done.1
  105.6 9.2 %mlp.3 = bf16[4,8,64,640]{3,2,1,0:T(8,128)(2,1)} custom-call(s32[1]{0:T(128)} %bitcast.me_ref, s32[1]{0:T(128)} %bitcast.1.turn_ref, bf16[80,1024]{1,0:T(8,128)(2,1)S(1)} %copy-done.1, bf16[80,1024]{1,0:T(8,128)(2,1)S(1)} %collective-permute-done.2.refs_1_, bf16[80,1024]{1,0:T(8,128)(2,1)S(1)} %collective-permute-done.3.refs_2_, ...), custom_call_target="tpu_custom_call", output_to_operand_aliasing={{}: (15, {})} | custom-call | flops 3355443200 | bytes 12000000 | tf_op jit(solution)/shard_map/mlp/pallas_call | solution.py:402
  (2 shorter events, 0.0 us)
Async XLA Ops:
  2.4 6.4 %copy-start.6 = (f32[3,80]{1,0:T(4,128)S(1)}, f32[3,80]{1,0:T(4,128)}, u32[]{:S(2)}) copy-start(f32[3,80]{1,0:T(4,128)} %param.13) | copy-start | bytes 2884
  2.4 7.8 %copy-start.3 = (f32[8,9,3,512]{3,0,2,1:T(8,128)S(1)}, f32[8,9,3,512]{3,0,2,1:T(8,128)}, u32[]{:S(2)}) copy-start(f32[8,9,3,512]{3,0,2,1:T(8,128)} %param.12) | copy-start | bytes 1327108
  2.4 25.0 %all-to-all-start.1 = ((bf16[8,80,1024]{2,1,0:T(8,128)(2,1)}), bf16[8,80,1024]{2,1,0:T(8,128)(2,1)S(1)}, u32[]{:S(2)}, u32[]{:S(2)}) async-start(bf16[8,80,1024]{2,1,0:T(8,128)(2,1)} %bitcast.13), calls=%async_computation.1 | async-start | bytes 2621440 | tf_op jit(solution)/shard_map/all_to_all | solution.py:455
  8.7 12.1 %collective-permute-start = (f32[3,80]{1,0:T(4,128)S(1)}, f32[3,80]{1,0:T(4,128)S(1)}, u32[]{:S(2)}, u32[]{:S(2)}) collective-permute-start(f32[3,80]{1,0:T(4,128)S(1)} %copy-done.6), channel_id=1, source_target_pairs={{0,4},{1,5},{2,6},{3,7},{4,0},{5,1},{6,2},{7,3},{8,12},{9,13},{10,... | collective-permute-start | bytes 2888 | tf_op jit(solution)/shard_map/ppermute | solution.py:450
  11.5 7.8 %copy-start.5 = (f32[640]{0:T(1024)S(1)}, f32[640]{0:T(1024)}, u32[]{:S(2)}) copy-start(f32[640]{0:T(1024)} %param.16) | copy-start | bytes 7684
  11.5 8.7 %copy-start.4 = (f32[1280]{0:T(1024)S(1)}, f32[1280]{0:T(1024)}, u32[]{:S(2)}) copy-start(f32[1280]{0:T(1024)} %param.18) | copy-start | bytes 15364
  27.3 8.0 %copy-start.2 = (bf16[8,80,1024]{2,1,0:T(8,128)(2,1)}, bf16[8,80,1024]{2,1,0:T(8,128)(2,1)S(1)}, u32[]{:S(2)}) copy-start(bf16[8,80,1024]{2,1,0:T(8,128)(2,1)S(1)} %all-to-all-done.1) | copy-start | bytes 3932164
  27.4 24.0 %all-to-all-start = ((bf16[8,80,1024]{2,1,0:T(8,128)(2,1)}), bf16[8,80,1024]{2,1,0:T(8,128)(2,1)S(1)}, u32[]{:S(2)}, u32[]{:S(2)}) async-start(bf16[8,80,1024]{2,1,0:T(8,128)(2,1)} %bitcast.16), calls=%async_computation | async-start | bytes 2621440 | tf_op jit(solution)/shard_map/all_to_all | solution.py:459
  32.7 23.8 %collective-permute-start.9 = (bf16[640,1024]{1,0:T(8,128)(2,1)S(1)}, bf16[640,1024]{1,0:T(8,128)(2,1)}, u32[]{:S(2)}, u32[]{:S(2)}) collective-permute-start(bf16[640,1024]{1,0:T(8,128)(2,1)S(1)} %bitcast.14), channel_id=1, source_target_pairs={{8,0},{9,1},{10,2},{11,3},{12,4},{13,5},{14,6},{15,7},{16,12},{17,... | collective-permute-start | bytes 3932168 | tf_op jit(solution)/shard_map/ppermute | solution.py:449
  51.4 14.5 %copy-start = (bf16[8,80,1024]{2,1,0:T(8,128)(2,1)}, bf16[8,80,1024]{2,1,0:T(8,128)(2,1)S(1)}, u32[]{:S(2)}) copy-start(bf16[8,80,1024]{2,1,0:T(8,128)(2,1)S(1)} %all-to-all-done) | copy-start | bytes 3932164
  51.4 19.5 %collective-permute-start.1 = (bf16[640,1024]{1,0:T(8,128)(2,1)S(1)}, bf16[640,1024]{1,0:T(8,128)(2,1)}, u32[]{:S(2)}, u32[]{:S(2)}) collective-permute-start(bf16[640,1024]{1,0:T(8,128)(2,1)S(1)} %bitcast.10), channel_id=1, source_target_pairs={{0,8},{1,9},{2,10},{3,11},{4,12},{5,13},{6,14},{7,15},{8,20},{9,21... | collective-permute-start | bytes 3932168 | tf_op jit(solution)/shard_map/ppermute | solution.py:449
  65.8 30.5 %all-to-all-start.2 = ((bf16[8,80,1024]{2,1,0:T(8,128)(2,1)}), bf16[8,80,1024]{2,1,0:T(8,128)(2,1)S(1)}, u32[]{:S(2)}, u32[]{:S(2)}) async-start(bf16[8,80,1024]{2,1,0:T(8,128)(2,1)} %bitcast.17), calls=%async_computation.2 | async-start | bytes 2621440 | tf_op jit(solution)/shard_map/all_to_all | solution.py:465
  80.9 8.9 %collective-permute-start.2 = (bf16[80,1024]{1,0:T(8,128)(2,1)}, bf16[80,1024]{1,0:T(8,128)(2,1)S(1)}, u32[]{:S(2)}, u32[]{:S(2)}) collective-permute-start(bf16[80,1024]{1,0:T(8,128)(2,1)} %get-tuple-element.22), channel_id=1, source_target_pairs={{0,1},{1,0},{2,3},{3,2},{4,5},{5,4},{6,7},{7,6},{8,9},{9,8},{10,11... | collective-permute-start | bytes 491528 | tf_op jit(solution)/shard_map/ppermute | solution.py:468
  81.5 13.1 %collective-permute-start.3 = (bf16[80,1024]{1,0:T(8,128)(2,1)}, bf16[80,1024]{1,0:T(8,128)(2,1)S(1)}, u32[]{:S(2)}, u32[]{:S(2)}) collective-permute-start(bf16[80,1024]{1,0:T(8,128)(2,1)} %get-tuple-element.23), channel_id=1, source_target_pairs={{0,2},{1,3},{2,0},{3,1},{4,6},{5,7},{6,4},{7,5},{8,10},{9,11},{10,... | collective-permute-start | bytes 491528 | tf_op jit(solution)/shard_map/ppermute | solution.py:468
  83.3 22.2 %collective-permute-start.4 = (bf16[80,1024]{1,0:T(8,128)(2,1)}, bf16[80,1024]{1,0:T(8,128)(2,1)S(1)}, u32[]{:S(2)}, u32[]{:S(2)}) collective-permute-start(bf16[80,1024]{1,0:T(8,128)(2,1)} %get-tuple-element.24), channel_id=1, source_target_pairs={{0,3},{1,2},{2,1},{3,0},{4,7},{5,6},{6,5},{7,4},{8,11},{9,10},{10,... | collective-permute-start | bytes 491528 | tf_op jit(solution)/shard_map/ppermute | solution.py:468
  84.8 20.8 %collective-permute-start.5 = (bf16[80,1024]{1,0:T(8,128)(2,1)}, bf16[80,1024]{1,0:T(8,128)(2,1)S(1)}, u32[]{:S(2)}, u32[]{:S(2)}) collective-permute-start(bf16[80,1024]{1,0:T(8,128)(2,1)} %get-tuple-element.25), channel_id=1, source_target_pairs={{0,4},{1,5},{2,6},{3,7},{4,0},{5,1},{6,2},{7,3},{8,12},{9,13},{10,... | collective-permute-start | bytes 491528 | tf_op jit(solution)/shard_map/ppermute | solution.py:468
  85.4 20.2 %collective-permute-start.6 = (bf16[80,1024]{1,0:T(8,128)(2,1)}, bf16[80,1024]{1,0:T(8,128)(2,1)S(1)}, u32[]{:S(2)}, u32[]{:S(2)}) collective-permute-start(bf16[80,1024]{1,0:T(8,128)(2,1)} %get-tuple-element.26), channel_id=1, source_target_pairs={{0,5},{1,4},{2,7},{3,6},{4,1},{5,0},{6,3},{7,2},{8,13},{9,12},{10,... | collective-permute-start | bytes 491528 | tf_op jit(solution)/shard_map/ppermute | solution.py:468
  89.8 15.8 %collective-permute-start.7 = (bf16[80,1024]{1,0:T(8,128)(2,1)}, bf16[80,1024]{1,0:T(8,128)(2,1)S(1)}, u32[]{:S(2)}, u32[]{:S(2)}) collective-permute-start(bf16[80,1024]{1,0:T(8,128)(2,1)} %get-tuple-element.27), channel_id=1, source_target_pairs={{0,6},{1,7},{2,4},{3,5},{4,2},{5,3},{6,0},{7,1},{8,14},{9,15},{10,... | collective-permute-start | bytes 491528 | tf_op jit(solution)/shard_map/ppermute | solution.py:468
  94.6 11.0 %collective-permute-start.8 = (bf16[80,1024]{1,0:T(8,128)(2,1)}, bf16[80,1024]{1,0:T(8,128)(2,1)S(1)}, u32[]{:S(2)}, u32[]{:S(2)}) collective-permute-start(bf16[80,1024]{1,0:T(8,128)(2,1)} %get-tuple-element.28), channel_id=1, source_target_pairs={{0,7},{1,6},{2,5},{3,4},{4,3},{5,2},{6,1},{7,0},{8,15},{9,14},{10,... | collective-permute-start | bytes 491528 | tf_op jit(solution)/shard_map/ppermute | solution.py:468
  96.3 9.3 %copy-start.1 = (bf16[80,1024]{1,0:T(8,128)(2,1)S(1)}, bf16[80,1024]{1,0:T(8,128)(2,1)}, u32[]{:S(2)}) copy-start(bf16[80,1024]{1,0:T(8,128)(2,1)} %get-tuple-element.21.refs_0_) | copy-start | bytes 491524

commit v5 on v4

--- a/solution.py
+++ b/solution.py
@@ -31,7 +31,7 @@
 HID = 1280
 MID = CHAN // 2
 LIMIT = 58 * 1024 * 1024
-GROUP = 2
+GROUP = 4
 ANY = pl.BlockSpec(memory_space=pl.ANY)
 SMEM = pl.BlockSpec(memory_space=pltpu.SMEM)
 VMEM = pl.BlockSpec(memory_space=pltpu.VMEM)
@@ -247,8 +247,7 @@
     pieces, rest = rest[:count], rest[count:]
     o_buf, g_buf, s_buf, l_buf, x_buf, w_buf, t_buf, g_sem, l_sem, w_sem, o_sem = rest
     halo_at, high_at = (BAND, 0) if half else (0, BAND)
-    moves = [(w_ref, w_buf.at[0]), (halo_ref, x_buf.at[1]), (back_ref, w_buf.at[1])]
-    moves += [] if half else [(high_ref, x_buf.at[0])]
+    moves = [(w_ref, w_buf.at[0]), (back_ref, w_buf.at[1])]
     ws = [pltpu.make_async_copy(ref, to, w_sem.at[n]) for n, (ref, to) in enumerate(moves)]
     gs, lows = [], []
     for s in range(STEPS):
@@ -256,17 +255,16 @@
         rows = pl.ds(s * STEP * 2 * FS, STEP * 2 * FS)
         gs.append(pltpu.make_async_copy(g_ref.at[half, part], g_buf.at[part], g_sem.at[s]))
         lows.append(pltpu.make_async_copy(low_ref.at[half, :, rows], l_buf.at[:, rows], l_sem.at[s]))
-    for c in ws[:1] + ws[3:] + ws[1:2]:
+    for c in ws[:1] + ws[2:]:
         c.start()
     for s in range(STEPS):
         gs[s].start()
         lows[s].start()
-    ws[2].start()
-    for c in ws[:1] + ws[3:]:
+    ws[1].start()
+    for c in ws[:1] + ws[2:]:
         c.wait()
-    dft_rows(high_ref if half else x_buf.at[0], w_buf[0], s_buf, high_at)
-    ws[1].wait()
-    dft_rows(x_buf.at[1], w_buf[0], s_buf, halo_at)
+    dft_rows(high_ref, w_buf[0], s_buf, high_at)
+    dft_rows(halo_ref, w_buf[0], s_buf, halo_at)
     theta = [theta_ref[k : k + 1, :] for k in range(KB)]
     for step in range(STEPS):
         gs[step].wait()
@@ -276,7 +274,7 @@
             rows = slice(block * 2 * FS, (block + 1) * 2 * FS)
             for i, row in enumerate(combine(p, theta)):
                 t_buf[i, rows, :] = (row + l_buf[i, rows, :]).astype(BF16)
-    ws[2].wait()
+    ws[1].wait()
     outs = []
     for pair in range(2):
         y = [
@@ -320,7 +318,7 @@
     count = LON_DEV if split else 1
     return pl.pallas_call(
         functools.partial(conv_kernel, half),
-        in_specs=[SMEM, ANY, ANY, VMEM if half else ANY, ANY, VMEM, ANY, ANY],
+        in_specs=[SMEM, ANY, ANY] + [VMEM] * 2 + [VMEM, ANY, ANY],
         out_specs=[ANY] * count,
         out_shape=[jax.ShapeDtypeStruct(shape, BF16)] * count,
         scratch_shapes=[
@@ -339,7 +337,7 @@
         compiler_params=params(),
         cost_estimate=cost(6e9, 1.2e7),
         name="conv",
-    )(me, coef, low, near(high) if half else high, halo, theta, onward, back)
+    )(me, coef, low, near(high), near(halo), theta, onward, back)
 
 
 def mlp_kernel(half, count, me_ref, turn_ref, *refs):

time: 116 us -> 115 us (level)
  transfers between devices with their start and end apart: 13 -> 13, of which waited for: 5 -> 5; matrix products, arithmetic and copies ran while one was open for 3% -> 3% of each run, Pallas kernels for 40% -> 41%
where the time goes in v5:
time: 115 us
  Pallas kernels  58 us (50%)
  starting transfers between devices  34.1 us (30%)
  waiting for transfers between devices  18.7 us (16%)
  local copies, waits for them, and re-layouts  3.5 us (3%)
    pallas_call x2, Pallas kernels, conv(): pl.pallas_call(functools.partial(conv_kernel, half), in_specs=[SMEM, ANY,...  19.8 us
    pallas_call x2, Pallas kernels, mlp(): pl.pallas_call(functools.partial(mlp_kernel, half, count), in_specs=[SMEM...  17.9 us
    ppermute x7, starting transfers between devices, shards(): lax.ppermute(pieces[k], 'lon', [(t, t ^ k) for t in range(lons)])  9.51 us
    all_to_all x1, waiting for transfers between devices, shards(): high = swap(pack(turn, fields, 1, coef, theta4, rest[0], rest[2]))  8.21 us
    ppermute x2, starting transfers between devices, shards(): lax.ppermute(v, ('lat', 'lon'), band_perm(lats, lons, step))  7.87 us
    pallas_call x1, Pallas kernels, coefs(): pl.pallas_call(coef_kernel, grid=(2,), in_specs=[smem, smem, smem, pl.Blo...  7.8 us
    pallas_call x1, Pallas kernels, low_share(): pl.pallas_call(low_kernel, grid=(2,), in_specs=[whole(CHAN, PTS), whole(N...  7.74 us
    all_to_all x1, starting transfers between devices, shards(): low = swap(packed_low)  6.35 us
  transfers between devices with their start and end apart: 13, of which 5 were waited for; matrix products, arithmetic and copies ran while one was open for 3% of the time, Pallas kernels for 41%

profile of v5, /device:TPU:1, one launch (start us, length us, event | category | flops | bytes accessed | tf_op | source)
XLA Modules:
  0.0 114.7 jit_solution(13090069166049856414)
XLA Ops:
  0.0 2.3 %pack.2.rest_0_ = bf16[640,1024]{1,0:T(8,128)(2,1)} custom-call(s32[1]{0:T(128)} %bitcast.1.turn_ref, bf16[4,8,64,640]{3,2,1,0:T(8,128)(2,1)} %refs_8_.1), custom_call_target="tpu_custom_call" | custom-call | bytes 2621440 | tf_op jit(solution)/shard_map/pack/pallas_call | solution.py:98
  2.4 0.0 copy-start.5
  2.4 0.0 copy-start.2
  2.4 6.3 %all-to-all-start.1 = ((bf16[8,80,1024]{2,1,0:T(8,128)(2,1)}), bf16[8,80,1024]{2,1,0:T(8,128)(2,1)S(1)}, u32[]{:S(2)}, u32[]{:S(2)}) async-start(bf16[8,80,1024]{2,1,0:T(8,128)(2,1)} %bitcast.13), calls=%async_computation.1 | async-start | bytes 2621440 | tf_op jit(solution)/shard_map/all_to_all | solution.py:453
  8.7 0.0 copy-done.5
  8.7 1.5 %collective-permute-start = (f32[3,80]{1,0:T(4,128)S(1)}, f32[3,80]{1,0:T(4,128)S(1)}, u32[]{:S(2)}, u32[]{:S(2)}) collective-permute-start(f32[3,80]{1,0:T(4,128)S(1)} %copy-done.5), channel_id=1, source_target_pairs={{0,4},{1,5},{2,6},{3,7},{4,0},{5,1},{6,2},{7,3},{8,12},{9,13},{10,... | collective-permute-start | bytes 2888 | tf_op jit(solution)/shard_map/ppermute | solution.py:448
  10.2 0.0 copy-done.2
  10.2 0.3 copy.14
  10.5 1.0 reshape.25.k_ref
  11.5 0.0 copy-start.4
  11.5 0.0 copy-start.3
  11.5 7.8 %coefs.1 = (bf16[2,16,384,128]{3,2,1,0:T(8,128)(2,1)}, bf16[2,16,384,256]{3,2,1,0:T(8,128)(2,1)}) custom-call(s32[8]{0:T(128)} %start_ref.1, s32[8]{0:T(128)} %count_ref.1, s32[1]{0:T(128)} %bitcast.2.first_ref, f32[2,108,512]{2,1,0:T(8,128)} %reshape.25.k_ref, bf16[512,512]{1,0:T(8,128)(2,1)} %constant.40.clone.w_ref, bf16[640,1024]{1,0:T(8,128)(2,1)} %pack.2.rest_0_), custom_call_target="tpu_custom_call" | custom-call | flops 8000000000 | bytes 10000000 | tf_op jit(solution)/shard_map/coefs/pallas_call | solution.py:176
  19.3 0.0 copy-done.4
  19.3 0.9 broadcast_in_dim.8.rest_2_.refs_2_.refs_9_
  20.2 0.0 copy-done.3
  20.2 0.6 broadcast_in_dim.7.rest_3_.refs_4_.refs_11_
  20.8 0.0 collective-permute-done
  20.8 0.7 tile.10.rest_1_.theta_ref
  21.5 2.4 %pack.3 = bf16[640,1024]{1,0:T(8,128)(2,1)} custom-call(s32[1]{0:T(128)} %bitcast.1.turn_ref, bf16[4,8,64,640]{3,2,1,0:T(8,128)(2,1)} %refs_8_.1, bf16[2,16,384,256]{3,2,1,0:T(8,128)(2,1)} %get-tuple-element.17.rest_0_.g_ref, f32[3,320]{1,0:T(4,128)} %tile.10.rest_1_.theta_ref, f32[640,1]{1,0:T(8,128)} %broadcast_in_dim.8.rest_2_.refs_2_.refs_9_, ...), custom_call_target="tpu_custom_call" | custom-call | bytes 2621440 | tf_op jit(solution)/shard_map/pack/pallas_call | solution.py:98
  23.9 3.5 %all-to-all-done.1 = bf16[8,80,1024]{2,1,0:T(8,128)(2,1)S(1)} async-done(((bf16[8,80,1024]{2,1,0:T(8,128)(2,1)}), bf16[8,80,1024]{2,1,0:T(8,128)(2,1)S(1)}, u32[]{:S(2)}, u32[]{:S(2)}) %all-to-all-start.1) | async-done | bytes 1310752 | tf_op jit(solution)/shard_map/all_to_all | solution.py:453
  27.3 0.0 copy-start.1
  27.4 5.4 %all-to-all-start = ((bf16[8,80,1024]{2,1,0:T(8,128)(2,1)}), bf16[8,80,1024]{2,1,0:T(8,128)(2,1)S(1)}, u32[]{:S(2)}, u32[]{:S(2)}) async-start(bf16[8,80,1024]{2,1,0:T(8,128)(2,1)} %bitcast.16), calls=%async_computation | async-start | bytes 2621440 | tf_op jit(solution)/shard_map/all_to_all | solution.py:457
  32.7 0.0 copy-done.1
  32.7 2.7 %collective-permute-start.9 = (bf16[640,1024]{1,0:T(8,128)(2,1)}, bf16[640,1024]{1,0:T(8,128)(2,1)S(1)}, u32[]{:S(2)}, u32[]{:S(2)}) collective-permute-start(bf16[640,1024]{1,0:T(8,128)(2,1)} %bitcast.14), channel_id=1, source_target_pairs={{8,0},{9,1},{10,2},{11,3},{12,4},{13,5},{14,6},{15,7},{16,12},{17,... | collective-permute-start | bytes 3932168 | tf_op jit(solution)/shard_map/ppermute | solution.py:447
  35.4 7.7 %low.1.low_ref = f32[2,4,512,320]{3,2,1,0:T(8,128)} custom-call(bf16[640,1024]{1,0:T(8,128)(2,1)} %bitcast.15, bf16[512,512]{1,0:T(8,128)(2,1)} %constant.40.clone.w_ref, bf16[2,16,384,128]{3,2,1,0:T(8,128)(2,1)} %get-tuple-element.18.g_ref, f32[3,320]{1,0:T(4,128)} %tile.10.rest_1_.theta_ref), custom_call_target="tpu_custom_call" | custom-call | flops 2000000000 | bytes 8000000 | tf_op jit(solution)/shard_map/low/pallas_call | solution.py:221
  43.2 8.2 %all-to-all-done = bf16[8,80,1024]{2,1,0:T(8,128)(2,1)S(1)} async-done(((bf16[8,80,1024]{2,1,0:T(8,128)(2,1)}), bf16[8,80,1024]{2,1,0:T(8,128)(2,1)S(1)}, u32[]{:S(2)}, u32[]{:S(2)}) %all-to-all-start) | async-done | bytes 1310752 | tf_op jit(solution)/shard_map/all_to_all | solution.py:457
  51.4 5.2 %collective-permute-start.1 = (bf16[640,1024]{1,0:T(8,128)(2,1)S(1)}, bf16[640,1024]{1,0:T(8,128)(2,1)}, u32[]{:S(2)}, u32[]{:S(2)}) collective-permute-start(bf16[640,1024]{1,0:T(8,128)(2,1)S(1)} %bitcast.10), channel_id=1, source_target_pairs={{0,8},{1,9},{2,10},{3,11},{4,12},{5,13},{6,14},{7,15},{8,20},{9,21... | collective-permute-start | bytes 3932168 | tf_op jit(solution)/shard_map/ppermute | solution.py:447
  56.6 0.0 collective-permute-done.9.halo_ref
  56.6 9.4 %conv.3 = bf16[640,1024]{1,0:T(8,128)(2,1)} custom-call(s32[1]{0:T(128)} %bitcast.me_ref, bf16[2,16,384,256]{3,2,1,0:T(8,128)(2,1)} %get-tuple-element.17.rest_0_.g_ref, f32[2,4,512,320]{3,2,1,0:T(8,128)} %low.1.low_ref, bf16[640,1024]{1,0:T(8,128)(2,1)S(1)} %bitcast.11, bf16[640,1024]{1,0:T(8,128)(2,1)S(1)} %collective-permute-done.9.halo_ref, ...), custom_call_target="tpu_custom_call" | custom-call | flops 6000000000 | bytes 12000000 | tf_op jit(solution)/shard_map/conv/pallas_call | solution.py:319
  66.0 3.6 %all-to-all-start.2 = ((bf16[8,80,1024]{2,1,0:T(8,128)(2,1)}), bf16[8,80,1024]{2,1,0:T(8,128)(2,1)S(1)}, u32[]{:S(2)}, u32[]{:S(2)}) async-start(bf16[8,80,1024]{2,1,0:T(8,128)(2,1)} %bitcast.17), calls=%async_computation.2 | async-start | bytes 2621440 | tf_op jit(solution)/shard_map/all_to_all | solution.py:463
  69.6 1.3 %collective-permute-done.1.halo_ref = bf16[640,1024]{1,0:T(8,128)(2,1)} collective-permute-done((bf16[640,1024]{1,0:T(8,128)(2,1)S(1)}, bf16[640,1024]{1,0:T(8,128)(2,1)}, u32[]{:S(2)}, u32[]{:S(2)}) %collective-permute-start.1) | collective-permute-done | bytes 1310752 | tf_op jit(solution)/shard_map/ppermute | solution.py:447
  70.9 10.4 %conv.2 = (bf16[80,1024]{1,0:T(8,128)(2,1)}, bf16[80,1024]{1,0:T(8,128)(2,1)}, bf16[80,1024]{1,0:T(8,128)(2,1)}, bf16[80,1024]{1,0:T(8,128)(2,1)}, bf16[80,1024]...) custom-call(s32[1]{0:T(128)} %bitcast.me_ref, ...), custom_call_target="tpu_custom_call" | custom-call | flops 6000000000 | bytes 12000000 | tf_op jit(solution)/shard_map/conv/pallas_call | solution.py:319
  81.3 0.7 collective-permute-start.2
  82.0 1.8 %collective-permute-start.3 = (bf16[80,1024]{1,0:T(8,128)(2,1)}, bf16[80,1024]{1,0:T(8,128)(2,1)S(1)}, u32[]{:S(2)}, u32[]{:S(2)}) collective-permute-start(bf16[80,1024]{1,0:T(8,128)(2,1)} %get-tuple-element.23), channel_id=1, source_target_pairs={{0,2},{1,3},{2,0},{3,1},{4,6},{5,7},{6,4},{7,5},{8,10},{9,11},{10,... | collective-permute-start | bytes 491528 | tf_op jit(solution)/shard_map/ppermute | solution.py:466
  83.8 1.4 %collective-permute-start.4 = (bf16[80,1024]{1,0:T(8,128)(2,1)}, bf16[80,1024]{1,0:T(8,128)(2,1)S(1)}, u32[]{:S(2)}, u32[]{:S(2)}) collective-permute-start(bf16[80,1024]{1,0:T(8,128)(2,1)} %get-tuple-element.24), channel_id=1, source_target_pairs={{0,3},{1,2},{2,1},{3,0},{4,7},{5,6},{6,5},{7,4},{8,11},{9,10},{10,... | collective-permute-start | bytes 491528 | tf_op jit(solution)/shard_map/ppermute | solution.py:466
  85.2 0.6 collective-permute-start.5
  85.8 0.0 collective-permute-start.6
  85.8 4.2 %collective-permute-done.2.refs_1_ = bf16[80,1024]{1,0:T(8,128)(2,1)S(1)} collective-permute-done((bf16[80,1024]{1,0:T(8,128)(2,1)}, bf16[80,1024]{1,0:T(8,128)(2,1)S(1)}, u32[]{:S(2)}, u32[]{:S(2)}) %collective-permute-start.2) | collective-permute-done | bytes 163872 | tf_op jit(solution)/shard_map/ppermute | solution.py:466
  90.0 3.3 %collective-permute-start.7 = (bf16[80,1024]{1,0:T(8,128)(2,1)}, bf16[80,1024]{1,0:T(8,128)(2,1)S(1)}, u32[]{:S(2)}, u32[]{:S(2)}) collective-permute-start(bf16[80,1024]{1,0:T(8,128)(2,1)} %get-tuple-element.27), channel_id=1, source_target_pairs={{0,6},{1,7},{2,4},{3,5},{4,2},{5,3},{6,0},{7,1},{8,14},{9,15},{10,... | collective-permute-start | bytes 491528 | tf_op jit(solution)/shard_map/ppermute | solution.py:466
  93.3 1.6 %collective-permute-done.3.refs_2_ = bf16[80,1024]{1,0:T(8,128)(2,1)S(1)} collective-permute-done((bf16[80,1024]{1,0:T(8,128)(2,1)}, bf16[80,1024]{1,0:T(8,128)(2,1)S(1)}, u32[]{:S(2)}, u32[]{:S(2)}) %collective-permute-start.3) | collective-permute-done | bytes 163872 | tf_op jit(solution)/shard_map/ppermute | solution.py:466
  94.9 1.7 %collective-permute-start.8 = (bf16[80,1024]{1,0:T(8,128)(2,1)}, bf16[80,1024]{1,0:T(8,128)(2,1)S(1)}, u32[]{:S(2)}, u32[]{:S(2)}) collective-permute-start(bf16[80,1024]{1,0:T(8,128)(2,1)} %get-tuple-element.28), channel_id=1, source_target_pairs={{0,7},{1,6},{2,5},{3,4},{4,3},{5,2},{6,1},{7,0},{8,15},{9,14},{10,... | collective-permute-start | bytes 491528 | tf_op jit(solution)/shard_map/ppermute | solution.py:466
  96.5 0.0 all-to-all-done.2
  96.5 0.0 copy-start
  96.5 9.1 %mlp.2.refs_13_ = bf16[4,8,64,640]{3,2,1,0:T(8,128)(2,1)} custom-call(s32[1]{0:T(128)} %bitcast.me_ref, s32[1]{0:T(128)} %bitcast.1.turn_ref, bf16[640,1024]{1,0:T(8,128)(2,1)S(1)} %bitcast.9, bf16[4,8,64,640]{3,2,1,0:T(8,128)(2,1)} %refs_8_.1, f32[640,1]{1,0:T(8,128)} %broadcast_in_dim.8.rest_2_.refs_2_.refs_9_, bf16[640,1280]{1,0:T(8,128)(2,1)} %refs_10_.1, ...), custom_call_target="tpu_custom_call" | custom-call | flops 3355443200 | bytes 12000000 | tf_op jit(solution)/shard_map/mlp/pallas_call | solution.py:400
  105.6 0.0 collective-permute-done.4.refs_3_
  105.6 0.0 collective-permute-done.5.refs_4_
  105.6 0.0 collective-permute-done.6.refs_5_
  105.6 0.0 collective-permute-done.7.refs_6_
  105.7 0.0 collective-permute-done.8.refs_7_
  105.7 0.0 copy-done
  105.7 8.9 %mlp.3 = bf16[4,8,64,640]{3,2,1,0:T(8,128)(2,1)} custom-call(s32[1]{0:T(128)} %bitcast.me_ref, s32[1]{0:T(128)} %bitcast.1.turn_ref, bf16[80,1024]{1,0:T(8,128)(2,1)S(1)} %copy-done, bf16[80,1024]{1,0:T(8,128)(2,1)S(1)} %collective-permute-done.2.refs_1_, bf16[80,1024]{1,0:T(8,128)(2,1)S(1)} %collective-permute-done.3.refs_2_, ...), custom_call_target="tpu_custom_call", output_to_operand_aliasing={{}: (15, {})} | custom-call | flops 3355443200 | bytes 12000000 | tf_op jit(solution)/shard_map/mlp/pallas_call | solution.py:400
  (2 shorter events, 0.0 us)
Async XLA Ops:
  2.4 6.4 %copy-start.5 = (f32[3,80]{1,0:T(4,128)S(1)}, f32[3,80]{1,0:T(4,128)}, u32[]{:S(2)}) copy-start(f32[3,80]{1,0:T(4,128)} %param.13) | copy-start | bytes 2884
  2.4 7.8 %copy-start.2 = (f32[8,9,3,512]{3,0,2,1:T(8,128)S(1)}, f32[8,9,3,512]{3,0,2,1:T(8,128)}, u32[]{:S(2)}) copy-start(f32[8,9,3,512]{3,0,2,1:T(8,128)} %param.12) | copy-start | bytes 1327108
  2.4 25.0 %all-to-all-start.1 = ((bf16[8,80,1024]{2,1,0:T(8,128)(2,1)}), bf16[8,80,1024]{2,1,0:T(8,128)(2,1)S(1)}, u32[]{:S(2)}, u32[]{:S(2)}) async-start(bf16[8,80,1024]{2,1,0:T(8,128)(2,1)} %bitcast.13), calls=%async_computation.1 | async-start | bytes 2621440 | tf_op jit(solution)/shard_map/all_to_all | solution.py:453
  8.7 12.1 %collective-permute-start = (f32[3,80]{1,0:T(4,128)S(1)}, f32[3,80]{1,0:T(4,128)S(1)}, u32[]{:S(2)}, u32[]{:S(2)}) collective-permute-start(f32[3,80]{1,0:T(4,128)S(1)} %copy-done.5), channel_id=1, source_target_pairs={{0,4},{1,5},{2,6},{3,7},{4,0},{5,1},{6,2},{7,3},{8,12},{9,13},{10,... | collective-permute-start | bytes 2888 | tf_op jit(solution)/shard_map/ppermute | solution.py:448
  11.5 7.8 %copy-start.4 = (f32[640]{0:T(1024)S(1)}, f32[640]{0:T(1024)}, u32[]{:S(2)}) copy-start(f32[640]{0:T(1024)} %param.16) | copy-start | bytes 7684
  11.5 8.7 %copy-start.3 = (f32[1280]{0:T(1024)S(1)}, f32[1280]{0:T(1024)}, u32[]{:S(2)}) copy-start(f32[1280]{0:T(1024)} %param.18) | copy-start | bytes 15364
  27.3 5.4 %copy-start.1 = (bf16[8,80,1024]{2,1,0:T(8,128)(2,1)}, bf16[8,80,1024]{2,1,0:T(8,128)(2,1)S(1)}, u32[]{:S(2)}) copy-start(bf16[8,80,1024]{2,1,0:T(8,128)(2,1)S(1)} %all-to-all-done.1) | copy-start | bytes 3932164
  27.4 24.0 %all-to-all-start = ((bf16[8,80,1024]{2,1,0:T(8,128)(2,1)}), bf16[8,80,1024]{2,1,0:T(8,128)(2,1)S(1)}, u32[]{:S(2)}, u32[]{:S(2)}) async-start(bf16[8,80,1024]{2,1,0:T(8,128)(2,1)} %bitcast.16), calls=%async_computation | async-start | bytes 2621440 | tf_op jit(solution)/shard_map/all_to_all | solution.py:457
  32.7 23.8 %collective-permute-start.9 = (bf16[640,1024]{1,0:T(8,128)(2,1)}, bf16[640,1024]{1,0:T(8,128)(2,1)S(1)}, u32[]{:S(2)}, u32[]{:S(2)}) collective-permute-start(bf16[640,1024]{1,0:T(8,128)(2,1)} %bitcast.14), channel_id=1, source_target_pairs={{8,0},{9,1},{10,2},{11,3},{12,4},{13,5},{14,6},{15,7},{16,12},{17,... | collective-permute-start | bytes 3932168 | tf_op jit(solution)/shard_map/ppermute | solution.py:447
  51.4 19.5 %collective-permute-start.1 = (bf16[640,1024]{1,0:T(8,128)(2,1)S(1)}, bf16[640,1024]{1,0:T(8,128)(2,1)}, u32[]{:S(2)}, u32[]{:S(2)}) collective-permute-start(bf16[640,1024]{1,0:T(8,128)(2,1)S(1)} %bitcast.10), channel_id=1, source_target_pairs={{0,8},{1,9},{2,10},{3,11},{4,12},{5,13},{6,14},{7,15},{8,20},{9,21... | collective-permute-start | bytes 3932168 | tf_op jit(solution)/shard_map/ppermute | solution.py:447
  66.0 30.6 %all-to-all-start.2 = ((bf16[8,80,1024]{2,1,0:T(8,128)(2,1)}), bf16[8,80,1024]{2,1,0:T(8,128)(2,1)S(1)}, u32[]{:S(2)}, u32[]{:S(2)}) async-start(bf16[8,80,1024]{2,1,0:T(8,128)(2,1)} %bitcast.17), calls=%async_computation.2 | async-start | bytes 2621440 | tf_op jit(solution)/shard_map/all_to_all | solution.py:463
  81.3 8.7 %collective-permute-start.2 = (bf16[80,1024]{1,0:T(8,128)(2,1)}, bf16[80,1024]{1,0:T(8,128)(2,1)S(1)}, u32[]{:S(2)}, u32[]{:S(2)}) collective-permute-start(bf16[80,1024]{1,0:T(8,128)(2,1)} %get-tuple-element.22), channel_id=1, source_target_pairs={{0,1},{1,0},{2,3},{3,2},{4,5},{5,4},{6,7},{7,6},{8,9},{9,8},{10,11... | collective-permute-start | bytes 491528 | tf_op jit(solution)/shard_map/ppermute | solution.py:466
  82.0 12.9 %collective-permute-start.3 = (bf16[80,1024]{1,0:T(8,128)(2,1)}, bf16[80,1024]{1,0:T(8,128)(2,1)S(1)}, u32[]{:S(2)}, u32[]{:S(2)}) collective-permute-start(bf16[80,1024]{1,0:T(8,128)(2,1)} %get-tuple-element.23), channel_id=1, source_target_pairs={{0,2},{1,3},{2,0},{3,1},{4,6},{5,7},{6,4},{7,5},{8,10},{9,11},{10,... | collective-permute-start | bytes 491528 | tf_op jit(solution)/shard_map/ppermute | solution.py:466
  83.8 21.8 %collective-permute-start.4 = (bf16[80,1024]{1,0:T(8,128)(2,1)}, bf16[80,1024]{1,0:T(8,128)(2,1)S(1)}, u32[]{:S(2)}, u32[]{:S(2)}) collective-permute-start(bf16[80,1024]{1,0:T(8,128)(2,1)} %get-tuple-element.24), channel_id=1, source_target_pairs={{0,3},{1,2},{2,1},{3,0},{4,7},{5,6},{6,5},{7,4},{8,11},{9,10},{10,... | collective-permute-start | bytes 491528 | tf_op jit(solution)/shard_map/ppermute | solution.py:466
  85.2 20.4 %collective-permute-start.5 = (bf16[80,1024]{1,0:T(8,128)(2,1)}, bf16[80,1024]{1,0:T(8,128)(2,1)S(1)}, u32[]{:S(2)}, u32[]{:S(2)}) collective-permute-start(bf16[80,1024]{1,0:T(8,128)(2,1)} %get-tuple-element.25), channel_id=1, source_target_pairs={{0,4},{1,5},{2,6},{3,7},{4,0},{5,1},{6,2},{7,3},{8,12},{9,13},{10,... | collective-permute-start | bytes 491528 | tf_op jit(solution)/shard_map/ppermute | solution.py:466
  85.8 19.8 %collective-permute-start.6 = (bf16[80,1024]{1,0:T(8,128)(2,1)}, bf16[80,1024]{1,0:T(8,128)(2,1)S(1)}, u32[]{:S(2)}, u32[]{:S(2)}) collective-permute-start(bf16[80,1024]{1,0:T(8,128)(2,1)} %get-tuple-element.26), channel_id=1, source_target_pairs={{0,5},{1,4},{2,7},{3,6},{4,1},{5,0},{6,3},{7,2},{8,13},{9,12},{10,... | collective-permute-start | bytes 491528 | tf_op jit(solution)/shard_map/ppermute | solution.py:466
  90.0 15.7 %collective-permute-start.7 = (bf16[80,1024]{1,0:T(8,128)(2,1)}, bf16[80,1024]{1,0:T(8,128)(2,1)S(1)}, u32[]{:S(2)}, u32[]{:S(2)}) collective-permute-start(bf16[80,1024]{1,0:T(8,128)(2,1)} %get-tuple-element.27), channel_id=1, source_target_pairs={{0,6},{1,7},{2,4},{3,5},{4,2},{5,3},{6,0},{7,1},{8,14},{9,15},{10,... | collective-permute-start | bytes 491528 | tf_op jit(solution)/shard_map/ppermute | solution.py:466
  94.9 10.8 %collective-permute-start.8 = (bf16[80,1024]{1,0:T(8,128)(2,1)}, bf16[80,1024]{1,0:T(8,128)(2,1)S(1)}, u32[]{:S(2)}, u32[]{:S(2)}) collective-permute-start(bf16[80,1024]{1,0:T(8,128)(2,1)} %get-tuple-element.28), channel_id=1, source_target_pairs={{0,7},{1,6},{2,5},{3,4},{4,3},{5,2},{6,1},{7,0},{8,15},{9,14},{10,... | collective-permute-start | bytes 491528 | tf_op jit(solution)/shard_map/ppermute | solution.py:466
  96.5 9.1 %copy-start = (bf16[80,1024]{1,0:T(8,128)(2,1)S(1)}, bf16[80,1024]{1,0:T(8,128)(2,1)}, u32[]{:S(2)}) copy-start(bf16[80,1024]{1,0:T(8,128)(2,1)} %get-tuple-element.21.refs_0_) | copy-start | bytes 491524
